TPU v7x, 32 devices: a whole 2x2x4 slice. The times are simulated.
32 devices in a mesh: probe: 4 (over y, x), seq: 8 (over z, core).
Axes of the slice: x: 2, y: 2, z: 4, core: 2. Of those that a mesh axis runs over, the one named last changes fastest.
Arguments:
- probe_bits: int32 [4, 8, 16384], P('probe', 'seq'), may hold values from 0 to 1
- noise_var: float32 [8, 16384], P('seq'), may hold values from 0.2 to 12
- kernel_spectrum: float32 [16384, 8], P('seq'), may hold values from 0.05 to 4, as said below
- symbol: float32 [16384, 8], P('seq'), may hold values from 0.3 to 3, as said below
- grad_prev: float32 [16384, 8], P('seq', 'probe'), may hold values from -6 to 6
Outputs:
- residual: float32 [4, 8, 16384], P('probe', 'seq')
- grad_total: float32 [16384, 8], P('seq', 'probe')
Inputs may be any that keep to these rules, and one draw needn't show every extreme that they name: kernel_spectrum at frequency k equals kernel_spectrum at frequency (131072 - k) mod 131072. symbol at frequency k equals symbol at frequency (131072 - k) mod 131072.
All inputs are finite; a program needn't handle non-finite values.
Results may differ from a plain program's by a relative error of at most 0.00017.
Values sent between devices are 32-bit elements; how exact they have to be, the bound alone decides.
No kernel may reach another device: no remote copies, remote signals or barrier semaphores. Data moves between devices by JAX's collectives and lax.ppermute only.
A program may use at most 64 MiB of HBM per device.

v0:
```python
import math

import jax
import jax.numpy as jnp
from jax import lax
from jax.sharding import PartitionSpec as P

highest = lax.Precision.HIGHEST
minor_width = 128


def dft_table(height, breadth, modulus, orient):
    left_index = jnp.arange(height, dtype=jnp.int32)[:, None]
    right_index = jnp.arange(breadth, dtype=jnp.int32)[None, :]
    phases = (
        orient * 2.0 * math.pi / modulus * (left_index * right_index % modulus).astype(jnp.float32)
    )
    return (jnp.cos(phases), jnp.sin(phases))


def complex_product(pattern, real_part, imaginary, cosine_table, sine_table):
    real_cos = jnp.einsum(pattern, real_part, cosine_table, precision=highest)
    real_sin = jnp.einsum(pattern, real_part, sine_table, precision=highest)
    if imaginary is None:
        return (real_cos, real_sin)
    imag_cos = jnp.einsum(pattern, imaginary, cosine_table, precision=highest)
    imag_sin = jnp.einsum(pattern, imaginary, sine_table, precision=highest)
    return (real_cos - imag_sin, real_sin + imag_cos)


def rotate(real_part, imaginary, cosine_table, sine_table):
    return (
        real_part * cosine_table - imaginary * sine_table,
        real_part * sine_table + imaginary * cosine_table,
    )


def forward_rows(series):
    major_len = series.shape[-2]
    length = major_len * minor_width
    cosine_table, sine_table = dft_table(major_len, major_len, major_len, -1.0)
    section_real, section_imag = complex_product(
        "...mi,mk->...ik", series, None, cosine_table, sine_table
    )
    turn_cos, turn_sin = dft_table(minor_width, major_len, length, -1.0)
    twisted_real, twisted_imag = rotate(section_real, section_imag, turn_cos, turn_sin)
    cosine_table, sine_table = dft_table(minor_width, minor_width, minor_width, -1.0)
    return complex_product("...ik,ij->...jk", twisted_real, twisted_imag, cosine_table, sine_table)


def inverse_rows(real_part, imaginary):
    major_len = real_part.shape[-1]
    length = major_len * minor_width
    cosine_table, sine_table = dft_table(minor_width, minor_width, minor_width, 1.0)
    section_real, section_imag = complex_product(
        "...jk,ji->...ik", real_part, imaginary, cosine_table, sine_table
    )
    turn_cos, turn_sin = dft_table(minor_width, major_len, length, 1.0)
    twisted_real, twisted_imag = rotate(section_real, section_imag, turn_cos, turn_sin)
    cosine_table, sine_table = dft_table(major_len, major_len, major_len, 1.0)
    final_real, unused = complex_product(
        "...ik,km->...mi", twisted_real, twisted_imag, cosine_table, sine_table
    )
    return final_real


def global_twiddle(local_rows, major_len, samples, orient):
    row_index = lax.axis_index("seq") * local_rows + jnp.arange(local_rows, dtype=jnp.int32)
    column_index = (
        jnp.arange(minor_width, dtype=jnp.int32)[:, None] * major_len
        + jnp.arange(major_len, dtype=jnp.int32)[None, :]
    )
    phases = (
        orient
        * 2.0
        * math.pi
        / samples
        * (row_index[:, None, None] * column_index[None, :, :] % samples).astype(jnp.float32)
    )
    return (jnp.cos(phases), jnp.sin(phases))


def forward_spectrum(series):
    local_rows = series.shape[1]
    major_len = series.shape[2]
    devices = lax.axis_size("seq")
    all_rows = local_rows * devices
    samples = all_rows * major_len * minor_width
    real_part, imaginary = forward_rows(series)
    turn_cos, turn_sin = global_twiddle(local_rows, major_len, samples, -1.0)
    turned_real, turned_imag = rotate(real_part, imaginary, turn_cos, turn_sin)
    arrived = lax.all_to_all(
        jnp.stack([turned_real, turned_imag]), "seq", split_axis=3, concat_axis=2, tiled=True
    )
    block = minor_width // devices * major_len
    arrived = arrived.reshape(arrived.shape[0], arrived.shape[1], all_rows, block)
    cosine_table, sine_table = dft_table(all_rows, all_rows, all_rows, -1.0)
    return complex_product("zrb,ra->zba", arrived[0], arrived[1], cosine_table, sine_table)


def inverse_field(spectrum_real, spectrum_imag):
    all_rows = spectrum_real.shape[2]
    block = spectrum_real.shape[1]
    devices = lax.axis_size("seq")
    major_len = block * devices // minor_width
    cosine_table, sine_table = dft_table(all_rows, all_rows, all_rows, 1.0)
    back_real, back_imag = complex_product(
        "zba,ar->zrb", spectrum_real, spectrum_imag, cosine_table, sine_table
    )
    stacked = jnp.stack([back_real, back_imag])
    stacked = stacked.reshape(
        stacked.shape[0], stacked.shape[1], all_rows, minor_width // devices, major_len
    )
    arrived = lax.all_to_all(stacked, "seq", split_axis=2, concat_axis=3, tiled=True)
    local_rows = arrived.shape[2]
    samples = all_rows * major_len * minor_width
    turn_cos, turn_sin = global_twiddle(local_rows, major_len, samples, 1.0)
    turned_real, turned_imag = rotate(arrived[0], arrived[1], turn_cos, turn_sin)
    return inverse_rows(turned_real, turned_imag) / samples


def shards(probe_bits, noise_var, kernel_spectrum, symbol, grad_prev):
    field_shape = (
        probe_bits.shape[0],
        probe_bits.shape[1],
        probe_bits.shape[2] // minor_width,
        minor_width,
    )
    sign_field = (2 * probe_bits - 1).astype(jnp.float32).reshape(field_shape)
    noise_field = noise_var.reshape(field_shape[1:])
    samples = kernel_spectrum.shape[1] * noise_var.shape[1]
    base_real, base_imag = forward_spectrum(sign_field)
    scaled_real = base_real / symbol
    scaled_imag = base_imag / symbol
    precond = inverse_field(scaled_real, scaled_imag)
    again_real, again_imag = forward_spectrum(precond)
    circulant = inverse_field(kernel_spectrum * again_real, kernel_spectrum * again_imag)
    kernel_image = circulant + noise_field * precond
    numerator, curvature = lax.psum(
        (jnp.sum(sign_field * precond), jnp.sum(precond * kernel_image)), "seq"
    )
    step_size = numerator / curvature
    residual = sign_field - step_size * kernel_image
    cross_term = lax.psum(jnp.sum(residual * kernel_image), "seq")
    weight = -2.0 * cross_term
    resid_real, resid_imag = forward_spectrum(residual)
    applied = (
        inverse_field(kernel_spectrum * resid_real, kernel_spectrum * resid_imag)
        + noise_field * residual
    )
    adjoint = (
        weight / curvature * sign_field
        - 2.0 * weight * step_size / curvature * kernel_image
        - 2.0 * step_size * applied
    )
    adjoint_real, adjoint_imag = forward_spectrum(adjoint)
    local_grad = -(adjoint_real[0] * base_real[0] + adjoint_imag[0] * base_imag[0]) / (
        samples * symbol * symbol
    )
    probes = lax.axis_size("probe")
    summed = lax.psum(local_grad, "probe")
    share_width = summed.shape[1] // probes
    own_share = lax.dynamic_slice_in_dim(
        summed, lax.axis_index("probe") * share_width, share_width, 1
    )
    grad_total = grad_prev + own_share / probes
    return (residual.reshape(probe_bits.shape), grad_total)


def solution(mesh):
    placed = (
        P("probe", "seq", None),
        P("seq", None),
        P("seq", None),
        P("seq", None),
        P("seq", "probe"),
    )
    return jax.shard_map(
        shards,
        mesh=mesh,
        in_specs=placed,
        out_specs=(P("probe", "seq", None), P("seq", "probe")),
        check_vma=False,
    )
```

profile of v0, /device:TPU:0, one launch (start us, length us, event | category | flops | bytes accessed | tf_op | source)
XLA Modules:
  0.0 199.3 jit_solution(10429030731968021779)
XLA Ops:
  7.2 0.9 add_convert_fusion
  9.0 0.7 fusion.74
  9.7 0.7 fusion.66
  10.5 0.7 convolution_add_fusion.13
  11.2 0.9 subtract_bitcast_fusion.3
  12.2 12.9 %all_to_all.28 = f32[2,1,1,128,128]{4,2,1,0,3:T(1,128)S(1)} all-to-all(f32[2,1,1,128,128]{4,2,1,0,3:T(1,128)S(1)} %copy.13), channel_id=1, replica_groups=mesh['probe'=4,'seq'=8] {'seq'}, dimensions={3} | all-to-all | bytes 262144 | tf_op jit(solution)/shard_map/all_to_all | solution.py:92
  26.5 0.5 copy-done.1
  28.6 9.3 %all_to_all.29 = f32[2,1,8,16,128]{4,3,1,0,2:T(8,128)S(1)} all-to-all(f32[2,1,8,16,128]{4,3,1,0,2:T(8,128)S(1)} %pad_maximum_fusion.1), channel_id=1, replica_groups=mesh['probe'=4,'seq'=8] {'seq'}, dimensions={2} | all-to-all | bytes 262144 | tf_op jit(solution)/shard_map/all_to_all | solution.py:114
  38.3 0.5 fusion.81
  39.3 0.5 convolution_add_fusion.12
  39.8 0.5 convolution_subtract_fusion.15
  40.4 0.8 fusion.49
  41.1 0.8 fusion.19
  42.8 0.7 fusion.72
  43.5 0.7 fusion.64
  44.2 0.7 convolution_add_fusion.11
  45.0 0.9 subtract_bitcast_fusion.2
  46.0 9.3 %all_to_all.30 = f32[2,1,1,128,128]{4,2,1,0,3:T(1,128)S(1)} all-to-all(f32[2,1,1,128,128]{4,2,1,0,3:T(1,128)S(1)} %copy.16), channel_id=1, replica_groups=mesh['probe'=4,'seq'=8] {'seq'}, dimensions={3} | all-to-all | bytes 262144 | tf_op jit(solution)/shard_map/all_to_all | solution.py:92
  56.3 0.8 copy-done
  59.1 9.3 %all_to_all.31 = f32[2,1,8,16,128]{4,3,1,0,2:T(8,128)S(1)} all-to-all(f32[2,1,8,16,128]{4,3,1,0,2:T(8,128)S(1)} %pad_maximum_fusion.3), channel_id=1, replica_groups=mesh['probe'=4,'seq'=8] {'seq'}, dimensions={2} | all-to-all | bytes 262144 | tf_op jit(solution)/shard_map/all_to_all | solution.py:114
  68.7 0.5 fusion.80
  69.7 0.5 convolution_add_fusion.10
  70.3 0.5 convolution_subtract_fusion.12
  70.8 0.8 fusion.42
  71.6 1.4 multiply_reduce_fusion.1
  73.0 14.9 %all-reduce = (f32[]{:T(128)}, f32[]{:T(128)}) all-reduce(f32[]{:T(128)} %get-tuple-element.11, f32[]{:T(128)} %get-tuple-element.10), channel_id=1, replica_groups=mesh['probe'=4,'seq'=8] {'seq'}, use_global_device_ids=true, to_apply=%region_1.2 | all-reduce | flops 2 | bytes 16 | tf_op jit(solution)/shard_map/psum | solution.py:139
  89.2 0.6 multiply_reduce_fusion
  90.7 0.7 fusion.70
  91.5 0.7 fusion.62
  92.2 0.7 convolution_add_fusion.9
  92.9 0.9 subtract_bitcast_fusion.1
  93.9 9.2 %all_to_all.32 = f32[2,1,1,128,128]{4,2,1,0,3:T(1,128)S(1)} all-to-all(f32[2,1,1,128,128]{4,2,1,0,3:T(1,128)S(1)} %copy.19), channel_id=1, replica_groups=mesh['probe'=4,'seq'=8] {'seq'}, dimensions={3} | all-to-all | bytes 262144 | tf_op jit(solution)/shard_map/all_to_all | solution.py:92
  106.1 0.6 pad_maximum_fusion.5
  106.7 3.4 %all-to-all-start.5 = ((f32[2,1,8,16,128]{4,3,1,0,2:T(8,128)}), f32[2,1,8,16,128]{4,3,1,0,2:T(8,128)S(1)}, u32[]{:S(2)}, u32[]{:S(2)}) async-start(f32[2,1,8,16,128]{4,3,1,0,2:T(8,128)} %pad_maximum_fusion.5), calls=%async_computation.5 | async-start | bytes 262144 | tf_op jit(solution)/shard_map/all_to_all | solution.py:114
  110.1 17.9 %psum.30 = f32[]{:T(128)} all-reduce(f32[]{:T(128)} %get-tuple-element.14), channel_id=1, replica_groups=mesh['probe'=4,'seq'=8] {'seq'}, use_global_device_ids=true, to_apply=%region_5.6 | all-reduce | flops 1 | bytes 8 | tf_op jit(solution)/shard_map/psum | solution.py:144
  131.1 0.5 fusion.79
  132.2 0.5 convolution_add_fusion.8
  132.7 0.5 convolution_subtract_fusion.9
  133.2 0.8 fusion.35
  134.0 0.8 fusion.21
  135.7 0.7 fusion.68
  136.4 0.7 fusion.60
  137.1 0.7 convolution_add_fusion.7
  137.8 0.9 subtract_bitcast_fusion
  138.9 9.2 %all_to_all.33 = f32[2,1,1,128,128]{4,2,1,0,3:T(1,128)S(1)} all-to-all(f32[2,1,1,128,128]{4,2,1,0,3:T(1,128)S(1)} %copy.22), channel_id=1, replica_groups=mesh['probe'=4,'seq'=8] {'seq'}, dimensions={3} | all-to-all | bytes 262144 | tf_op jit(solution)/shard_map/all_to_all | solution.py:92
  149.4 0.9 fusion.3
  150.4 40.7 %all-reduce.3.cloned.1.call-done = f32[2048,8]{0,1:T(8,128)} async-done(((f32[2048,8]{0,1:T(8,128)}), f32[2048,8]{0,1:T(8,128)}) %all-reduce.3.cloned.1.call-update) | async-done | bytes 65552 | tf_op jit(solution)/shard_map/psum | solution.py:161
  191.0 1.5 multiply_add_fusion.4
  (84 shorter events, 16.9 us)
Async XLA Ops:
  26.1 0.8 copy-start.1
  56.3 0.8 copy-start
  70.8 0.8 copy-start.4
  89.8 44.2 %copy-start.2 = (f32[128,128]{1,0:T(8,128)}, f32[128,128]{1,0:T(8,128)S(1)}, u32[]{:S(2)}) copy-start(f32[128,128]{1,0:T(8,128)S(1)} %get-tuple-element.15) | copy-start | bytes 196612
  106.7 24.0 %all-to-all-start.5 = ((f32[2,1,8,16,128]{4,3,1,0,2:T(8,128)}), f32[2,1,8,16,128]{4,3,1,0,2:T(8,128)S(1)}, u32[]{:S(2)}, u32[]{:S(2)}) async-start(f32[2,1,8,16,128]{4,3,1,0,2:T(8,128)} %pad_maximum_fusion.5), calls=%async_computation.5 | async-start | bytes 262144 | tf_op jit(solution)/shard_map/all_to_all | solution.py:114
  110.1 80.9 %all-reduce.3.cloned.1.call-start = ((), (), s32[]{:S(2)}) async-start(), calls=%async_computation.7 | async-start | bytes 131072 | tf_op jit(solution)/shard_map/psum | solution.py:161
  150.3 40.7 %copy-start.3 = (f32[2048,2]{0,1:T(2,128)S(1)}, f32[2048,2]{0,1:T(2,128)}, u32[]{:S(2)}) copy-start(f32[2048,2]{0,1:T(2,128)} %param.9) | copy-start | bytes 49156
Sparse Core Ops, SparseCore 0:
  150.5 40.4 all-reduce.2
where the time goes:
time: 200 us; the launch traced here: 199 us
  blocking collectives  91.8 us (46%)
  waiting for transfers between devices  40.7 us (20%)
  matrix products  36.2 us (18%)
  between operations  18.9 us (9%)
  other arithmetic  4.75 us (2%)
  local copies, waits for them, and re-layouts  3.59 us (2%)
  starting transfers between devices  3.41 us (2%)
    psum x1, waiting for transfers between devices, shards(): summed = lax.psum(local_grad, 'probe')  40.7 us
    all_to_all x4, blocking collectives, forward_spectrum(): lax.all_to_all(jnp.stack([turned_real, turned_imag]), 'seq', split_axis=3...  40.5 us
    all_to_all x2, blocking collectives, inverse_field(): lax.all_to_all(stacked, 'seq', split_axis=2, concat_axis=3, tiled=True)  18.5 us
    psum x1, blocking collectives, shards(): cross_term = lax.psum(jnp.sum(residual * kernel_image), 'seq')  17.9 us
    psum x1, blocking collectives, shards(): lax.psum((jnp.sum(sign_field * precond), jnp.sum(precond * kernel_image))...  14.9 us
    dot_general x21, matrix products, complex_product(): real_cos = jnp.einsum(pattern, real_part, cosine_table, precision=highest)  10.6 us
    dot_general x17, matrix products, complex_product(): imag_sin = jnp.einsum(pattern, imaginary, sine_table, precision=highest)  10.1 us
    dot_general x18, matrix products, complex_product(): real_sin = jnp.einsum(pattern, real_part, sine_table, precision=highest)  8.35 us
  transfers between devices with their start and end apart: 2, of which 1 were waited for; matrix products, arithmetic and copies ran while one was open for 0% of the time, Pallas kernels for 0%

commit v1 on v0

--- a/solution.py
+++ b/solution.py
@@ -1,9 +1,387 @@
+import functools
 import math
 
 import jax
 import jax.numpy as jnp
+import numpy as np
 from jax import lax
+from jax.experimental import pallas as pl
+from jax.experimental.pallas import tpu as pltpu
 from jax.sharding import PartitionSpec as P
+
+lanes = 128
+lead = 8
+near = jnp.bfloat16
+exact = jnp.float32
+
+
+def split_table(table):
+    high = table.astype(near)
+    low = (table - high.astype(np.float64)).astype(near)
+    return high, low
+
+
+def angle_parts(phase):
+    return np.cos(phase), np.sin(phase)
+
+
+@functools.cache
+def tables(rows):
+    index = np.arange(lanes, dtype=np.float64)
+    row_len = lanes * lanes
+    turn = -2.0 * np.pi
+    c, s = angle_parts(turn * (np.outer(index, index) % lanes) / lanes)
+    forward = np.block([[c, s], [-s, c]])
+    high, low = split_table(forward)
+    right = np.concatenate([high, high, low], 0)
+    left = np.ascontiguousarray(right.T)
+    real_high, real_low = high[:lanes], low[:lanes]
+    sign_right = np.concatenate([real_high, real_low], 0)
+    real_right = np.concatenate([real_high, real_high, real_low], 0)
+    back_high, back_low = split_table(np.concatenate([c, s], 0))
+    back_right = np.concatenate([back_high, back_high, back_low], 0)
+    wc, ws = angle_parts(turn * np.outer(index, index) / row_len)
+    small_turn = np.concatenate([wc, ws], 1).astype(np.float32)
+    flat = (index[:, None] * lanes + index[None, :])[None]
+    row = np.arange(rows, dtype=np.float64)[:, None, None]
+    gc, gs = angle_parts(turn * flat * row / (rows * row_len))
+    big_turn = np.concatenate([gc, gs], 2).astype(np.float32)
+    return {
+        "right": right,
+        "left": left,
+        "sign_right": sign_right,
+        "real_right": real_right,
+        "back_right": back_right,
+        "small_turn": small_turn,
+        "big_turn": big_turn,
+    }
+
+
+@functools.cache
+def block_left(rows):
+    left = tables(rows)["left"]
+    depth = lanes // rows
+    parts = [
+        np.concatenate([left[k * depth : (k + 1) * depth], left[lanes + k * depth : lanes + (k + 1) * depth]], 0)
+        for k in range(rows)
+    ]
+    return np.stack(parts)
+
+
+def split(x):
+    high = x.astype(near)
+    return high, (x - high.astype(exact)).astype(near)
+
+
+def stacked(first, second, axis):
+    fh, fl = split(first)
+    sh, sl = split(second)
+    return jnp.concatenate([fh, sh, fl, sl, fh, sh], axis)
+
+
+def times(left, right):
+    return jnp.dot(left, right, preferred_element_type=exact)
+
+
+def turned(re, im, cos, sin):
+    return re * cos - im * sin, re * sin + im * cos
+
+
+def turned_back(re, im, cos, sin):
+    return re * cos + im * sin, im * cos - re * sin
+
+
+def add(x, y):
+    return x[0] + y[0], x[1] + y[1]
+
+
+def sub(x, y):
+    return x[0] - y[0], x[1] - y[1]
+
+
+def unit_turn(x, k, n, orient):
+    k = (k * orient) % n
+    if k == 0:
+        return x
+    if 4 * k == n:
+        return -x[1], x[0]
+    if 2 * k == n:
+        return -x[0], -x[1]
+    if 4 * k == 3 * n:
+        return x[1], -x[0]
+    cos, sin = math.cos(2 * math.pi * k / n), math.sin(2 * math.pi * k / n)
+    return x[0] * cos - x[1] * sin, x[0] * sin + x[1] * cos
+
+
+def small_dft(xs, orient):
+    n = len(xs)
+    if n == 1:
+        return xs
+    even, odd = small_dft(xs[0::2], orient), small_dft(xs[1::2], orient)
+    odd = [unit_turn(x, k, n, orient) for k, x in enumerate(odd)]
+    return [add(e, o) for e, o in zip(even, odd)] + [sub(e, o) for e, o in zip(even, odd)]
+
+
+def half_dft(xs, orient):
+    n = 2 * len(xs)
+    even = small_dft(xs, orient)
+    odd = small_dft([unit_turn(x, k, n, orient) for k, x in enumerate(xs)], orient)
+    return [(odd if r % 2 else even)[r // 2] for r in range(n)]
+
+
+def pack_kernel(half, bits, noise, kernel, symbol, signs_out, spectra_out, noise_out):
+    signs_out[...] = (2 * bits[...] - 1).astype(exact).T
+    noise_out[...] = noise[...].T
+    depth = kernel.shape[0]
+    for a in range(half):
+        spectra_out[a * depth : (a + 1) * depth] = kernel[:, a]
+        spectra_out[(half + a) * depth : (half + a + 1) * depth] = symbol[:, a]
+    middle = jnp.concatenate([kernel[0, half : half + 1], symbol[0, half : half + 1]], 0)
+    spectra_out[2 * half * depth :] = jnp.concatenate([middle] * (lead // 2), 0)
+
+
+def spectrum_kernel(rows, *refs):
+    signs = refs[:rows]
+    sign_right, left, small_turn, big_turn, spectrum, work = refs[rows:]
+    me = lax.axis_index("seq")
+    wc, ws = small_turn[:, :lanes], small_turn[:, lanes:]
+    for pair in range(rows // 2):
+        columns = []
+        for j in (2 * pair, 2 * pair + 1):
+            x = signs[j][...].astype(near)
+            section = times(jnp.concatenate([x, x], 1), sign_right[...])
+            columns.append(stacked(*turned(section[:, :lanes], section[:, lanes:], wc, ws), 0))
+        done = times(left[...], jnp.concatenate(columns, 1))
+        for k, j in enumerate((2 * pair, 2 * pair + 1)):
+            r = me ^ j
+            re, im = done[:lanes, k * lanes : (k + 1) * lanes], done[lanes:, k * lanes : (k + 1) * lanes]
+            re, im = turned(re, im, big_turn[r, :, :lanes], big_turn[r, :, lanes:])
+            work[r, 0] = re
+            work[r, 1] = im
+    for t in range(0, lanes, lead):
+        at = slice(t, t + lead)
+        out = small_dft([(work[r, 0, at], work[r, 1, at]) for r in range(rows)], -1)
+        for a in range(rows):
+            spectrum[a, 0, at] = out[a][0]
+            spectrum[a, 1, at] = out[a][1]
+
+
+def inverse_kernel(rows, *refs):
+    blocks = refs[:rows]
+    spectrum, left, back_right, small_turn, big_turn, precond, circulant, kernel, symbol, ends, work = refs[rows:]
+    half = rows // 2
+    depth = lanes // rows
+    samples = rows * lanes * lanes
+    me = lax.axis_index("seq")
+    for j in range(rows):
+        place = pl.multiple_of((me ^ j) * depth, depth)
+        for a in range(half):
+            kernel[a, pl.ds(place, depth)] = blocks[j][a * depth : (a + 1) * depth]
+            symbol[a, pl.ds(place, depth)] = blocks[j][(half + a) * depth : (half + a + 1) * depth]
+        ends[me ^ j] = blocks[j][2 * half * depth :]
+    middle = spectrum[half, 0, 0:1, 0:1] / ends[0, 1:2, 0:1] / samples
+    middle_image = middle * ends[0, 0:1, 0:1]
+    for t in range(0, lanes, lead):
+        at = slice(t, t + lead)
+        first, second = [], []
+        for a in range(half):
+            scale = 2.0 / samples / symbol[a, at]
+            if a == 0 and t == 0:
+                zero = (lax.broadcasted_iota(jnp.int32, (lead, lanes), 0) == 0) & (
+                    lax.broadcasted_iota(jnp.int32, (lead, lanes), 1) == 0
+                )
+                scale = jnp.where(zero, 0.5 * scale, scale)
+            re, im = spectrum[a, 0, at] * scale, spectrum[a, 1, at] * scale
+            first.append((re, im))
+            second.append((re * kernel[a, at], im * kernel[a, at]))
+        for field, entries in enumerate((first, second)):
+            out = half_dft(entries, 1)
+            for r in range(rows):
+                re, im = turned_back(*out[r], big_turn[r, at, :lanes], big_turn[r, at, lanes:])
+                work[r, field, 0, at] = re
+                work[r, field, 1, at] = im
+    wc, ws = small_turn[:, :lanes], small_turn[:, lanes:]
+    for r in range(rows):
+        columns = [stacked(work[r, field, 1], work[r, field, 0], 0) for field in range(2)]
+        done = times(left[...], jnp.concatenate(columns, 1))
+        lined = []
+        for field in range(2):
+            at = slice(field * lanes, (field + 1) * lanes)
+            lined.append(stacked(*turned_back(done[lanes:, at], done[:lanes, at], wc, ws), 1))
+        done = times(jnp.concatenate(lined, 0), back_right[...])
+        sign = 1.0 if r % 2 == 0 else -1.0
+        precond[r] = done[:lanes] + sign * middle
+        circulant[r] = done[lanes:] + sign * middle_image
+
+
+def whole_sum(x):
+    return jnp.sum(jnp.sum(x, axis=0, keepdims=True), axis=1, keepdims=True)
+
+
+def adjoint_kernel(rows, probes, *refs):
+    signs, noises = refs[:rows], refs[rows : 2 * rows]
+    refs = refs[2 * rows :]
+    precond, circulant, spectrum, kernel, symbol, block, real_right, small_turn, big_turn, residual_out = refs[:10]
+    outs = refs[10 : 10 + probes]
+    image, field, work, shares = refs[10 + probes :]
+    depth = lanes // rows
+    samples = rows * lanes * lanes
+    me = lax.axis_index("seq")
+    numerator = jnp.zeros((lanes, lanes), exact)
+    curvature = jnp.zeros((lanes, lanes), exact)
+    for j in range(rows):
+        p = precond[me ^ j]
+        ki = circulant[me ^ j] + noises[j][...] * p
+        image[j] = ki
+        numerator += signs[j][...] * p
+        curvature += p * ki
+    numerator, curvature = whole_sum(numerator), whole_sum(curvature)
+    step_size = numerator / curvature
+    cross = jnp.zeros((lanes, lanes), exact)
+    for j in range(rows):
+        residual = signs[j][...] - step_size * image[j]
+        cross += residual * image[j]
+        field[j] = residual
+    weight = -2.0 * whole_sum(cross)
+    residual_out[...] = field[0].T
+    wc, ws = small_turn[:, :lanes], small_turn[:, lanes:]
+    own = pl.multiple_of(me * depth, depth)
+    for j in range(rows):
+        r = me ^ j
+        lined = []
+        for x in (precond[r], field[j]):
+            high, low = split(noises[j][...] * x)
+            lined.append(jnp.concatenate([high, low, high], 1))
+        section = times(jnp.concatenate(lined, 0), real_right[...])
+        columns = []
+        for k in range(2):
+            at = slice(k * lanes, (k + 1) * lanes)
+            columns.append(stacked(*turned(section[at, :lanes], section[at, lanes:], wc, ws), 0))
+        done = times(block[me], jnp.concatenate(columns, 1))
+        gc, gs = big_turn[r, pl.ds(own, depth), :lanes], big_turn[r, pl.ds(own, depth), lanes:]
+        for k in range(2):
+            at = slice(k * lanes, (k + 1) * lanes)
+            re, im = turned(done[:depth, at], done[depth:, at], gc, gs)
+            work[r, k, 0] = re
+            work[r, k, 1] = im
+    noisy = small_dft([(work[r, 0, 0], work[r, 0, 1]) for r in range(rows)], -1)
+    noisy_residual = small_dft([(work[r, 1, 0], work[r, 1, 1]) for r in range(rows)], -1)
+    for a in range(rows):
+        k, s = kernel[:, a], symbol[:, a]
+        total = 0.0
+        for part in range(2):
+            base = spectrum[a, part, pl.ds(own, depth)]
+            ki = k * (base / s) + noisy[a][part]
+            applied = k * (base - step_size * ki) + noisy_residual[a][part]
+            adjoint = (
+                (weight / curvature) * base
+                - (2.0 * weight * step_size / curvature) * ki
+                - (2.0 * step_size) * applied
+            )
+            total += adjoint * base
+        shares[a] = -total / (samples * s * s)
+    width = rows // probes
+    column = lax.axis_index("probe")
+    for d in range(probes):
+        for k in range(width):
+            outs[d][:, k] = shares[(column ^ d) * width + k]
+
+
+def finish_kernel(probes, *refs):
+    parts, before, out = refs[:probes], refs[probes], refs[probes + 1]
+    out[...] = before[...] + sum(part[...] for part in parts) / probes
+
+
+def call(kernel, outs, scratch, *operands):
+    whole = pl.BlockSpec(memory_space=pltpu.VMEM)
+    shapes = tuple(jax.ShapeDtypeStruct(shape, exact) for shape in outs)
+    return pl.pallas_call(
+        kernel,
+        out_shape=shapes,
+        in_specs=[whole] * len(operands),
+        out_specs=(whole,) * len(shapes),
+        scratch_shapes=[pltpu.VMEM(shape, exact) for shape in scratch],
+        compiler_params=pltpu.CompilerParams(vmem_limit_bytes=24 << 20),
+    )(*operands)
+
+
+def swapped(x, axis, d):
+    return lax.ppermute(x, axis, [(i, i ^ d) for i in range(lax.axis_size(axis))])
+
+
+def spread(x):
+    near_block = swapped(x, "seq", 1)
+    got = [x, near_block]
+    for d in range(2, lax.axis_size("seq"), 2):
+        there = swapped(x, "seq", d)
+        got += [there, swapped(there, "seq", 1)]
+    return got
+
+
+def gathered_shards(probe_bits, noise_var, kernel_spectrum, symbol, grad_prev):
+    rows = kernel_spectrum.shape[1]
+    probes = lax.axis_size("probe")
+    half, depth, width = rows // 2, lanes // rows, rows // probes
+    t = tables(rows)
+    kernel = kernel_spectrum.T.reshape(rows, depth, lanes).transpose(1, 0, 2)
+    symbols = symbol.T.reshape(rows, depth, lanes).transpose(1, 0, 2)
+    before = grad_prev.T.reshape(width, depth, lanes).transpose(1, 0, 2)
+    square = (lanes, lanes)
+    signs, spectra, noise = call(
+        functools.partial(pack_kernel, half),
+        [square, (2 * half * depth + lead, lanes), square],
+        [],
+        probe_bits.reshape(square),
+        noise_var.reshape(square),
+        kernel,
+        symbols,
+    )
+    signs, spectra, noise = spread(signs), spread(spectra), spread(noise)
+    whole = (rows, 2, *square)
+    (spectrum,) = call(
+        functools.partial(spectrum_kernel, rows),
+        [whole],
+        [whole],
+        *signs,
+        t["sign_right"],
+        t["left"],
+        t["small_turn"],
+        t["big_turn"],
+    )
+    field = (rows, *square)
+    precond, circulant = call(
+        functools.partial(inverse_kernel, rows),
+        [field, field],
+        [(half, *square), (half, *square), (rows, lead, lanes), (rows, 2, 2, *square)],
+        *spectra,
+        spectrum,
+        t["left"],
+        t["back_right"],
+        t["small_turn"],
+        t["big_turn"],
+    )
+    share = (depth, width, lanes)
+    residual, *parts = call(
+        functools.partial(adjoint_kernel, rows, probes),
+        [square] + [share] * probes,
+        [field, field, (rows, 2, 2, depth, lanes), (rows, depth, lanes)],
+        *signs,
+        *noise,
+        precond,
+        circulant,
+        spectrum,
+        kernel,
+        symbols,
+        block_left(rows),
+        t["real_right"],
+        t["small_turn"],
+        t["big_turn"],
+    )
+    parts = [parts[0]] + [swapped(parts[d], "probe", d) for d in range(1, probes)]
+    (total,) = call(functools.partial(finish_kernel, probes), [share], [], *parts, before)
+    total = total.transpose(1, 0, 2).reshape(width, depth * lanes).T
+    return residual.reshape(probe_bits.shape), total
+
 
 highest = lax.Precision.HIGHEST
 minor_width = 128
@@ -167,6 +545,12 @@
     return (residual.reshape(probe_bits.shape), grad_total)
 
 
+def fits(mesh, cols, rows):
+    seq, probe = mesh.shape["seq"], mesh.shape["probe"]
+    powers = all(n & (n - 1) == 0 for n in (rows, seq, probe))
+    return powers and rows == seq == lead and rows % probe == 0 and probe > 1 and cols == lanes * lanes
+
+
 def solution(mesh):
     placed = (
         P("probe", "seq", None),
@@ -175,10 +559,15 @@
         P("seq", None),
         P("seq", "probe"),
     )
-    return jax.shard_map(
-        shards,
-        mesh=mesh,
-        in_specs=placed,
-        out_specs=(P("probe", "seq", None), P("seq", "probe")),
-        check_vma=False,
-    )
+
+    def whole(probe_bits, noise_var, kernel_spectrum, symbol, grad_prev):
+        small = fits(mesh, *symbol.shape)
+        return jax.shard_map(
+            gathered_shards if small else shards,
+            mesh=mesh,
+            in_specs=placed,
+            out_specs=(P("probe", "seq", None), P("seq", "probe")),
+            check_vma=False,
+        )(probe_bits, noise_var, kernel_spectrum, symbol, grad_prev)
+
+    return whole

time: 200 us -> 50.6 us (0.25)
  blocking collectives: 91.8 us -> 0 us
  matrix products: 36.2 us -> 0 us
  waiting for transfers between devices: 40.7 us -> 10.3 us
  starting transfers between devices: 3.41 us -> 24.6 us
  between operations: 18.9 us -> 0.81 us
  Pallas kernels: 0 us -> 8.93 us
  other arithmetic: 4.75 us -> 0 us
  local copies, waits for them, and re-layouts: 3.59 us -> 5.62 us
    all_to_all x6 -> x0, blocking collectives: 59 us -> none  [the longest x4 40.5 us: forward_spectrum(): lax.all_to_all(jnp.stack([turned_real, turned_imag]), 'seq', split_axis=3...]
    psum x1 -> x0, waiting for transfers between devices: 40.7 us -> none  [shards(): summed = lax.psum(local_grad, 'probe')]
    dot_general x70 -> x0, matrix products: 36.2 us -> none  [the longest x21 10.6 us: complex_product(): real_cos = jnp.einsum(pattern, real_part, cosine_table, precision=highest)]
    psum x2 -> x0, blocking collectives: 32.7 us -> none  [the longest x1 17.9 us: shards(): cross_term = lax.psum(jnp.sum(residual * kernel_image), 'seq')]
    ppermute x0 -> x24, starting transfers between devices: none -> 24.6 us  [swapped(): lax.ppermute(x, axis, [(i, i ^ d) for i in range(lax.axis_size(axis))])]
    ppermute x0 -> x24, waiting for transfers between devices: none -> 10.3 us  [swapped(): lax.ppermute(x, axis, [(i, i ^ d) for i in range(lax.axis_size(axis))])]
    pallas_call x0 -> x5, Pallas kernels: none -> 8.93 us  [call(): pl.pallas_call(kernel, out_shape=shapes, in_specs=[whole] * len(operands)...]
    unnamed x10 -> x30, local copies, waits for them, and re-layouts: 1.42 us -> 5.62 us
  transfers between devices with their start and end apart: 2 -> 24, of which waited for: 1 -> 7; matrix products, arithmetic and copies ran while one was open for 0% -> 0% of each run, Pallas kernels for 0% -> 8%
where the time goes in v1:
time: 50.6 us; the launch traced here: 50.2 us
  starting transfers between devices  24.6 us (49%)
  waiting for transfers between devices  10.3 us (20%)
  Pallas kernels  8.93 us (18%)
  local copies, waits for them, and re-layouts  5.62 us (11%)
  between operations  0.81 us (2%)
    ppermute x24, starting transfers between devices, swapped(): lax.ppermute(x, axis, [(i, i ^ d) for i in range(lax.axis_size(axis))])  24.6 us
    ppermute x24, waiting for transfers between devices, swapped(): lax.ppermute(x, axis, [(i, i ^ d) for i in range(lax.axis_size(axis))])  10.3 us
    pallas_call x5, Pallas kernels, call(): pl.pallas_call(kernel, out_shape=shapes, in_specs=[whole] * len(operands)...  8.93 us
    unnamed x30, local copies, waits for them, and re-layouts  5.62 us
  transfers between devices with their start and end apart: 24, of which 7 were waited for; matrix products, arithmetic and copies ran while one was open for 0% of the time, Pallas kernels for 8%

profile of v1, /device:TPU:0, one launch (start us, length us, event | category | flops | bytes accessed | tf_op | source)
XLA Modules:
  0.0 50.2 jit_solution(15642596760879956229)
XLA Ops:
  0.6 0.0 copy-start.5
  0.6 0.8 %copy-done.5 = f32[2048,8]{0,1:T(8,128)S(1)} copy-done((f32[2048,8]{0,1:T(8,128)S(1)}, f32[2048,8]{0,1:T(8,128)}, u32[]{:S(2)}) %copy-start.5) | copy-done | bytes 65560
  1.5 0.8 %copy-done.7 = f32[2048,8]{0,1:T(8,128)S(1)} copy-done((f32[2048,8]{0,1:T(8,128)S(1)}, f32[2048,8]{0,1:T(8,128)}, u32[]{:S(2)}) %copy-start.7) | copy-done | bytes 65560
  2.3 0.8 %copy-done.12 = s32[1,1,16384]{2,1,0:T(1,128)S(1)} copy-done((s32[1,1,16384]{2,1,0:T(1,128)S(1)}, s32[1,1,16384]{2,1,0:T(1,128)}, u32[]{:S(2)}) %copy-start.12) | copy-done | bytes 65560
  3.2 0.8 %copy-done.13 = f32[1,16384]{1,0:T(1,128)S(1)} copy-done((f32[1,16384]{1,0:T(1,128)S(1)}, f32[1,16384]{1,0:T(1,128)}, u32[]{:S(2)}) %copy-start.13) | copy-done | bytes 65560
  4.0 0.1 shard_map.131
  4.1 3.1 %collective-permute-start.1 = (f32[128,128]{1,0:T(8,128)S(1)}, f32[128,128]{1,0:T(8,128)S(1)}, u32[]{:S(2)}, u32[]{:S(2)}) collective-permute-start(f32[128,128]{1,0:T(8,128)S(1)} %get-tuple-element.12.refs_0_), channel_id=1, source_target_pairs={{0,2},{1,3},{2,0},{3,1},{4,6},{5,7},{6,4},{7,5},{8,10},{9,11},{10,... | collective-permute-start | bytes 196616 | tf_op jit(solution)/shard_map/ppermute | solution.py:309
  7.2 2.6 %collective-permute-start.3 = (f32[128,128]{1,0:T(8,128)S(1)}, f32[128,128]{1,0:T(8,128)S(1)}, u32[]{:S(2)}, u32[]{:S(2)}) collective-permute-start(f32[128,128]{1,0:T(8,128)S(1)} %get-tuple-element.12.refs_0_), channel_id=1, source_target_pairs={{0,4},{1,5},{2,6},{3,7},{4,0},{5,1},{6,2},{7,3},{8,12},{9,13},{10,... | collective-permute-start | bytes 196616 | tf_op jit(solution)/shard_map/ppermute | solution.py:309
  9.8 0.0 collective-permute-start.5
  9.8 0.0 collective-permute-start
  9.8 1.9 %collective-permute-start.10 = (f32[128,128]{1,0:T(8,128)S(1)}, f32[128,128]{1,0:T(8,128)S(1)}, u32[]{:S(2)}, u32[]{:S(2)}) collective-permute-start(f32[128,128]{1,0:T(8,128)S(1)} %get-tuple-element.13.refs_8_), channel_id=1, source_target_pairs={{0,4},{1,5},{2,6},{3,7},{4,0},{5,1},{6,2},{7,3},{8,12},{9,13},{10,... | collective-permute-start | bytes 196616 | tf_op jit(solution)/shard_map/ppermute | solution.py:309
  11.7 2.4 %collective-permute-start.12 = (f32[128,128]{1,0:T(8,128)S(1)}, f32[128,128]{1,0:T(8,128)S(1)}, u32[]{:S(2)}, u32[]{:S(2)}) collective-permute-start(f32[128,128]{1,0:T(8,128)S(1)} %get-tuple-element.13.refs_8_), channel_id=1, source_target_pairs={{0,6},{1,7},{2,4},{3,5},{4,2},{5,3},{6,0},{7,1},{8,14},{9,15},{10,... | collective-permute-start | bytes 196616 | tf_op jit(solution)/shard_map/ppermute | solution.py:309
  14.1 0.4 collective-permute-done.3.refs_4_
  14.5 3.1 %collective-permute-start.15 = (f32[136,128]{1,0:T(8,128)S(1)}, f32[136,128]{1,0:T(8,128)S(1)}, u32[]{:S(2)}, u32[]{:S(2)}) collective-permute-start(f32[136,128]{1,0:T(8,128)S(1)} %get-tuple-element.14.refs_0_), channel_id=1, source_target_pairs={{0,2},{1,3},{2,0},{3,1},{4,6},{5,7},{6,4},{7,5},{8,10},{9,11},{10,... | collective-permute-start | bytes 208904 | tf_op jit(solution)/shard_map/ppermute | solution.py:309
  17.6 0.0 collective-permute-done.5.refs_6_
  17.6 5.2 %collective-permute-start.17 = (f32[136,128]{1,0:T(8,128)S(1)}, f32[136,128]{1,0:T(8,128)S(1)}, u32[]{:S(2)}, u32[]{:S(2)}) collective-permute-start(f32[136,128]{1,0:T(8,128)S(1)} %get-tuple-element.14.refs_0_), channel_id=1, source_target_pairs={{0,4},{1,5},{2,6},{3,7},{4,0},{5,1},{6,2},{7,3},{8,12},{9,13},{10,... | collective-permute-start | bytes 208904 | tf_op jit(solution)/shard_map/ppermute | solution.py:309
  22.9 0.0 collective-permute-done.refs_1_
  22.9 0.3 collective-permute-start.19
  23.1 0.3 collective-permute-start.8
  23.5 3.9 %collective-permute-done.8.refs_10_ = f32[128,128]{1,0:T(8,128)S(1)} collective-permute-done((f32[128,128]{1,0:T(8,128)S(1)}, f32[128,128]{1,0:T(8,128)S(1)}, u32[]{:S(2)}, u32[]{:S(2)}) %collective-permute-start.8) | collective-permute-done | bytes 65568 | tf_op jit(solution)/shard_map/ppermute | solution.py:309
  27.4 0.5 %collective-permute-start.16 = (f32[136,128]{1,0:T(8,128)S(1)}, f32[136,128]{1,0:T(8,128)S(1)}, u32[]{:S(2)}, u32[]{:S(2)}) collective-permute-start(f32[136,128]{1,0:T(8,128)S(1)} %collective-permute-done.15.refs_2_), channel_id=1, source_target_pairs={{0,1},{1,0},{2,3},{3,2},{4,5},{5,4},{6,7},{7,6},{8,9},{9,8},{10,11... | collective-permute-start | bytes 208904 | tf_op jit(solution)/shard_map/ppermute | solution.py:309
  27.9 0.1 collective-permute-start.18
  28.0 1.0 %collective-permute-done.19.refs_6_ = f32[136,128]{1,0:T(8,128)S(1)} collective-permute-done((f32[136,128]{1,0:T(8,128)S(1)}, f32[136,128]{1,0:T(8,128)S(1)}, u32[]{:S(2)}, u32[]{:S(2)}) %collective-permute-start.19) | collective-permute-done | bytes 69664 | tf_op jit(solution)/shard_map/ppermute | solution.py:309
  29.0 0.5 %collective-permute-start.6 = (f32[128,128]{1,0:T(8,128)S(1)}, f32[128,128]{1,0:T(8,128)S(1)}, u32[]{:S(2)}, u32[]{:S(2)}) collective-permute-start(f32[128,128]{1,0:T(8,128)S(1)} %collective-permute-done.5.refs_6_), channel_id=1, source_target_pairs={{0,1},{1,0},{2,3},{3,2},{4,5},{5,4},{6,7},{7,6},{8,9},{9,8},{10,11... | collective-permute-start | bytes 196616 | tf_op jit(solution)/shard_map/ppermute | solution.py:309
  29.5 0.1 collective-permute-start.20
  29.6 0.7 %collective-permute-done.4.refs_5_ = f32[128,128]{1,0:T(8,128)S(1)} collective-permute-done((f32[128,128]{1,0:T(8,128)S(1)}, f32[128,128]{1,0:T(8,128)S(1)}, u32[]{:S(2)}, u32[]{:S(2)}) %collective-permute-start.4) | collective-permute-done | bytes 65568 | tf_op jit(solution)/shard_map/ppermute | solution.py:309
  30.2 0.2 collective-permute-start.7
  30.4 0.0 collective-permute-done.6.refs_7_
  30.4 0.4 collective-permute-start.11
  30.8 0.2 collective-permute-start.13
  30.9 0.4 collective-permute-start.9
  31.3 1.2 %copy-done = f32[8,128,256]{2,1,0:T(8,128)S(1)} copy-done((f32[8,128,256]{2,1,0:T(8,128)S(1)}, f32[8,128,256]{2,1,0:T(8,128)}, u32[]{:S(2)}) %copy-start) | copy-done | bytes 1048600
  32.5 1.0 %copy-done.2 = bf16[256,768]{1,0:T(8,128)(2,1)S(1)} copy-done((bf16[256,768]{1,0:T(8,128)(2,1)S(1)}, bf16[256,768]{1,0:T(8,128)(2,1)}, u32[]{:S(2)}) %copy-start.2) | copy-done | bytes 393240
  33.5 1.3 %shard_map.132.refs_8_.refs_18_ = f32[8,2,128,128]{3,2,1,0:T(8,128)S(1)} custom-call(f32[128,128]{1,0:T(8,128)S(1)} %get-tuple-element.12.refs_0_, f32[128,128]{1,0:T(8,128)S(1)} %collective-permute-done.refs_1_, f32[128,128]{1,0:T(8,128)S(1)} %collective-permute-done.1.refs_2_, f32[128,128]{1,0:T(8,128)S(1)} %collective-permute-done.2.refs_3_, ...), custom_call_target="tpu_custom_call" | custom-call | tf_op jit(solution)/shard_map/pallas_call | solution.py:298
  34.9 0.0 copy-start.4
  34.9 0.0 copy-start.6
  34.9 0.0 copy-start.8
  34.9 0.0 copy-start.9
  34.9 2.8 %shard_map.133 = (f32[8,128,128]{2,1,0:T(8,128)S(1)}, f32[8,128,128]{2,1,0:T(8,128)S(1)}) custom-call(f32[136,128]{1,0:T(8,128)S(1)} %get-tuple-element.14.refs_0_, f32[136,128]{1,0:T(8,128)S(1)} %collective-permute-done.14.refs_1_, f32[136,128]{1,0:T(8,128)S(1)} %collective-permute-done.15.refs_2_, f32[136,128]{1,0:T(8,128)S(1)} %collective-permute-done.16.refs_3_, ...), custom_call_target="tpu_custom_call" | custom-call | tf_op jit(solution)/shard_map/pallas_call | solution.py:298
  37.8 0.0 copy-start.14
  37.8 4.1 %shard_map.134 = (f32[128,128]{1,0:T(8,128)}, f32[16,2,128]{2,1,0:T(2,128)S(1)}, f32[16,2,128]{2,1,0:T(2,128)S(1)}, f32[16,2,128]{2,1,0:T(2,128)S(1)}, f32[16,2,128]{2,1,0:T(2,128)S(1)}) custom-call(f32[128,128]{1,0:T(8,128)S(1)} %get-tuple-element.12.refs_0_, f32[128,128]{1,0:T(8,128)S(1)} %collective-permute-done.refs_1_, ...), custom_call_target="tpu_custom_call" | custom-call | tf_op jit(solution)/shard_map/pallas_call | solution.py:298
  41.9 1.5 %collective-permute-start.21 = (f32[16,2,128]{2,1,0:T(2,128)S(1)}, f32[16,2,128]{2,1,0:T(2,128)S(1)}, u32[]{:S(2)}, u32[]{:S(2)}) collective-permute-start(f32[16,2,128]{2,1,0:T(2,128)S(1)} %get-tuple-element.19), channel_id=1, source_target_pairs={{0,8},{8,0},{16,24},{24,16},{1,9},{9,1},{17,25},{25,17},{2,10},{10... | collective-permute-start | bytes 49160 | tf_op jit(solution)/shard_map/ppermute | solution.py:309
  43.4 1.5 %collective-permute-start.22 = (f32[16,2,128]{2,1,0:T(2,128)S(1)}, f32[16,2,128]{2,1,0:T(2,128)S(1)}, u32[]{:S(2)}, u32[]{:S(2)}) collective-permute-start(f32[16,2,128]{2,1,0:T(2,128)S(1)} %get-tuple-element.20), channel_id=1, source_target_pairs={{0,16},{8,24},{16,0},{24,8},{1,17},{9,25},{17,1},{25,9},{2,18},{10... | collective-permute-start | bytes 49160 | tf_op jit(solution)/shard_map/ppermute | solution.py:309
  44.9 0.5 collective-permute-start.23
  45.4 0.2 collective-permute-done.21.refs_1_
  45.6 1.5 %collective-permute-done.22.refs_2_ = f32[16,2,128]{2,1,0:T(2,128)S(1)} collective-permute-done((f32[16,2,128]{2,1,0:T(2,128)S(1)}, f32[16,2,128]{2,1,0:T(2,128)S(1)}, u32[]{:S(2)}, u32[]{:S(2)}) %collective-permute-start.22) | collective-permute-done | bytes 16416 | tf_op jit(solution)/shard_map/ppermute | solution.py:309
  47.1 2.4 %collective-permute-done.23.refs_3_ = f32[16,2,128]{2,1,0:T(2,128)S(1)} collective-permute-done((f32[16,2,128]{2,1,0:T(2,128)S(1)}, f32[16,2,128]{2,1,0:T(2,128)S(1)}, u32[]{:S(2)}, u32[]{:S(2)}) %collective-permute-start.23) | collective-permute-done | bytes 16416 | tf_op jit(solution)/shard_map/ppermute | solution.py:309
  49.6 0.6 %shard_map.135 = f32[16,2,128]{2,1,0:T(2,128)} custom-call(f32[16,2,128]{2,1,0:T(2,128)S(1)} %get-tuple-element.18.refs_0_, f32[16,2,128]{2,1,0:T(2,128)S(1)} %collective-permute-done.21.refs_1_, f32[16,2,128]{2,1,0:T(2,128)S(1)} %collective-permute-done.22.refs_2_, f32[16,2,128]{2,1,0:T(2,128)S(1)} %collective-permute-done.23.refs_3_, ...), custom_call_target="tpu_custom_call" | custom-call | tf_op jit(solution)/shard_map/pallas_call | solution.py:298
  (35 shorter events, 0.1 us)
Async XLA Ops:
  0.6 0.8 %copy-start.5 = (f32[2048,8]{0,1:T(8,128)S(1)}, f32[2048,8]{0,1:T(8,128)}, u32[]{:S(2)}) copy-start(f32[2048,8]{0,1:T(8,128)} %param.14) | copy-start | bytes 196612
  1.5 0.8 %copy-start.7 = (f32[2048,8]{0,1:T(8,128)S(1)}, f32[2048,8]{0,1:T(8,128)}, u32[]{:S(2)}) copy-start(f32[2048,8]{0,1:T(8,128)} %param.15) | copy-start | bytes 196612
  2.3 0.8 %copy-start.12 = (s32[1,1,16384]{2,1,0:T(1,128)S(1)}, s32[1,1,16384]{2,1,0:T(1,128)}, u32[]{:S(2)}) copy-start(s32[1,1,16384]{2,1,0:T(1,128)} %param.12) | copy-start | bytes 196612
  3.2 0.8 %copy-start.13 = (f32[1,16384]{1,0:T(1,128)S(1)}, f32[1,16384]{1,0:T(1,128)}, u32[]{:S(2)}) copy-start(f32[1,16384]{1,0:T(1,128)} %param.13) | copy-start | bytes 196612
  4.0 27.3 %copy-start.3 = (f32[128,256]{1,0:T(8,128)S(1)}, f32[128,256]{1,0:T(8,128)}, u32[]{:S(2)}) copy-start(f32[128,256]{1,0:T(8,128)} %constant.16.clone.refs_10_.refs_11_.refs_23_) | copy-start | bytes 393220
  4.0 27.3 %copy-start.11 = (bf16[256,256]{1,0:T(8,128)(2,1)S(1)}, bf16[256,256]{1,0:T(8,128)(2,1)}, u32[]{:S(2)}) copy-start(bf16[256,256]{1,0:T(8,128)(2,1)} %constant.14.clone.refs_8_) | copy-start | bytes 393220
  4.1 7.6 %collective-permute-start.1 = (f32[128,128]{1,0:T(8,128)S(1)}, f32[128,128]{1,0:T(8,128)S(1)}, u32[]{:S(2)}, u32[]{:S(2)}) collective-permute-start(f32[128,128]{1,0:T(8,128)S(1)} %get-tuple-element.12.refs_0_), channel_id=1, source_target_pairs={{0,2},{1,3},{2,0},{3,1},{4,6},{5,7},{6,4},{7,5},{8,10},{9,11},{10,... | collective-permute-start | bytes 196616 | tf_op jit(solution)/shard_map/ppermute | solution.py:309
  7.2 7.4 %collective-permute-start.3 = (f32[128,128]{1,0:T(8,128)S(1)}, f32[128,128]{1,0:T(8,128)S(1)}, u32[]{:S(2)}, u32[]{:S(2)}) collective-permute-start(f32[128,128]{1,0:T(8,128)S(1)} %get-tuple-element.12.refs_0_), channel_id=1, source_target_pairs={{0,4},{1,5},{2,6},{3,7},{4,0},{5,1},{6,2},{7,3},{8,12},{9,13},{10,... | collective-permute-start | bytes 196616 | tf_op jit(solution)/shard_map/ppermute | solution.py:309
  9.8 7.9 %collective-permute-start.5 = (f32[128,128]{1,0:T(8,128)S(1)}, f32[128,128]{1,0:T(8,128)S(1)}, u32[]{:S(2)}, u32[]{:S(2)}) collective-permute-start(f32[128,128]{1,0:T(8,128)S(1)} %get-tuple-element.12.refs_0_), channel_id=1, source_target_pairs={{0,6},{1,7},{2,4},{3,5},{4,2},{5,3},{6,0},{7,1},{8,14},{9,15},{10,... | collective-permute-start | bytes 196616 | tf_op jit(solution)/shard_map/ppermute | solution.py:309
  9.8 13.1 %collective-permute-start = (f32[128,128]{1,0:T(8,128)S(1)}, f32[128,128]{1,0:T(8,128)S(1)}, u32[]{:S(2)}, u32[]{:S(2)}) collective-permute-start(f32[128,128]{1,0:T(8,128)S(1)} %get-tuple-element.12.refs_0_), channel_id=1, source_target_pairs={{0,1},{1,0},{2,3},{3,2},{4,5},{5,4},{6,7},{7,6},{8,9},{9,8},{10,11... | collective-permute-start | bytes 196616 | tf_op jit(solution)/shard_map/ppermute | solution.py:309
  9.8 13.4 %collective-permute-start.10 = (f32[128,128]{1,0:T(8,128)S(1)}, f32[128,128]{1,0:T(8,128)S(1)}, u32[]{:S(2)}, u32[]{:S(2)}) collective-permute-start(f32[128,128]{1,0:T(8,128)S(1)} %get-tuple-element.13.refs_8_), channel_id=1, source_target_pairs={{0,4},{1,5},{2,6},{3,7},{4,0},{5,1},{6,2},{7,3},{8,12},{9,13},{10,... | collective-permute-start | bytes 196616 | tf_op jit(solution)/shard_map/ppermute | solution.py:309
  11.7 11.8 %collective-permute-start.12 = (f32[128,128]{1,0:T(8,128)S(1)}, f32[128,128]{1,0:T(8,128)S(1)}, u32[]{:S(2)}, u32[]{:S(2)}) collective-permute-start(f32[128,128]{1,0:T(8,128)S(1)} %get-tuple-element.13.refs_8_), channel_id=1, source_target_pairs={{0,6},{1,7},{2,4},{3,5},{4,2},{5,3},{6,0},{7,1},{8,14},{9,15},{10,... | collective-permute-start | bytes 196616 | tf_op jit(solution)/shard_map/ppermute | solution.py:309
  14.5 12.9 %collective-permute-start.15 = (f32[136,128]{1,0:T(8,128)S(1)}, f32[136,128]{1,0:T(8,128)S(1)}, u32[]{:S(2)}, u32[]{:S(2)}) collective-permute-start(f32[136,128]{1,0:T(8,128)S(1)} %get-tuple-element.14.refs_0_), channel_id=1, source_target_pairs={{0,2},{1,3},{2,0},{3,1},{4,6},{5,7},{6,4},{7,5},{8,10},{9,11},{10,... | collective-permute-start | bytes 208904 | tf_op jit(solution)/shard_map/ppermute | solution.py:309
  17.6 10.3 %collective-permute-start.17 = (f32[136,128]{1,0:T(8,128)S(1)}, f32[136,128]{1,0:T(8,128)S(1)}, u32[]{:S(2)}, u32[]{:S(2)}) collective-permute-start(f32[136,128]{1,0:T(8,128)S(1)} %get-tuple-element.14.refs_0_), channel_id=1, source_target_pairs={{0,4},{1,5},{2,6},{3,7},{4,0},{5,1},{6,2},{7,3},{8,12},{9,13},{10,... | collective-permute-start | bytes 208904 | tf_op jit(solution)/shard_map/ppermute | solution.py:309
  22.9 6.1 %collective-permute-start.19 = (f32[136,128]{1,0:T(8,128)S(1)}, f32[136,128]{1,0:T(8,128)S(1)}, u32[]{:S(2)}, u32[]{:S(2)}) collective-permute-start(f32[136,128]{1,0:T(8,128)S(1)} %get-tuple-element.14.refs_0_), channel_id=1, source_target_pairs={{0,6},{1,7},{2,4},{3,5},{4,2},{5,3},{6,0},{7,1},{8,14},{9,15},{10,... | collective-permute-start | bytes 208904 | tf_op jit(solution)/shard_map/ppermute | solution.py:309
  23.1 4.3 %collective-permute-start.8 = (f32[128,128]{1,0:T(8,128)S(1)}, f32[128,128]{1,0:T(8,128)S(1)}, u32[]{:S(2)}, u32[]{:S(2)}) collective-permute-start(f32[128,128]{1,0:T(8,128)S(1)} %get-tuple-element.13.refs_8_), channel_id=1, source_target_pairs={{0,2},{1,3},{2,0},{3,1},{4,6},{5,7},{6,4},{7,5},{8,10},{9,11},{10,... | collective-permute-start | bytes 196616 | tf_op jit(solution)/shard_map/ppermute | solution.py:309
  23.5 5.5 %collective-permute-start.14 = (f32[136,128]{1,0:T(8,128)S(1)}, f32[136,128]{1,0:T(8,128)S(1)}, u32[]{:S(2)}, u32[]{:S(2)}) collective-permute-start(f32[136,128]{1,0:T(8,128)S(1)} %get-tuple-element.14.refs_0_), channel_id=1, source_target_pairs={{0,1},{1,0},{2,3},{3,2},{4,5},{5,4},{6,7},{7,6},{8,9},{9,8},{10,11... | collective-permute-start | bytes 208904 | tf_op jit(solution)/shard_map/ppermute | solution.py:309
  27.4 2.1 %collective-permute-start.2 = (f32[128,128]{1,0:T(8,128)S(1)}, f32[128,128]{1,0:T(8,128)S(1)}, u32[]{:S(2)}, u32[]{:S(2)}) collective-permute-start(f32[128,128]{1,0:T(8,128)S(1)} %collective-permute-done.1.refs_2_), channel_id=1, source_target_pairs={{0,1},{1,0},{2,3},{3,2},{4,5},{5,4},{6,7},{7,6},{8,9},{9,8},{10,11... | collective-permute-start | bytes 196616 | tf_op jit(solution)/shard_map/ppermute | solution.py:309
  27.4 3.3 %collective-permute-start.16 = (f32[136,128]{1,0:T(8,128)S(1)}, f32[136,128]{1,0:T(8,128)S(1)}, u32[]{:S(2)}, u32[]{:S(2)}) collective-permute-start(f32[136,128]{1,0:T(8,128)S(1)} %collective-permute-done.15.refs_2_), channel_id=1, source_target_pairs={{0,1},{1,0},{2,3},{3,2},{4,5},{5,4},{6,7},{7,6},{8,9},{9,8},{10,11... | collective-permute-start | bytes 208904 | tf_op jit(solution)/shard_map/ppermute | solution.py:309
  27.9 3.0 %collective-permute-start.18 = (f32[136,128]{1,0:T(8,128)S(1)}, f32[136,128]{1,0:T(8,128)S(1)}, u32[]{:S(2)}, u32[]{:S(2)}) collective-permute-start(f32[136,128]{1,0:T(8,128)S(1)} %collective-permute-done.17.refs_4_), channel_id=1, source_target_pairs={{0,1},{1,0},{2,3},{3,2},{4,5},{5,4},{6,7},{7,6},{8,9},{9,8},{10,11... | collective-permute-start | bytes 208904 | tf_op jit(solution)/shard_map/ppermute | solution.py:309
  29.0 1.3 %collective-permute-start.4 = (f32[128,128]{1,0:T(8,128)S(1)}, f32[128,128]{1,0:T(8,128)S(1)}, u32[]{:S(2)}, u32[]{:S(2)}) collective-permute-start(f32[128,128]{1,0:T(8,128)S(1)} %collective-permute-done.3.refs_4_), channel_id=1, source_target_pairs={{0,1},{1,0},{2,3},{3,2},{4,5},{5,4},{6,7},{7,6},{8,9},{9,8},{10,11... | collective-permute-start | bytes 196616 | tf_op jit(solution)/shard_map/ppermute | solution.py:309
  29.0 1.4 %collective-permute-start.6 = (f32[128,128]{1,0:T(8,128)S(1)}, f32[128,128]{1,0:T(8,128)S(1)}, u32[]{:S(2)}, u32[]{:S(2)}) collective-permute-start(f32[128,128]{1,0:T(8,128)S(1)} %collective-permute-done.5.refs_6_), channel_id=1, source_target_pairs={{0,1},{1,0},{2,3},{3,2},{4,5},{5,4},{6,7},{7,6},{8,9},{9,8},{10,11... | collective-permute-start | bytes 196616 | tf_op jit(solution)/shard_map/ppermute | solution.py:309
  29.5 5.4 %collective-permute-start.20 = (f32[136,128]{1,0:T(8,128)S(1)}, f32[136,128]{1,0:T(8,128)S(1)}, u32[]{:S(2)}, u32[]{:S(2)}) collective-permute-start(f32[136,128]{1,0:T(8,128)S(1)} %collective-permute-done.19.refs_6_), channel_id=1, source_target_pairs={{0,1},{1,0},{2,3},{3,2},{4,5},{5,4},{6,7},{7,6},{8,9},{9,8},{10,11... | collective-permute-start | bytes 208904 | tf_op jit(solution)/shard_map/ppermute | solution.py:309
  30.2 7.5 %collective-permute-start.7 = (f32[128,128]{1,0:T(8,128)S(1)}, f32[128,128]{1,0:T(8,128)S(1)}, u32[]{:S(2)}, u32[]{:S(2)}) collective-permute-start(f32[128,128]{1,0:T(8,128)S(1)} %get-tuple-element.13.refs_8_), channel_id=1, source_target_pairs={{0,1},{1,0},{2,3},{3,2},{4,5},{5,4},{6,7},{7,6},{8,9},{9,8},{10,11... | collective-permute-start | bytes 196616 | tf_op jit(solution)/shard_map/ppermute | solution.py:309
  30.4 7.3 %collective-permute-start.11 = (f32[128,128]{1,0:T(8,128)S(1)}, f32[128,128]{1,0:T(8,128)S(1)}, u32[]{:S(2)}, u32[]{:S(2)}) collective-permute-start(f32[128,128]{1,0:T(8,128)S(1)} %collective-permute-done.10.refs_12_), channel_id=1, source_target_pairs={{0,1},{1,0},{2,3},{3,2},{4,5},{5,4},{6,7},{7,6},{8,9},{9,8},{10,11... | collective-permute-start | bytes 196616 | tf_op jit(solution)/shard_map/ppermute | solution.py:309
  30.8 7.0 %collective-permute-start.13 = (f32[128,128]{1,0:T(8,128)S(1)}, f32[128,128]{1,0:T(8,128)S(1)}, u32[]{:S(2)}, u32[]{:S(2)}) collective-permute-start(f32[128,128]{1,0:T(8,128)S(1)} %collective-permute-done.12.refs_14_), channel_id=1, source_target_pairs={{0,1},{1,0},{2,3},{3,2},{4,5},{5,4},{6,7},{7,6},{8,9},{9,8},{10,11... | collective-permute-start | bytes 196616 | tf_op jit(solution)/shard_map/ppermute | solution.py:309
  30.9 6.8 %collective-permute-start.9 = (f32[128,128]{1,0:T(8,128)S(1)}, f32[128,128]{1,0:T(8,128)S(1)}, u32[]{:S(2)}, u32[]{:S(2)}) collective-permute-start(f32[128,128]{1,0:T(8,128)S(1)} %collective-permute-done.8.refs_10_), channel_id=1, source_target_pairs={{0,1},{1,0},{2,3},{3,2},{4,5},{5,4},{6,7},{7,6},{8,9},{9,8},{10,11... | collective-permute-start | bytes 196616 | tf_op jit(solution)/shard_map/ppermute | solution.py:309
  31.3 1.2 %copy-start = (f32[8,128,256]{2,1,0:T(8,128)S(1)}, f32[8,128,256]{2,1,0:T(8,128)}, u32[]{:S(2)}) copy-start(f32[8,128,256]{2,1,0:T(8,128)} %constant.17.clone.refs_11_.refs_12_.refs_24_) | copy-start | bytes 3145732
  32.5 1.0 %copy-start.2 = (bf16[256,768]{1,0:T(8,128)(2,1)S(1)}, bf16[256,768]{1,0:T(8,128)(2,1)}, u32[]{:S(2)}) copy-start(bf16[256,768]{1,0:T(8,128)(2,1)} %constant.15.clone.refs_9_) | copy-start | bytes 1179652
  33.5 1.4 %copy-start.1 = (f32[8,128,256]{2,1,0:T(8,128)S(1)}, f32[8,128,256]{2,1,0:T(8,128)}, u32[]{:S(2)}) copy-start(f32[8,128,256]{2,1,0:T(8,128)} %constant.17.clone.refs_11_.refs_12_.refs_24_) | copy-start | bytes 3145732
  33.5 1.4 %copy-start.10 = (bf16[768,128]{1,0:T(8,128)(2,1)S(1)}, bf16[768,128]{1,0:T(8,128)(2,1)}, u32[]{:S(2)}) copy-start(bf16[768,128]{1,0:T(8,128)(2,1)} %constant.18.clone.refs_10_) | copy-start | bytes 589828
  34.9 2.9 %copy-start.4 = (bf16[8,32,768]{2,1,0:T(8,128)(2,1)S(1)}, bf16[8,32,768]{2,1,0:T(8,128)(2,1)}, u32[]{:S(2)}) copy-start(bf16[8,32,768]{2,1,0:T(8,128)(2,1)} %constant.19.clone.refs_21_) | copy-start | bytes 1179652
  34.9 2.9 %copy-start.6 = (f32[2048,8]{0,1:T(8,128)S(1)}, f32[2048,8]{0,1:T(8,128)}, u32[]{:S(2)}) copy-start(f32[2048,8]{0,1:T(8,128)} %param.14) | copy-start | bytes 196612
  34.9 2.9 %copy-start.8 = (f32[2048,8]{0,1:T(8,128)S(1)}, f32[2048,8]{0,1:T(8,128)}, u32[]{:S(2)}) copy-start(f32[2048,8]{0,1:T(8,128)} %param.15) | copy-start | bytes 196612
  34.9 2.9 %copy-start.9 = (bf16[384,256]{1,0:T(8,128)(2,1)S(1)}, bf16[384,256]{1,0:T(8,128)(2,1)}, u32[]{:S(2)}) copy-start(bf16[384,256]{1,0:T(8,128)(2,1)} %constant.20.clone.refs_22_) | copy-start | bytes 589828
  37.8 11.8 %copy-start.14 = (f32[2048,2]{0,1:T(2,128)S(1)}, f32[2048,2]{0,1:T(2,128)}, u32[]{:S(2)}) copy-start(f32[2048,2]{0,1:T(2,128)} %param.16) | copy-start | bytes 49156
  41.9 3.7 %collective-permute-start.21 = (f32[16,2,128]{2,1,0:T(2,128)S(1)}, f32[16,2,128]{2,1,0:T(2,128)S(1)}, u32[]{:S(2)}, u32[]{:S(2)}) collective-permute-start(f32[16,2,128]{2,1,0:T(2,128)S(1)} %get-tuple-element.19), channel_id=1, source_target_pairs={{0,8},{8,0},{16,24},{24,16},{1,9},{9,1},{17,25},{25,17},{2,10},{10... | collective-permute-start | bytes 49160 | tf_op jit(solution)/shard_map/ppermute | solution.py:309
  43.4 3.7 %collective-permute-start.22 = (f32[16,2,128]{2,1,0:T(2,128)S(1)}, f32[16,2,128]{2,1,0:T(2,128)S(1)}, u32[]{:S(2)}, u32[]{:S(2)}) collective-permute-start(f32[16,2,128]{2,1,0:T(2,128)S(1)} %get-tuple-element.20), channel_id=1, source_target_pairs={{0,16},{8,24},{16,0},{24,8},{1,17},{9,25},{17,1},{25,9},{2,18},{10... | collective-permute-start | bytes 49160 | tf_op jit(solution)/shard_map/ppermute | solution.py:309
  44.9 4.6 %collective-permute-start.23 = (f32[16,2,128]{2,1,0:T(2,128)S(1)}, f32[16,2,128]{2,1,0:T(2,128)S(1)}, u32[]{:S(2)}, u32[]{:S(2)}) collective-permute-start(f32[16,2,128]{2,1,0:T(2,128)S(1)} %get-tuple-element.21), channel_id=1, source_target_pairs={{0,24},{8,16},{16,8},{24,0},{1,25},{9,17},{17,9},{25,1},{2,26},{10... | collective-permute-start | bytes 49160 | tf_op jit(solution)/shard_map/ppermute | solution.py:309

commit v2 on v1

--- a/solution.py
+++ b/solution.py
@@ -28,44 +28,16 @@
 @functools.cache
 def tables(rows):
     index = np.arange(lanes, dtype=np.float64)
-    row_len = lanes * lanes
     turn = -2.0 * np.pi
     c, s = angle_parts(turn * (np.outer(index, index) % lanes) / lanes)
-    forward = np.block([[c, s], [-s, c]])
-    high, low = split_table(forward)
-    right = np.concatenate([high, high, low], 0)
-    left = np.ascontiguousarray(right.T)
-    real_high, real_low = high[:lanes], low[:lanes]
-    sign_right = np.concatenate([real_high, real_low], 0)
-    real_right = np.concatenate([real_high, real_high, real_low], 0)
-    back_high, back_low = split_table(np.concatenate([c, s], 0))
-    back_right = np.concatenate([back_high, back_high, back_low], 0)
+    c_high, c_low = split_table(c)
+    s_high, s_low = split_table(s)
+    row_len = lanes * lanes
     wc, ws = angle_parts(turn * np.outer(index, index) / row_len)
-    small_turn = np.concatenate([wc, ws], 1).astype(np.float32)
-    flat = (index[:, None] * lanes + index[None, :])[None]
-    row = np.arange(rows, dtype=np.float64)[:, None, None]
-    gc, gs = angle_parts(turn * flat * row / (rows * row_len))
-    big_turn = np.concatenate([gc, gs], 2).astype(np.float32)
-    return {
-        "right": right,
-        "left": left,
-        "sign_right": sign_right,
-        "real_right": real_right,
-        "back_right": back_right,
-        "small_turn": small_turn,
-        "big_turn": big_turn,
-    }
-
-
-@functools.cache
-def block_left(rows):
-    left = tables(rows)["left"]
-    depth = lanes // rows
-    parts = [
-        np.concatenate([left[k * depth : (k + 1) * depth], left[lanes + k * depth : lanes + (k + 1) * depth]], 0)
-        for k in range(rows)
-    ]
-    return np.stack(parts)
+    flat = index[:, None] * lanes + index[None, :]
+    gc, gs = angle_parts(turn * flat / (rows * row_len))
+    turns = np.stack([np.concatenate([wc, ws], 1), np.concatenate([gc, gs], 1)])
+    return np.stack([c_high, s_high, c_low, s_low]), turns.astype(np.float32)
 
 
 def split(x):
@@ -129,27 +101,53 @@
     return [(odd if r % 2 else even)[r // 2] for r in range(n)]
 
 
-def pack_kernel(half, bits, noise, kernel, symbol, signs_out, spectra_out, noise_out):
-    signs_out[...] = (2 * bits[...] - 1).astype(exact).T
-    noise_out[...] = noise[...].T
+def pack_kernel(half, *refs):
+    sources, out, landed, done = refs[:4], refs[4], refs[5:9], refs[9]
+    copies = [pltpu.make_async_copy(sources[i], landed[i], done.at[i]) for i in range(4)]
+    for copy in copies:
+        copy.start()
+    bits, noise, kernel, symbol = landed
+    copies[0].wait()
+    out[:lanes] = (2 * bits[...] - 1).astype(exact).T
+    copies[1].wait()
+    out[lanes : 2 * lanes] = noise[...].T
+    copies[2].wait()
+    copies[3].wait()
     depth = kernel.shape[0]
     for a in range(half):
-        spectra_out[a * depth : (a + 1) * depth] = kernel[:, a]
-        spectra_out[(half + a) * depth : (half + a + 1) * depth] = symbol[:, a]
+        at = 2 * lanes + a * depth
+        out[at : at + depth] = kernel[:, a]
+        at += half * depth
+        out[at : at + depth] = symbol[:, a]
     middle = jnp.concatenate([kernel[0, half : half + 1], symbol[0, half : half + 1]], 0)
-    spectra_out[2 * half * depth :] = jnp.concatenate([middle] * (lead // 2), 0)
+    out[2 * (lanes + half * depth) :] = jnp.concatenate([middle] * (lead // 2), 0)
 
 
 def spectrum_kernel(rows, *refs):
-    signs = refs[:rows]
-    sign_right, left, small_turn, big_turn, spectrum, work = refs[rows:]
+    blocks = refs[:rows]
+    dft, turns, spectrum, left, big_turn, work = refs[rows:]
     me = lax.axis_index("seq")
-    wc, ws = small_turn[:, :lanes], small_turn[:, lanes:]
+    c_high, s_high, c_low, s_low = (dft[k] for k in range(4))
+    left[:lanes] = jnp.concatenate([c_high, -s_high, c_high, -s_high, c_low, -s_low], 1)
+    left[lanes:] = jnp.concatenate([s_high, c_high, s_high, c_high, s_low, c_low], 1)
+    sign_right = jnp.concatenate(
+        [jnp.concatenate([c_high, s_high], 1), jnp.concatenate([c_low, s_low], 1)], 0
+    )
+    for t in range(0, lanes, lead):
+        at = slice(t, t + lead)
+        one = turns[1, at, :lanes], turns[1, at, lanes:]
+        powers = [(jnp.ones((lead, lanes), exact), jnp.zeros((lead, lanes), exact)), one]
+        for r in range(2, rows):
+            powers.append(turned(*powers[r // 2], *powers[r - r // 2]))
+        for r in range(rows):
+            big_turn[r, at, :lanes] = powers[r][0]
+            big_turn[r, at, lanes:] = powers[r][1]
+    wc, ws = turns[0, :, :lanes], turns[0, :, lanes:]
     for pair in range(rows // 2):
         columns = []
         for j in (2 * pair, 2 * pair + 1):
-            x = signs[j][...].astype(near)
-            section = times(jnp.concatenate([x, x], 1), sign_right[...])
+            x = blocks[j][:lanes].astype(near)
+            section = times(jnp.concatenate([x, x], 1), sign_right)
             columns.append(stacked(*turned(section[:, :lanes], section[:, lanes:], wc, ws), 0))
         done = times(left[...], jnp.concatenate(columns, 1))
         for k, j in enumerate((2 * pair, 2 * pair + 1)):
@@ -168,7 +166,7 @@
 
 def inverse_kernel(rows, *refs):
     blocks = refs[:rows]
-    spectrum, left, back_right, small_turn, big_turn, precond, circulant, kernel, symbol, ends, work = refs[rows:]
+    spectrum, left, dft, turns, big_turn, precond, circulant, kernel, symbol, ends, work = refs[rows:]
     half = rows // 2
     depth = lanes // rows
     samples = rows * lanes * lanes
@@ -176,9 +174,11 @@
     for j in range(rows):
         place = pl.multiple_of((me ^ j) * depth, depth)
         for a in range(half):
-            kernel[a, pl.ds(place, depth)] = blocks[j][a * depth : (a + 1) * depth]
-            symbol[a, pl.ds(place, depth)] = blocks[j][(half + a) * depth : (half + a + 1) * depth]
-        ends[me ^ j] = blocks[j][2 * half * depth :]
+            at = 2 * lanes + a * depth
+            kernel[a, pl.ds(place, depth)] = blocks[j][at : at + depth]
+            at += half * depth
+            symbol[a, pl.ds(place, depth)] = blocks[j][at : at + depth]
+        ends[me ^ j] = blocks[j][2 * lanes + 2 * half * depth :]
     middle = spectrum[half, 0, 0:1, 0:1] / ends[0, 1:2, 0:1] / samples
     middle_image = middle * ends[0, 0:1, 0:1]
     for t in range(0, lanes, lead):
@@ -200,7 +200,8 @@
                 re, im = turned_back(*out[r], big_turn[r, at, :lanes], big_turn[r, at, lanes:])
                 work[r, field, 0, at] = re
                 work[r, field, 1, at] = im
-    wc, ws = small_turn[:, :lanes], small_turn[:, lanes:]
+    wc, ws = turns[0, :, :lanes], turns[0, :, lanes:]
+    back_right = jnp.concatenate([dft[k] for k in (0, 1, 0, 1, 2, 3)], 0)
     for r in range(rows):
         columns = [stacked(work[r, field, 1], work[r, field, 0], 0) for field in range(2)]
         done = times(left[...], jnp.concatenate(columns, 1))
@@ -208,7 +209,7 @@
         for field in range(2):
             at = slice(field * lanes, (field + 1) * lanes)
             lined.append(stacked(*turned_back(done[lanes:, at], done[:lanes, at], wc, ws), 1))
-        done = times(jnp.concatenate(lined, 0), back_right[...])
+        done = times(jnp.concatenate(lined, 0), back_right)
         sign = 1.0 if r % 2 == 0 else -1.0
         precond[r] = done[:lanes] + sign * middle
         circulant[r] = done[lanes:] + sign * middle_image
@@ -219,9 +220,10 @@
 
 
 def adjoint_kernel(rows, probes, *refs):
-    signs, noises = refs[:rows], refs[rows : 2 * rows]
-    refs = refs[2 * rows :]
-    precond, circulant, spectrum, kernel, symbol, block, real_right, small_turn, big_turn, residual_out = refs[:10]
+    signs = [refs[j].at[:lanes] for j in range(rows)]
+    noises = [refs[j].at[lanes : 2 * lanes] for j in range(rows)]
+    refs = refs[rows:]
+    precond, circulant, spectrum, kernel, symbol, left, dft, turns, big_turn, residual_out = refs[:10]
     outs = refs[10 : 10 + probes]
     image, field, work, shares = refs[10 + probes :]
     depth = lanes // rows
@@ -244,20 +246,22 @@
         field[j] = residual
     weight = -2.0 * whole_sum(cross)
     residual_out[...] = field[0].T
-    wc, ws = small_turn[:, :lanes], small_turn[:, lanes:]
+    wc, ws = turns[0, :, :lanes], turns[0, :, lanes:]
     own = pl.multiple_of(me * depth, depth)
+    real_right = jnp.concatenate([jnp.concatenate([dft[k], dft[k + 1]], 1) for k in (0, 0, 2)], 0)
+    block = jnp.concatenate([left[pl.ds(own, depth)], left[pl.ds(pl.multiple_of(lanes + own, depth), depth)]], 0)
     for j in range(rows):
         r = me ^ j
         lined = []
         for x in (precond[r], field[j]):
             high, low = split(noises[j][...] * x)
             lined.append(jnp.concatenate([high, low, high], 1))
-        section = times(jnp.concatenate(lined, 0), real_right[...])
+        section = times(jnp.concatenate(lined, 0), real_right)
         columns = []
         for k in range(2):
             at = slice(k * lanes, (k + 1) * lanes)
             columns.append(stacked(*turned(section[at, :lanes], section[at, lanes:], wc, ws), 0))
-        done = times(block[me], jnp.concatenate(columns, 1))
+        done = times(block, jnp.concatenate(columns, 1))
         gc, gs = big_turn[r, pl.ds(own, depth), :lanes], big_turn[r, pl.ds(own, depth), lanes:]
         for k in range(2):
             at = slice(k * lanes, (k + 1) * lanes)
@@ -287,14 +291,10 @@
             outs[d][:, k] = shares[(column ^ d) * width + k]
 
 
-def finish_kernel(probes, *refs):
-    parts, before, out = refs[:probes], refs[probes], refs[probes + 1]
-    out[...] = before[...] + sum(part[...] for part in parts) / probes
-
-
 def call(kernel, outs, scratch, *operands):
     whole = pl.BlockSpec(memory_space=pltpu.VMEM)
-    shapes = tuple(jax.ShapeDtypeStruct(shape, exact) for shape in outs)
+    typed = [out if isinstance(out[0], tuple) else (out, exact) for out in outs]
+    shapes = tuple(jax.ShapeDtypeStruct(shape, dtype) for shape, dtype in typed)
     return pl.pallas_call(
         kernel,
         out_shape=shapes,
@@ -309,76 +309,81 @@
     return lax.ppermute(x, axis, [(i, i ^ d) for i in range(lax.axis_size(axis))])
 
 
+def after(x, *earlier):
+    return lax.optimization_barrier((x, *earlier))[0]
+
+
 def spread(x):
-    near_block = swapped(x, "seq", 1)
-    got = [x, near_block]
-    for d in range(2, lax.axis_size("seq"), 2):
-        there = swapped(x, "seq", d)
-        got += [there, swapped(there, "seq", 1)]
-    return got
+    got = {1: swapped(x, "seq", 1)}
+    for d in reversed(range(2, lax.axis_size("seq"), 2)):
+        got[d] = swapped(x, "seq", d)
+        got[d + 1] = swapped(got[d], "seq", 1)
+    return [x] + [got[d] for d in sorted(got)]
 
 
 def gathered_shards(probe_bits, noise_var, kernel_spectrum, symbol, grad_prev):
     rows = kernel_spectrum.shape[1]
     probes = lax.axis_size("probe")
     half, depth, width = rows // 2, lanes // rows, rows // probes
-    t = tables(rows)
     kernel = kernel_spectrum.T.reshape(rows, depth, lanes).transpose(1, 0, 2)
     symbols = symbol.T.reshape(rows, depth, lanes).transpose(1, 0, 2)
     before = grad_prev.T.reshape(width, depth, lanes).transpose(1, 0, 2)
     square = (lanes, lanes)
-    signs, spectra, noise = call(
+    dft, turns = tables(rows)
+    packed = (2 * (lanes + half * depth) + lead, lanes)
+    block = pl.pallas_call(
         functools.partial(pack_kernel, half),
-        [square, (2 * half * depth + lead, lanes), square],
-        [],
-        probe_bits.reshape(square),
-        noise_var.reshape(square),
-        kernel,
-        symbols,
-    )
-    signs, spectra, noise = spread(signs), spread(spectra), spread(noise)
+        out_shape=jax.ShapeDtypeStruct(packed, exact),
+        in_specs=[pl.BlockSpec(memory_space=pl.ANY)] * 4,
+        out_specs=pl.BlockSpec(memory_space=pltpu.VMEM),
+        scratch_shapes=[
+            pltpu.VMEM(square, jnp.int32),
+            pltpu.VMEM(square, exact),
+            pltpu.VMEM(kernel.shape, exact),
+            pltpu.VMEM(kernel.shape, exact),
+            pltpu.SemaphoreType.DMA((4,)),
+        ],
+    )(probe_bits.reshape(square), noise_var.reshape(square), kernel, symbols)
+    blocks = spread(block)
     whole = (rows, 2, *square)
-    (spectrum,) = call(
+    spectrum, left, big_turn = call(
         functools.partial(spectrum_kernel, rows),
+        [whole, ((2 * lanes, 6 * lanes), near), (rows, lanes, 2 * lanes)],
         [whole],
-        [whole],
-        *signs,
-        t["sign_right"],
-        t["left"],
-        t["small_turn"],
-        t["big_turn"],
+        *blocks,
+        dft,
+        turns,
     )
     field = (rows, *square)
     precond, circulant = call(
         functools.partial(inverse_kernel, rows),
         [field, field],
         [(half, *square), (half, *square), (rows, lead, lanes), (rows, 2, 2, *square)],
-        *spectra,
+        *blocks,
         spectrum,
-        t["left"],
-        t["back_right"],
-        t["small_turn"],
-        t["big_turn"],
+        left,
+        dft,
+        turns,
+        big_turn,
     )
     share = (depth, width, lanes)
     residual, *parts = call(
         functools.partial(adjoint_kernel, rows, probes),
         [square] + [share] * probes,
         [field, field, (rows, 2, 2, depth, lanes), (rows, depth, lanes)],
-        *signs,
-        *noise,
+        *blocks,
         precond,
         circulant,
         spectrum,
         kernel,
         symbols,
-        block_left(rows),
-        t["real_right"],
-        t["small_turn"],
-        t["big_turn"],
-    )
-    parts = [parts[0]] + [swapped(parts[d], "probe", d) for d in range(1, probes)]
-    (total,) = call(functools.partial(finish_kernel, probes), [share], [], *parts, before)
+        left,
+        dft,
+        turns,
+        big_turn,
+    )
+    arrived = [swapped(parts[d], "probe", d) for d in reversed(range(1, probes))]
+    total = before + sum(arrived, parts[0]) / probes
     total = total.transpose(1, 0, 2).reshape(width, depth * lanes).T
     return residual.reshape(probe_bits.shape), total
 

time: 50.6 us -> 43.4 us (0.86)
  starting transfers between devices: 24.6 us -> 9.76 us
  waiting for transfers between devices: 10.3 us -> 21 us
  local copies, waits for them, and re-layouts: 5.62 us -> 0.97 us
  Pallas kernels: 8.93 us -> 10.2 us
  other arithmetic: 0 us -> 0.63 us
    ppermute x24 -> x10, starting transfers between devices: 24.6 us -> 9.76 us  [swapped(): lax.ppermute(x, axis, [(i, i ^ d) for i in range(lax.axis_size(axis))])]
    ppermute x24 -> x10, waiting for transfers between devices: 10.3 us -> 21 us  [swapped(): lax.ppermute(x, axis, [(i, i ^ d) for i in range(lax.axis_size(axis))])]
    unnamed x30 -> x14, local copies, waits for them, and re-layouts: 5.62 us -> 0.97 us
    pallas_call x0 -> x1, Pallas kernels: none -> 1.84 us  [gathered_shards(): pl.pallas_call(functools.partial(pack_kernel, half), out_shape=jax.ShapeD...]
    transpose x0 -> x1, other arithmetic: none -> 0.63 us  [gathered_shards(): total = total.transpose(1, 0, 2).reshape(width, depth * lanes).T]
    pallas_call x5 -> x3, Pallas kernels: 8.93 us -> 8.34 us  [call(): pl.pallas_call(kernel, out_shape=shapes, in_specs=[whole] * len(operands)...]
  transfers between devices with their start and end apart: 24 -> 10, of which waited for: 7 -> 7; matrix products, arithmetic and copies ran while one was open for 0% -> 0% of each run, Pallas kernels for 8% -> 0%
where the time goes in v2:
time: 43.4 us; the launch traced here: 43.3 us
  waiting for transfers between devices  21 us (48%)
  Pallas kernels  10.2 us (24%)
  starting transfers between devices  9.76 us (22%)
  local copies, waits for them, and re-layouts  0.97 us (2%)
  between operations  0.73 us (2%)
  other arithmetic  0.63 us (1%)
    ppermute x10, waiting for transfers between devices, swapped(): lax.ppermute(x, axis, [(i, i ^ d) for i in range(lax.axis_size(axis))])  21 us
    ppermute x10, starting transfers between devices, swapped(): lax.ppermute(x, axis, [(i, i ^ d) for i in range(lax.axis_size(axis))])  9.76 us
    pallas_call x3, Pallas kernels, call(): pl.pallas_call(kernel, out_shape=shapes, in_specs=[whole] * len(operands)...  8.34 us
    pallas_call x1, Pallas kernels, gathered_shards(): pl.pallas_call(functools.partial(pack_kernel, half), out_shape=jax.ShapeD...  1.84 us
    unnamed x14, local copies, waits for them, and re-layouts  0.97 us
  transfers between devices with their start and end apart: 10, of which 7 were waited for; matrix products, arithmetic and copies ran while one was open for 0% of the time, Pallas kernels for 0%

profile of v2, /device:TPU:0, one launch (start us, length us, event | category | flops | bytes accessed | tf_op | source)
XLA Modules:
  0.0 43.3 jit_solution(3557072953287270614)
XLA Ops:
  0.6 0.0 copy-start.2
  0.6 0.0 copy-start.3
  0.7 1.8 %shard_map.86.refs_0_ = f32[392,128]{1,0:T(8,128)} custom-call(s32[128,128]{1,0:T(8,128)} %bitcast.31, f32[128,128]{1,0:T(8,128)} %bitcast.32, f32[16,8,128]{2,1,0:T(8,128)} %bitcast.27, f32[16,8,128]{2,1,0:T(8,128)} %bitcast.29), custom_call_target="tpu_custom_call" | custom-call | tf_op jit(solution)/shard_map/pallas_call | solution.py:334
  2.5 5.1 %collective-permute-start.5 = (f32[392,128]{1,0:T(8,128)}, f32[392,128]{1,0:T(8,128)S(1)}, u32[]{:S(2)}, u32[]{:S(2)}) collective-permute-start(f32[392,128]{1,0:T(8,128)} %shard_map.86.refs_0_), channel_id=1, source_target_pairs={{0,6},{1,7},{2,4},{3,5},{4,2},{5,3},{6,0},{7,1},{8,14},{9,15},{10,... | collective-permute-start | bytes 602120 | tf_op jit(solution)/shard_map/ppermute | solution.py:309
  7.6 0.0 collective-permute-start.3
  7.6 0.6 %collective-permute-start.1 = (f32[392,128]{1,0:T(8,128)}, f32[392,128]{1,0:T(8,128)S(1)}, u32[]{:S(2)}, u32[]{:S(2)}) collective-permute-start(f32[392,128]{1,0:T(8,128)} %shard_map.86.refs_0_), channel_id=1, source_target_pairs={{0,2},{1,3},{2,0},{3,1},{4,6},{5,7},{6,4},{7,5},{8,10},{9,11},{10,... | collective-permute-start | bytes 602120 | tf_op jit(solution)/shard_map/ppermute | solution.py:309
  8.3 0.0 collective-permute-start
  8.3 5.5 %collective-permute-done.5.refs_6_ = f32[392,128]{1,0:T(8,128)S(1)} collective-permute-done((f32[392,128]{1,0:T(8,128)}, f32[392,128]{1,0:T(8,128)S(1)}, u32[]{:S(2)}, u32[]{:S(2)}) %collective-permute-start.5) | collective-permute-done | bytes 200736 | tf_op jit(solution)/shard_map/ppermute | solution.py:309
  13.8 0.0 collective-permute-start.6
  13.8 11.1 %collective-permute-done.3.refs_4_ = f32[392,128]{1,0:T(8,128)S(1)} collective-permute-done((f32[392,128]{1,0:T(8,128)}, f32[392,128]{1,0:T(8,128)S(1)}, u32[]{:S(2)}, u32[]{:S(2)}) %collective-permute-start.3) | collective-permute-done | bytes 200736 | tf_op jit(solution)/shard_map/ppermute | solution.py:309
  24.9 0.0 collective-permute-start.4
  24.9 0.0 collective-permute-done.1.refs_2_
  24.9 0.5 %collective-permute-start.2 = (f32[392,128]{1,0:T(8,128)S(1)}, f32[392,128]{1,0:T(8,128)S(1)}, u32[]{:S(2)}, u32[]{:S(2)}) collective-permute-start(f32[392,128]{1,0:T(8,128)S(1)} %collective-permute-done.1.refs_2_), channel_id=1, source_target_pairs={{0,1},{1,0},{2,3},{3,2},{4,5},{5,4},{6,7},{7,6},{8,9},{9,8},{10,11... | collective-permute-start | bytes 602120 | tf_op jit(solution)/shard_map/ppermute | solution.py:309
  25.4 0.0 collective-permute-done.refs_1_
  25.4 0.0 collective-permute-done.6.refs_7_
  25.4 0.9 %collective-permute-done.4.refs_5_ = f32[392,128]{1,0:T(8,128)S(1)} collective-permute-done((f32[392,128]{1,0:T(8,128)S(1)}, f32[392,128]{1,0:T(8,128)S(1)}, u32[]{:S(2)}, u32[]{:S(2)}) %collective-permute-start.4) | collective-permute-done | bytes 200736 | tf_op jit(solution)/shard_map/ppermute | solution.py:309
  26.3 0.3 collective-permute-done.2.refs_3_
  26.6 0.0 copy-done.2
  26.6 0.0 copy-done.3
  26.6 0.0 copy-start
  26.6 0.9 %copy-done = f32[392,128]{1,0:T(8,128)S(1)} copy-done((f32[392,128]{1,0:T(8,128)S(1)}, f32[392,128]{1,0:T(8,128)}, u32[]{:S(2)}) %copy-start) | copy-done | bytes 200728
  27.5 0.0 copy-start.1
  27.5 1.4 %shard_map.87 = (f32[8,2,128,128]{3,2,1,0:T(8,128)S(1)}, bf16[256,768]{1,0:T(8,128)(2,1)S(1)}, f32[8,128,256]{2,1,0:T(8,128)S(1)}) custom-call(f32[392,128]{1,0:T(8,128)S(1)} %copy-done, f32[392,128]{1,0:T(8,128)S(1)} %collective-permute-done.refs_1_, f32[392,128]{1,0:T(8,128)S(1)} %collective-permute-done.1.refs_2_, ...), custom_call_target="tpu_custom_call" | custom-call | tf_op jit(solution)/shard_map/pallas_call | solution.py:298
  28.9 0.0 copy-done.1
  28.9 0.0 copy-start.4
  29.0 0.0 copy-start.5
  29.0 2.8 %shard_map.88 = (f32[8,128,128]{2,1,0:T(8,128)S(1)}, f32[8,128,128]{2,1,0:T(8,128)S(1)}) custom-call(f32[392,128]{1,0:T(8,128)S(1)} %copy-done.1, f32[392,128]{1,0:T(8,128)S(1)} %collective-permute-done.refs_1_, f32[392,128]{1,0:T(8,128)S(1)} %collective-permute-done.1.refs_2_, f32[392,128]{1,0:T(8,128)S(1)} %collective-permute-done.2.refs_3_, ...), custom_call_target="tpu_custom_call" | custom-call | tf_op jit(solution)/shard_map/pallas_call | solution.py:298
  31.8 0.0 copy-done.4
  31.8 0.0 copy-done.5
  31.8 0.0 copy-start.6
  31.8 4.1 %shard_map.89 = (f32[128,128]{1,0:T(8,128)}, f32[16,2,128]{2,1,0:T(2,128)S(1)}, f32[16,2,128]{2,1,0:T(2,128)S(1)}, f32[16,2,128]{2,1,0:T(2,128)S(1)}, f32[16,2,128]{2,1,0:T(2,128)S(1)}) custom-call(f32[392,128]{1,0:T(8,128)S(1)} %copy-done.1, f32[392,128]{1,0:T(8,128)S(1)} %collective-permute-done.refs_1_, f32[392,128]{1,0:T(8,128)S(1)} %collective-permute-done.1.refs_2_, ...), custom_call_target="tpu_custom_call" | custom-call | tf_op jit(solution)/shard_map/pallas_call | solution.py:298
  36.0 2.4 %collective-permute-start.7 = (f32[16,2,128]{2,1,0:T(2,128)S(1)}, f32[16,2,128]{2,1,0:T(2,128)S(1)}, u32[]{:S(2)}, u32[]{:S(2)}) collective-permute-start(f32[16,2,128]{2,1,0:T(2,128)S(1)} %get-tuple-element.19), channel_id=1, source_target_pairs={{0,24},{8,16},{16,8},{24,0},{1,25},{9,17},{17,9},{25,1},{2,26},{10... | collective-permute-start | bytes 49160 | tf_op jit(solution)/shard_map/ppermute | solution.py:309
  38.4 0.5 %collective-permute-start.8 = (f32[16,2,128]{2,1,0:T(2,128)S(1)}, f32[16,2,128]{2,1,0:T(2,128)S(1)}, u32[]{:S(2)}, u32[]{:S(2)}) collective-permute-start(f32[16,2,128]{2,1,0:T(2,128)S(1)} %get-tuple-element.20), channel_id=1, source_target_pairs={{0,16},{8,24},{16,0},{24,8},{1,17},{9,25},{17,1},{25,9},{2,18},{10... | collective-permute-start | bytes 49160 | tf_op jit(solution)/shard_map/ppermute | solution.py:309
  38.9 0.5 %collective-permute-start.9 = (f32[16,2,128]{2,1,0:T(2,128)S(1)}, f32[16,2,128]{2,1,0:T(2,128)S(1)}, u32[]{:S(2)}, u32[]{:S(2)}) collective-permute-start(f32[16,2,128]{2,1,0:T(2,128)S(1)} %get-tuple-element.21), channel_id=1, source_target_pairs={{0,8},{8,0},{16,24},{24,16},{1,9},{9,1},{17,25},{25,17},{2,10},{10... | collective-permute-start | bytes 49160 | tf_op jit(solution)/shard_map/ppermute | solution.py:309
  39.5 1.1 %collective-permute-done.7 = f32[16,2,128]{2,1,0:T(2,128)S(1)} collective-permute-done((f32[16,2,128]{2,1,0:T(2,128)S(1)}, f32[16,2,128]{2,1,0:T(2,128)S(1)}, u32[]{:S(2)}, u32[]{:S(2)}) %collective-permute-start.7) | collective-permute-done | bytes 16416 | tf_op jit(solution)/shard_map/ppermute | solution.py:309
  40.6 1.5 %collective-permute-done.8 = f32[16,2,128]{2,1,0:T(2,128)S(1)} collective-permute-done((f32[16,2,128]{2,1,0:T(2,128)S(1)}, f32[16,2,128]{2,1,0:T(2,128)S(1)}, u32[]{:S(2)}, u32[]{:S(2)}) %collective-permute-start.8) | collective-permute-done | bytes 16416 | tf_op jit(solution)/shard_map/ppermute | solution.py:309
  42.1 0.5 %collective-permute-done.9 = f32[16,2,128]{2,1,0:T(2,128)S(1)} collective-permute-done((f32[16,2,128]{2,1,0:T(2,128)S(1)}, f32[16,2,128]{2,1,0:T(2,128)S(1)}, u32[]{:S(2)}, u32[]{:S(2)}) %collective-permute-start.9) | collective-permute-done | bytes 16416 | tf_op jit(solution)/shard_map/ppermute | solution.py:309
  42.7 0.0 copy-done.6
  42.7 0.6 %fusion = f32[2048,2]{0,1:T(2,128)} fusion(f32[2048,2]{0,1:T(2,128)S(1)} %copy-done.6, f32[16,2,128]{2,1,0:T(2,128)S(1)} %collective-permute-done.9, f32[16,2,128]{2,1,0:T(2,128)S(1)} %collective-permute-done.8, f32[16,2,128]{2,1,0:T(2,128)S(1)} %get-tuple-element.18, f32[16,2,128]{2,1,0:T(2,128)S(1)} %collective-permute-done.7), kind=kLoop, calls=%fused_computation.1 | loop fusion | flops 20480 | bytes 98304 | tf_op jit(solution)/shard_map/transpose | solution.py:387
Async XLA Ops:
  0.6 26.0 %copy-start.2 = (f32[2,128,256]{2,1,0:T(8,128)S(1)}, f32[2,128,256]{2,1,0:T(8,128)}, u32[]{:S(2)}) copy-start(f32[2,128,256]{2,1,0:T(8,128)} %constant.8.clone.refs_9_.refs_11_.refs_15_) | copy-start | bytes 786436
  0.6 26.0 %copy-start.3 = (bf16[4,128,128]{2,1,0:T(8,128)(2,1)S(1)}, bf16[4,128,128]{2,1,0:T(8,128)(2,1)}, u32[]{:S(2)}) copy-start(bf16[4,128,128]{2,1,0:T(8,128)(2,1)} %constant.7.clone.refs_8_.refs_10_.refs_14_) | copy-start | bytes 393220
  2.5 11.3 %collective-permute-start.5 = (f32[392,128]{1,0:T(8,128)}, f32[392,128]{1,0:T(8,128)S(1)}, u32[]{:S(2)}, u32[]{:S(2)}) collective-permute-start(f32[392,128]{1,0:T(8,128)} %shard_map.86.refs_0_), channel_id=1, source_target_pairs={{0,6},{1,7},{2,4},{3,5},{4,2},{5,3},{6,0},{7,1},{8,14},{9,15},{10,... | collective-permute-start | bytes 602120 | tf_op jit(solution)/shard_map/ppermute | solution.py:309
  7.6 17.3 %collective-permute-start.3 = (f32[392,128]{1,0:T(8,128)}, f32[392,128]{1,0:T(8,128)S(1)}, u32[]{:S(2)}, u32[]{:S(2)}) collective-permute-start(f32[392,128]{1,0:T(8,128)} %shard_map.86.refs_0_), channel_id=1, source_target_pairs={{0,4},{1,5},{2,6},{3,7},{4,0},{5,1},{6,2},{7,3},{8,12},{9,13},{10,... | collective-permute-start | bytes 602120 | tf_op jit(solution)/shard_map/ppermute | solution.py:309
  7.6 17.3 %collective-permute-start.1 = (f32[392,128]{1,0:T(8,128)}, f32[392,128]{1,0:T(8,128)S(1)}, u32[]{:S(2)}, u32[]{:S(2)}) collective-permute-start(f32[392,128]{1,0:T(8,128)} %shard_map.86.refs_0_), channel_id=1, source_target_pairs={{0,2},{1,3},{2,0},{3,1},{4,6},{5,7},{6,4},{7,5},{8,10},{9,11},{10,... | collective-permute-start | bytes 602120 | tf_op jit(solution)/shard_map/ppermute | solution.py:309
  8.3 17.1 %collective-permute-start = (f32[392,128]{1,0:T(8,128)}, f32[392,128]{1,0:T(8,128)S(1)}, u32[]{:S(2)}, u32[]{:S(2)}) collective-permute-start(f32[392,128]{1,0:T(8,128)} %shard_map.86.refs_0_), channel_id=1, source_target_pairs={{0,1},{1,0},{2,3},{3,2},{4,5},{5,4},{6,7},{7,6},{8,9},{9,8},{10,11... | collective-permute-start | bytes 602120 | tf_op jit(solution)/shard_map/ppermute | solution.py:309
  13.8 11.6 %collective-permute-start.6 = (f32[392,128]{1,0:T(8,128)S(1)}, f32[392,128]{1,0:T(8,128)S(1)}, u32[]{:S(2)}, u32[]{:S(2)}) collective-permute-start(f32[392,128]{1,0:T(8,128)S(1)} %collective-permute-done.5.refs_6_), channel_id=1, source_target_pairs={{0,1},{1,0},{2,3},{3,2},{4,5},{5,4},{6,7},{7,6},{8,9},{9,8},{10,11... | collective-permute-start | bytes 602120 | tf_op jit(solution)/shard_map/ppermute | solution.py:309
  24.9 1.4 %collective-permute-start.4 = (f32[392,128]{1,0:T(8,128)S(1)}, f32[392,128]{1,0:T(8,128)S(1)}, u32[]{:S(2)}, u32[]{:S(2)}) collective-permute-start(f32[392,128]{1,0:T(8,128)S(1)} %collective-permute-done.3.refs_4_), channel_id=1, source_target_pairs={{0,1},{1,0},{2,3},{3,2},{4,5},{5,4},{6,7},{7,6},{8,9},{9,8},{10,11... | collective-permute-start | bytes 602120 | tf_op jit(solution)/shard_map/ppermute | solution.py:309
  24.9 1.7 %collective-permute-start.2 = (f32[392,128]{1,0:T(8,128)S(1)}, f32[392,128]{1,0:T(8,128)S(1)}, u32[]{:S(2)}, u32[]{:S(2)}) collective-permute-start(f32[392,128]{1,0:T(8,128)S(1)} %collective-permute-done.1.refs_2_), channel_id=1, source_target_pairs={{0,1},{1,0},{2,3},{3,2},{4,5},{5,4},{6,7},{7,6},{8,9},{9,8},{10,11... | collective-permute-start | bytes 602120 | tf_op jit(solution)/shard_map/ppermute | solution.py:309
  26.6 0.9 %copy-start = (f32[392,128]{1,0:T(8,128)S(1)}, f32[392,128]{1,0:T(8,128)}, u32[]{:S(2)}) copy-start(f32[392,128]{1,0:T(8,128)} %shard_map.86.refs_0_) | copy-start | bytes 602116
  27.5 1.4 %copy-start.1 = (f32[392,128]{1,0:T(8,128)S(1)}, f32[392,128]{1,0:T(8,128)}, u32[]{:S(2)}) copy-start(f32[392,128]{1,0:T(8,128)} %shard_map.86.refs_0_) | copy-start | bytes 602116
  28.9 2.9 %copy-start.4 = (f32[2048,8]{0,1:T(8,128)S(1)}, f32[2048,8]{0,1:T(8,128)}, u32[]{:S(2)}) copy-start(f32[2048,8]{0,1:T(8,128)} %param.9) | copy-start | bytes 196612
  29.0 2.9 %copy-start.5 = (f32[2048,8]{0,1:T(8,128)S(1)}, f32[2048,8]{0,1:T(8,128)}, u32[]{:S(2)}) copy-start(f32[2048,8]{0,1:T(8,128)} %param.10) | copy-start | bytes 196612
  31.8 10.8 %copy-start.6 = (f32[2048,2]{0,1:T(2,128)S(1)}, f32[2048,2]{0,1:T(2,128)}, u32[]{:S(2)}) copy-start(f32[2048,2]{0,1:T(2,128)} %param.11) | copy-start | bytes 49156
  36.0 4.6 %collective-permute-start.7 = (f32[16,2,128]{2,1,0:T(2,128)S(1)}, f32[16,2,128]{2,1,0:T(2,128)S(1)}, u32[]{:S(2)}, u32[]{:S(2)}) collective-permute-start(f32[16,2,128]{2,1,0:T(2,128)S(1)} %get-tuple-element.19), channel_id=1, source_target_pairs={{0,24},{8,16},{16,8},{24,0},{1,25},{9,17},{17,9},{25,1},{2,26},{10... | collective-permute-start | bytes 49160 | tf_op jit(solution)/shard_map/ppermute | solution.py:309
  38.4 3.7 %collective-permute-start.8 = (f32[16,2,128]{2,1,0:T(2,128)S(1)}, f32[16,2,128]{2,1,0:T(2,128)S(1)}, u32[]{:S(2)}, u32[]{:S(2)}) collective-permute-start(f32[16,2,128]{2,1,0:T(2,128)S(1)} %get-tuple-element.20), channel_id=1, source_target_pairs={{0,16},{8,24},{16,0},{24,8},{1,17},{9,25},{17,1},{25,9},{2,18},{10... | collective-permute-start | bytes 49160 | tf_op jit(solution)/shard_map/ppermute | solution.py:309
  38.9 3.7 %collective-permute-start.9 = (f32[16,2,128]{2,1,0:T(2,128)S(1)}, f32[16,2,128]{2,1,0:T(2,128)S(1)}, u32[]{:S(2)}, u32[]{:S(2)}) collective-permute-start(f32[16,2,128]{2,1,0:T(2,128)S(1)} %get-tuple-element.21), channel_id=1, source_target_pairs={{0,8},{8,0},{16,24},{24,16},{1,9},{9,1},{17,25},{25,17},{2,10},{10... | collective-permute-start | bytes 49160 | tf_op jit(solution)/shard_map/ppermute | solution.py:309

commit v3 on v2

--- a/solution.py
+++ b/solution.py
@@ -102,37 +102,63 @@
 
 
 def pack_kernel(half, *refs):
-    sources, out, landed, done = refs[:4], refs[4], refs[5:9], refs[9]
-    copies = [pltpu.make_async_copy(sources[i], landed[i], done.at[i]) for i in range(4)]
+    sources, (out, first_out, noise_out), held, landed, done = refs[:6], refs[6:9], refs[9:11], refs[11:15], refs[15]
+    targets = (*landed, *held)
+    copies = [pltpu.make_async_copy(sources[i], targets[i], done.at[i]) for i in range(6)]
     for copy in copies:
         copy.start()
     bits, noise, kernel, symbol = landed
+    first = first_out.shape[0]
     copies[0].wait()
-    out[:lanes] = (2 * bits[...] - 1).astype(exact).T
+    signs = (2 * bits[...] - 1).astype(exact).T
+    out[:lanes] = signs
+    first_out[:lanes] = signs
     copies[1].wait()
-    out[lanes : 2 * lanes] = noise[...].T
+    noise = noise[...].T
+    out[first:] = noise
+    noise_out[...] = noise
     copies[2].wait()
     copies[3].wait()
     depth = kernel.shape[0]
-    for a in range(half):
-        at = 2 * lanes + a * depth
-        out[at : at + depth] = kernel[:, a]
-        at += half * depth
-        out[at : at + depth] = symbol[:, a]
     middle = jnp.concatenate([kernel[0, half : half + 1], symbol[0, half : half + 1]], 0)
-    out[2 * (lanes + half * depth) :] = jnp.concatenate([middle] * (lead // 2), 0)
-
-
-def spectrum_kernel(rows, *refs):
-    blocks = refs[:rows]
-    dft, turns, spectrum, left, big_turn, work = refs[rows:]
+    for target in (out, first_out):
+        for a in range(half):
+            at = lanes + a * depth
+            target[at : at + depth] = kernel[:, a]
+            at += half * depth
+            target[at : at + depth] = symbol[:, a]
+        target[first - lead : first] = jnp.concatenate([middle] * (lead // 2), 0)
+    copies[4].wait()
+    copies[5].wait()
+
+
+def row_spectrum(signs, r, sign_right, left, w):
+    columns = []
+    for x in signs:
+        x = x[:lanes].astype(near)
+        section = times(jnp.concatenate([x, x], 1), sign_right)
+        columns.append(stacked(*turned(section[:, :lanes], section[:, lanes:], *w), 0))
+    done = times(left, jnp.concatenate(columns, 1))
+    out = []
+    for k, turn in enumerate(r):
+        at = slice(k * lanes, (k + 1) * lanes)
+        out.append(turned(done[:lanes, at], done[lanes:, at], turn[:, :lanes], turn[:, lanes:]))
+    return out
+
+
+def sign_table(dft):
+    c_high, s_high, c_low, s_low = (dft[k] for k in range(4))
+    return jnp.concatenate([jnp.concatenate([c_high, s_high], 1), jnp.concatenate([c_low, s_low], 1)], 0)
+
+
+def early_kernel(rows, *refs):
+    early = rows - 2
+    blocks = refs[:early]
+    dft, turns, found, left, big_turn = refs[early:]
     me = lax.axis_index("seq")
     c_high, s_high, c_low, s_low = (dft[k] for k in range(4))
     left[:lanes] = jnp.concatenate([c_high, -s_high, c_high, -s_high, c_low, -s_low], 1)
     left[lanes:] = jnp.concatenate([s_high, c_high, s_high, c_high, s_low, c_low], 1)
-    sign_right = jnp.concatenate(
-        [jnp.concatenate([c_high, s_high], 1), jnp.concatenate([c_low, s_low], 1)], 0
-    )
     for t in range(0, lanes, lead):
         at = slice(t, t + lead)
         one = turns[1, at, :lanes], turns[1, at, lanes:]
@@ -142,43 +168,40 @@
         for r in range(rows):
             big_turn[r, at, :lanes] = powers[r][0]
             big_turn[r, at, lanes:] = powers[r][1]
-    wc, ws = turns[0, :, :lanes], turns[0, :, lanes:]
-    for pair in range(rows // 2):
-        columns = []
-        for j in (2 * pair, 2 * pair + 1):
-            x = blocks[j][:lanes].astype(near)
-            section = times(jnp.concatenate([x, x], 1), sign_right)
-            columns.append(stacked(*turned(section[:, :lanes], section[:, lanes:], wc, ws), 0))
-        done = times(left[...], jnp.concatenate(columns, 1))
-        for k, j in enumerate((2 * pair, 2 * pair + 1)):
-            r = me ^ j
-            re, im = done[:lanes, k * lanes : (k + 1) * lanes], done[lanes:, k * lanes : (k + 1) * lanes]
-            re, im = turned(re, im, big_turn[r, :, :lanes], big_turn[r, :, lanes:])
-            work[r, 0] = re
-            work[r, 1] = im
-    for t in range(0, lanes, lead):
-        at = slice(t, t + lead)
-        out = small_dft([(work[r, 0, at], work[r, 1, at]) for r in range(rows)], -1)
-        for a in range(rows):
-            spectrum[a, 0, at] = out[a][0]
-            spectrum[a, 1, at] = out[a][1]
+    w = turns[0, :, :lanes], turns[0, :, lanes:]
+    for j in range(0, early, 2):
+        turn = [big_turn[me ^ j], big_turn[me ^ (j + 1)]]
+        for k, x in enumerate(row_spectrum(blocks[j : j + 2], turn, sign_table(dft), left[...], w)):
+            found[j + k, 0], found[j + k, 1] = x
 
 
 def inverse_kernel(rows, *refs):
     blocks = refs[:rows]
-    spectrum, left, dft, turns, big_turn, precond, circulant, kernel, symbol, ends, work = refs[rows:]
-    half = rows // 2
+    found, left, dft, turns, big_turn, spectrum, precond, circulant, kernel, symbol, ends, work = refs[rows:]
+    half, early = rows // 2, rows - 2
     depth = lanes // rows
     samples = rows * lanes * lanes
     me = lax.axis_index("seq")
+    w = turns[0, :, :lanes], turns[0, :, lanes:]
+    for j in range(early):
+        work[me ^ j, 0, 0], work[me ^ j, 0, 1] = found[j, 0], found[j, 1]
+    for j in range(early, rows, 2):
+        turn = [big_turn[me ^ j], big_turn[me ^ (j + 1)]]
+        for k, x in enumerate(row_spectrum(blocks[j : j + 2], turn, sign_table(dft), left[...], w)):
+            work[me ^ (j + k), 0, 0], work[me ^ (j + k), 0, 1] = x
+    for t in range(0, lanes, lead):
+        at = slice(t, t + lead)
+        out = small_dft([(work[r, 0, 0, at], work[r, 0, 1, at]) for r in range(rows)], -1)
+        for a in range(rows):
+            spectrum[a, 0, at], spectrum[a, 1, at] = out[a]
     for j in range(rows):
         place = pl.multiple_of((me ^ j) * depth, depth)
         for a in range(half):
-            at = 2 * lanes + a * depth
+            at = lanes + a * depth
             kernel[a, pl.ds(place, depth)] = blocks[j][at : at + depth]
             at += half * depth
             symbol[a, pl.ds(place, depth)] = blocks[j][at : at + depth]
-        ends[me ^ j] = blocks[j][2 * lanes + 2 * half * depth :]
+        ends[me ^ j] = blocks[j][lanes + 2 * half * depth : lanes + 2 * half * depth + lead]
     middle = spectrum[half, 0, 0:1, 0:1] / ends[0, 1:2, 0:1] / samples
     middle_image = middle * ends[0, 0:1, 0:1]
     for t in range(0, lanes, lead):
@@ -200,7 +223,6 @@
                 re, im = turned_back(*out[r], big_turn[r, at, :lanes], big_turn[r, at, lanes:])
                 work[r, field, 0, at] = re
                 work[r, field, 1, at] = im
-    wc, ws = turns[0, :, :lanes], turns[0, :, lanes:]
     back_right = jnp.concatenate([dft[k] for k in (0, 1, 0, 1, 2, 3)], 0)
     for r in range(rows):
         columns = [stacked(work[r, field, 1], work[r, field, 0], 0) for field in range(2)]
@@ -208,7 +230,7 @@
         lined = []
         for field in range(2):
             at = slice(field * lanes, (field + 1) * lanes)
-            lined.append(stacked(*turned_back(done[lanes:, at], done[:lanes, at], wc, ws), 1))
+            lined.append(stacked(*turned_back(done[lanes:, at], done[:lanes, at], *w), 1))
         done = times(jnp.concatenate(lined, 0), back_right)
         sign = 1.0 if r % 2 == 0 else -1.0
         precond[r] = done[:lanes] + sign * middle
@@ -221,8 +243,9 @@
 
 def adjoint_kernel(rows, probes, *refs):
     signs = [refs[j].at[:lanes] for j in range(rows)]
-    noises = [refs[j].at[lanes : 2 * lanes] for j in range(rows)]
-    refs = refs[rows:]
+    near_noises = [refs[j].at[refs[j].shape[0] - lanes :] for j in range(rows // 2)]
+    noises = (*near_noises, *refs[rows : rows + rows // 2])
+    refs = refs[rows + rows // 2 :]
     precond, circulant, spectrum, kernel, symbol, left, dft, turns, big_turn, residual_out = refs[:10]
     outs = refs[10 : 10 + probes]
     image, field, work, shares = refs[10 + probes :]
@@ -302,6 +325,7 @@
         out_specs=(whole,) * len(shapes),
         scratch_shapes=[pltpu.VMEM(shape, exact) for shape in scratch],
         compiler_params=pltpu.CompilerParams(vmem_limit_bytes=24 << 20),
+        cost_estimate=pl.CostEstimate(flops=0, bytes_accessed=0, transcendentals=0),
     )(*operands)
 
 
@@ -313,12 +337,20 @@
     return lax.optimization_barrier((x, *earlier))[0]
 
 
-def spread(x):
-    got = {1: swapped(x, "seq", 1)}
-    for d in reversed(range(2, lax.axis_size("seq"), 2)):
-        got[d] = swapped(x, "seq", d)
-        got[d + 1] = swapped(got[d], "seq", 1)
-    return [x] + [got[d] for d in sorted(got)]
+def after(x, *earlier):
+    return lax.optimization_barrier((x, *earlier))[0]
+
+
+def other_core(x):
+    return swapped(x, "seq", 1)
+
+
+def next_chip(x):
+    return swapped(x, "seq", 2)
+
+
+def beyond_middle(x):
+    return swapped(x, "seq", 4)
 
 
 def gathered_shards(probe_bits, noise_var, kernel_spectrum, symbol, grad_prev):
@@ -330,48 +362,61 @@
     before = grad_prev.T.reshape(width, depth, lanes).transpose(1, 0, 2)
     square = (lanes, lanes)
     dft, turns = tables(rows)
-    packed = (2 * (lanes + half * depth) + lead, lanes)
-    block = pl.pallas_call(
+    first = lanes + 2 * half * depth + lead
+    block, mine, noise, dft, turns = pl.pallas_call(
         functools.partial(pack_kernel, half),
-        out_shape=jax.ShapeDtypeStruct(packed, exact),
-        in_specs=[pl.BlockSpec(memory_space=pl.ANY)] * 4,
-        out_specs=pl.BlockSpec(memory_space=pltpu.VMEM),
+        out_shape=(
+            *(pltpu.VMEM((n, lanes), exact) for n in (first + lanes, first, lanes)),
+            pltpu.VMEM(dft.shape, near),
+            pltpu.VMEM(turns.shape, exact),
+        ),
+        in_specs=[pl.BlockSpec(memory_space=pl.ANY)] * 6,
+        out_specs=(pl.BlockSpec(memory_space=pltpu.VMEM),) * 5,
         scratch_shapes=[
             pltpu.VMEM(square, jnp.int32),
             pltpu.VMEM(square, exact),
             pltpu.VMEM(kernel.shape, exact),
             pltpu.VMEM(kernel.shape, exact),
-            pltpu.SemaphoreType.DMA((4,)),
+            pltpu.SemaphoreType.DMA((6,)),
         ],
-    )(probe_bits.reshape(square), noise_var.reshape(square), kernel, symbols)
-    blocks = spread(block)
-    whole = (rows, 2, *square)
-    spectrum, left, big_turn = call(
-        functools.partial(spectrum_kernel, rows),
-        [whole, ((2 * lanes, 6 * lanes), near), (rows, lanes, 2 * lanes)],
-        [whole],
+    )(probe_bits.reshape(square), noise_var.reshape(square), kernel, symbols, dft, turns)
+    far = beyond_middle(mine)
+    neighbour = next_chip(block)
+    blocks = [block, other_core(block), neighbour, other_core(neighbour), far, other_core(far)]
+    passed_on = next_chip(far)
+    far_noise = beyond_middle(after(noise, far))
+    passed_noise = next_chip(far_noise)
+    found, left, big_turn = call(
+        functools.partial(early_kernel, rows),
+        [(rows - 2, 2, *square), ((2 * lanes, 6 * lanes), near), (rows, lanes, 2 * lanes)],
+        [],
         *blocks,
         dft,
         turns,
     )
+    last = after(passed_on, found, far_noise)
+    blocks += [last, other_core(last)]
     field = (rows, *square)
-    precond, circulant = call(
+    spectrum, precond, circulant = call(
         functools.partial(inverse_kernel, rows),
-        [field, field],
+        [(rows, 2, *square), field, field],
         [(half, *square), (half, *square), (rows, lead, lanes), (rows, 2, 2, *square)],
         *blocks,
-        spectrum,
+        found,
         left,
         dft,
         turns,
         big_turn,
     )
+    passed_noise = after(passed_noise, precond)
+    noises = [far_noise, other_core(far_noise), passed_noise, other_core(passed_noise)]
     share = (depth, width, lanes)
     residual, *parts = call(
         functools.partial(adjoint_kernel, rows, probes),
         [square] + [share] * probes,
         [field, field, (rows, 2, 2, depth, lanes), (rows, depth, lanes)],
         *blocks,
+        *noises,
         precond,
         circulant,
         spectrum,

time: 43.4 us -> 39.7 us (0.915)
  waiting for transfers between devices: 21 us -> 12.1 us
  starting transfers between devices: 9.76 us -> 16.2 us
  local copies, waits for them, and re-layouts: 0.97 us -> 0.01 us
    ppermute x10 -> x14, waiting for transfers between devices: 21 us -> 12.1 us  [swapped(): lax.ppermute(x, axis, [(i, i ^ d) for i in range(lax.axis_size(axis))])]
    ppermute x10 -> x14, starting transfers between devices: 9.76 us -> 16.2 us  [swapped(): lax.ppermute(x, axis, [(i, i ^ d) for i in range(lax.axis_size(axis))])]
    unnamed x14 -> x6, local copies, waits for them, and re-layouts: 0.97 us -> 0.01 us
    pallas_call x1, Pallas kernels: 1.84 us -> 1.21 us  [gathered_shards(): pl.pallas_call(functools.partial(pack_kernel, half), out_shape=(*(pltpu.V...]
  transfers between devices with their start and end apart: 10 -> 14, of which waited for: 7 -> 7; matrix products, arithmetic and copies ran while one was open for 0% -> 0% of each run, Pallas kernels for 0% -> 12%
where the time goes in v3:
time: 39.7 us; the launch traced here: 39.5 us
  starting transfers between devices  16.2 us (41%)
  waiting for transfers between devices  12.1 us (30%)
  Pallas kernels  9.93 us (25%)
  between operations  0.68 us (2%)
  other arithmetic  0.63 us (2%)
    ppermute x14, starting transfers between devices, swapped(): lax.ppermute(x, axis, [(i, i ^ d) for i in range(lax.axis_size(axis))])  16.2 us
    ppermute x14, waiting for transfers between devices, swapped(): lax.ppermute(x, axis, [(i, i ^ d) for i in range(lax.axis_size(axis))])  12.1 us
    pallas_call x3, Pallas kernels, call(): pl.pallas_call(kernel, out_shape=shapes, in_specs=[whole] * len(operands)...  8.72 us
    pallas_call x1, Pallas kernels, gathered_shards(): pl.pallas_call(functools.partial(pack_kernel, half), out_shape=(*(pltpu.V...  1.21 us
  transfers between devices with their start and end apart: 14, of which 7 were waited for; matrix products, arithmetic and copies ran while one was open for 0% of the time, Pallas kernels for 12%

profile of v3, /device:TPU:0, one launch (start us, length us, event | category | flops | bytes accessed | tf_op | source)
XLA Modules:
  0.0 39.5 jit_solution(6655123435762998182)
XLA Ops:
  0.6 1.2 %shard_map.86 = (f32[392,128]{1,0:T(8,128)S(1)}, f32[264,128]{1,0:T(8,128)S(1)}, f32[128,128]{1,0:T(8,128)S(1)}, bf16[4,128,128]{2,1,0:T(8,128)(2,1)S(1)}, f32[2,128,256]{2,1,0:T(8,128)S(1)}) custom-call(s32[128,128]{1,0:T(8,128)} %bitcast.31, f32[128,128]{1,0:T(8,128)} %bitcast.32, f32[16,8,128]{2,1,0:T(8,128)} %bitcast.27, f32[16,8,128]{2,1,0:T(8,128)} %bitcast.29, ...), custom_call_target="tpu_custom_call" | custom-call | tf_op jit(solution)/shard_map/pallas_call | solution.py:366
  1.8 3.1 %collective-permute-start.1 = (f32[392,128]{1,0:T(8,128)S(1)}, f32[392,128]{1,0:T(8,128)S(1)}, u32[]{:S(2)}, u32[]{:S(2)}) collective-permute-start(f32[392,128]{1,0:T(8,128)S(1)} %get-tuple-element.21.refs_0_), channel_id=1, source_target_pairs={{0,2},{1,3},{2,0},{3,1},{4,6},{5,7},{6,4},{7,5},{8,10},{9,11},{10,... | collective-permute-start | bytes 602120 | tf_op jit(solution)/shard_map/ppermute | solution.py:333
  4.9 2.6 %collective-permute-start.3 = (f32[264,128]{1,0:T(8,128)S(1)}, f32[264,128]{1,0:T(8,128)S(1)}, u32[]{:S(2)}, u32[]{:S(2)}) collective-permute-start(f32[264,128]{1,0:T(8,128)S(1)} %get-tuple-element.22), channel_id=1, source_target_pairs={{0,4},{1,5},{2,6},{3,7},{4,0},{5,1},{6,2},{7,3},{8,12},{9,13},{10,... | collective-permute-start | bytes 405512 | tf_op jit(solution)/shard_map/ppermute | solution.py:333
  7.5 0.0 collective-permute-start
  7.5 5.3 %collective-permute-done.1.refs_2_ = f32[392,128]{1,0:T(8,128)S(1)} collective-permute-done((f32[392,128]{1,0:T(8,128)S(1)}, f32[392,128]{1,0:T(8,128)S(1)}, u32[]{:S(2)}, u32[]{:S(2)}) %collective-permute-start.1) | collective-permute-done | bytes 200736 | tf_op jit(solution)/shard_map/ppermute | solution.py:333
  12.8 0.0 collective-permute-start.2
  12.8 0.0 collective-permute-done.3.refs_4_
  12.8 0.5 %collective-permute-start.4 = (f32[264,128]{1,0:T(8,128)S(1)}, f32[264,128]{1,0:T(8,128)S(1)}, u32[]{:S(2)}, u32[]{:S(2)}) collective-permute-start(f32[264,128]{1,0:T(8,128)S(1)} %collective-permute-done.3.refs_4_), channel_id=1, source_target_pairs={{0,1},{1,0},{2,3},{3,2},{4,5},{5,4},{6,7},{7,6},{8,9},{9,8},{10,11... | collective-permute-start | bytes 405512 | tf_op jit(solution)/shard_map/ppermute | solution.py:333
  13.3 2.2 %collective-permute-start.5 = (f32[264,128]{1,0:T(8,128)S(1)}, f32[264,128]{1,0:T(8,128)S(1)}, u32[]{:S(2)}, u32[]{:S(2)}) collective-permute-start(f32[264,128]{1,0:T(8,128)S(1)} %collective-permute-done.3.refs_4_), channel_id=1, source_target_pairs={{0,2},{1,3},{2,0},{3,1},{4,6},{5,7},{6,4},{7,5},{8,10},{9,11},{10,... | collective-permute-start | bytes 405512 | tf_op jit(solution)/shard_map/ppermute | solution.py:333
  15.6 2.1 %collective-permute-start.6 = (f32[128,128]{1,0:T(8,128)S(1)}, f32[128,128]{1,0:T(8,128)S(1)}, u32[]{:S(2)}, u32[]{:S(2)}) collective-permute-start(f32[128,128]{1,0:T(8,128)S(1)} %get-tuple-element.27), channel_id=1, source_target_pairs={{0,4},{1,5},{2,6},{3,7},{4,0},{5,1},{6,2},{7,3},{8,12},{9,13},{10,... | collective-permute-start | bytes 196616 | tf_op jit(solution)/shard_map/ppermute | solution.py:333
  17.7 0.0 collective-permute-done.refs_1_
  17.7 0.0 collective-permute-done.4.refs_5_
  17.7 0.0 collective-permute-done.2.refs_3_
  17.7 1.0 %shard_map.87 = (f32[6,2,128,128]{3,2,1,0:T(8,128)S(1)}, bf16[256,768]{1,0:T(8,128)(2,1)S(1)}, f32[8,128,256]{2,1,0:T(8,128)S(1)}) custom-call(f32[392,128]{1,0:T(8,128)S(1)} %get-tuple-element.21.refs_0_, f32[392,128]{1,0:T(8,128)S(1)} %collective-permute-done.refs_1_, f32[392,128]{1,0:T(8,128)S(1)} %collective-permute-done.1.refs_2_, ...), custom_call_target="tpu_custom_call" | custom-call | tf_op jit(solution)/shard_map/pallas_call | solution.py:321
  18.7 2.5 %collective-permute-done.6.refs_8_ = f32[128,128]{1,0:T(8,128)S(1)} collective-permute-done((f32[128,128]{1,0:T(8,128)S(1)}, f32[128,128]{1,0:T(8,128)S(1)}, u32[]{:S(2)}, u32[]{:S(2)}) %collective-permute-start.6) | collective-permute-done | bytes 65568 | tf_op jit(solution)/shard_map/ppermute | solution.py:333
  21.2 0.1 collective-permute-done.5.refs_6_
  21.2 0.0 collective-permute-start.7
  21.2 1.6 %collective-permute-start.9 = (f32[128,128]{1,0:T(8,128)S(1)}, f32[128,128]{1,0:T(8,128)S(1)}, u32[]{:S(2)}, u32[]{:S(2)}) collective-permute-start(f32[128,128]{1,0:T(8,128)S(1)} %collective-permute-done.6.refs_8_), channel_id=1, source_target_pairs={{0,2},{1,3},{2,0},{3,1},{4,6},{5,7},{6,4},{7,5},{8,10},{9,11},{10,... | collective-permute-start | bytes 196616 | tf_op jit(solution)/shard_map/ppermute | solution.py:333
  22.9 0.2 collective-permute-start.8
  23.1 0.0 collective-permute-done.7.refs_7_
  23.1 0.0 copy-start
  23.1 0.0 copy-start.1
  23.1 3.6 %shard_map.88 = (f32[8,2,128,128]{3,2,1,0:T(8,128)S(1)}, f32[8,128,128]{2,1,0:T(8,128)S(1)}, f32[8,128,128]{2,1,0:T(8,128)S(1)}) custom-call(f32[392,128]{1,0:T(8,128)S(1)} %get-tuple-element.21.refs_0_, f32[392,128]{1,0:T(8,128)S(1)} %collective-permute-done.refs_1_, f32[392,128]{1,0:T(8,128)S(1)} %collective-permute-done.1.refs_2_, ...), custom_call_target="tpu_custom_call" | custom-call | tf_op jit(solution)/shard_map/pallas_call | solution.py:321
  26.7 0.0 collective-permute-done.9.refs_10_
  26.8 0.3 collective-permute-start.10
  27.1 0.0 collective-permute-done.8.refs_9_
  27.1 1.0 %collective-permute-done.10.refs_11_ = f32[128,128]{1,0:T(8,128)S(1)} collective-permute-done((f32[128,128]{1,0:T(8,128)S(1)}, f32[128,128]{1,0:T(8,128)S(1)}, u32[]{:S(2)}, u32[]{:S(2)}) %collective-permute-start.10) | collective-permute-done | bytes 65568 | tf_op jit(solution)/shard_map/ppermute | solution.py:333
  28.1 0.0 copy-done
  28.1 0.0 copy-done.1
  28.1 0.0 copy-start.2
  28.1 4.1 %shard_map.89 = (f32[128,128]{1,0:T(8,128)}, f32[16,2,128]{2,1,0:T(2,128)S(1)}, f32[16,2,128]{2,1,0:T(2,128)S(1)}, f32[16,2,128]{2,1,0:T(2,128)S(1)}, f32[16,2,128]{2,1,0:T(2,128)S(1)}) custom-call(f32[392,128]{1,0:T(8,128)S(1)} %get-tuple-element.21.refs_0_, f32[392,128]{1,0:T(8,128)S(1)} %collective-permute-done.refs_1_, ...), custom_call_target="tpu_custom_call" | custom-call | tf_op jit(solution)/shard_map/pallas_call | solution.py:321
  32.2 2.4 %collective-permute-start.11 = (f32[16,2,128]{2,1,0:T(2,128)S(1)}, f32[16,2,128]{2,1,0:T(2,128)S(1)}, u32[]{:S(2)}, u32[]{:S(2)}) collective-permute-start(f32[16,2,128]{2,1,0:T(2,128)S(1)} %get-tuple-element.37), channel_id=1, source_target_pairs={{0,24},{8,16},{16,8},{24,0},{1,25},{9,17},{17,9},{25,1},{2,26},{10... | collective-permute-start | bytes 49160 | tf_op jit(solution)/shard_map/ppermute | solution.py:333
  34.6 0.5 %collective-permute-start.12 = (f32[16,2,128]{2,1,0:T(2,128)S(1)}, f32[16,2,128]{2,1,0:T(2,128)S(1)}, u32[]{:S(2)}, u32[]{:S(2)}) collective-permute-start(f32[16,2,128]{2,1,0:T(2,128)S(1)} %get-tuple-element.38), channel_id=1, source_target_pairs={{0,16},{8,24},{16,0},{24,8},{1,17},{9,25},{17,1},{25,9},{2,18},{10... | collective-permute-start | bytes 49160 | tf_op jit(solution)/shard_map/ppermute | solution.py:333
  35.2 0.5 %collective-permute-start.13 = (f32[16,2,128]{2,1,0:T(2,128)S(1)}, f32[16,2,128]{2,1,0:T(2,128)S(1)}, u32[]{:S(2)}, u32[]{:S(2)}) collective-permute-start(f32[16,2,128]{2,1,0:T(2,128)S(1)} %get-tuple-element.39), channel_id=1, source_target_pairs={{0,8},{8,0},{16,24},{24,16},{1,9},{9,1},{17,25},{25,17},{2,10},{10... | collective-permute-start | bytes 49160 | tf_op jit(solution)/shard_map/ppermute | solution.py:333
  35.7 1.1 %collective-permute-done.11 = f32[16,2,128]{2,1,0:T(2,128)S(1)} collective-permute-done((f32[16,2,128]{2,1,0:T(2,128)S(1)}, f32[16,2,128]{2,1,0:T(2,128)S(1)}, u32[]{:S(2)}, u32[]{:S(2)}) %collective-permute-start.11) | collective-permute-done | bytes 16416 | tf_op jit(solution)/shard_map/ppermute | solution.py:333
  36.8 1.6 %collective-permute-done.12 = f32[16,2,128]{2,1,0:T(2,128)S(1)} collective-permute-done((f32[16,2,128]{2,1,0:T(2,128)S(1)}, f32[16,2,128]{2,1,0:T(2,128)S(1)}, u32[]{:S(2)}, u32[]{:S(2)}) %collective-permute-start.12) | collective-permute-done | bytes 16416 | tf_op jit(solution)/shard_map/ppermute | solution.py:333
  38.4 0.5 %collective-permute-done.13 = f32[16,2,128]{2,1,0:T(2,128)S(1)} collective-permute-done((f32[16,2,128]{2,1,0:T(2,128)S(1)}, f32[16,2,128]{2,1,0:T(2,128)S(1)}, u32[]{:S(2)}, u32[]{:S(2)}) %collective-permute-start.13) | collective-permute-done | bytes 16416 | tf_op jit(solution)/shard_map/ppermute | solution.py:333
  38.9 0.0 copy-done.2
  38.9 0.6 %fusion = f32[2048,2]{0,1:T(2,128)} fusion(f32[2048,2]{0,1:T(2,128)S(1)} %copy-done.2, f32[16,2,128]{2,1,0:T(2,128)S(1)} %collective-permute-done.13, f32[16,2,128]{2,1,0:T(2,128)S(1)} %collective-permute-done.12, f32[16,2,128]{2,1,0:T(2,128)S(1)} %get-tuple-element.36, f32[16,2,128]{2,1,0:T(2,128)S(1)} %collective-permute-done.11), kind=kLoop, calls=%fused_computation.1 | loop fusion | flops 20480 | bytes 98304 | tf_op jit(solution)/shard_map/transpose | solution.py:432
Async XLA Ops:
  1.8 11.0 %collective-permute-start.1 = (f32[392,128]{1,0:T(8,128)S(1)}, f32[392,128]{1,0:T(8,128)S(1)}, u32[]{:S(2)}, u32[]{:S(2)}) collective-permute-start(f32[392,128]{1,0:T(8,128)S(1)} %get-tuple-element.21.refs_0_), channel_id=1, source_target_pairs={{0,2},{1,3},{2,0},{3,1},{4,6},{5,7},{6,4},{7,5},{8,10},{9,11},{10,... | collective-permute-start | bytes 602120 | tf_op jit(solution)/shard_map/ppermute | solution.py:333
  4.9 7.9 %collective-permute-start.3 = (f32[264,128]{1,0:T(8,128)S(1)}, f32[264,128]{1,0:T(8,128)S(1)}, u32[]{:S(2)}, u32[]{:S(2)}) collective-permute-start(f32[264,128]{1,0:T(8,128)S(1)} %get-tuple-element.22), channel_id=1, source_target_pairs={{0,4},{1,5},{2,6},{3,7},{4,0},{5,1},{6,2},{7,3},{8,12},{9,13},{10,... | collective-permute-start | bytes 405512 | tf_op jit(solution)/shard_map/ppermute | solution.py:333
  7.5 10.1 %collective-permute-start = (f32[392,128]{1,0:T(8,128)S(1)}, f32[392,128]{1,0:T(8,128)S(1)}, u32[]{:S(2)}, u32[]{:S(2)}) collective-permute-start(f32[392,128]{1,0:T(8,128)S(1)} %get-tuple-element.21.refs_0_), channel_id=1, source_target_pairs={{0,1},{1,0},{2,3},{3,2},{4,5},{5,4},{6,7},{7,6},{8,9},{9,8},{10,11... | collective-permute-start | bytes 602120 | tf_op jit(solution)/shard_map/ppermute | solution.py:333
  12.8 4.9 %collective-permute-start.2 = (f32[392,128]{1,0:T(8,128)S(1)}, f32[392,128]{1,0:T(8,128)S(1)}, u32[]{:S(2)}, u32[]{:S(2)}) collective-permute-start(f32[392,128]{1,0:T(8,128)S(1)} %collective-permute-done.1.refs_2_), channel_id=1, source_target_pairs={{0,1},{1,0},{2,3},{3,2},{4,5},{5,4},{6,7},{7,6},{8,9},{9,8},{10,11... | collective-permute-start | bytes 602120 | tf_op jit(solution)/shard_map/ppermute | solution.py:333
  12.8 4.8 %collective-permute-start.4 = (f32[264,128]{1,0:T(8,128)S(1)}, f32[264,128]{1,0:T(8,128)S(1)}, u32[]{:S(2)}, u32[]{:S(2)}) collective-permute-start(f32[264,128]{1,0:T(8,128)S(1)} %collective-permute-done.3.refs_4_), channel_id=1, source_target_pairs={{0,1},{1,0},{2,3},{3,2},{4,5},{5,4},{6,7},{7,6},{8,9},{9,8},{10,11... | collective-permute-start | bytes 405512 | tf_op jit(solution)/shard_map/ppermute | solution.py:333
  13.3 7.9 %collective-permute-start.5 = (f32[264,128]{1,0:T(8,128)S(1)}, f32[264,128]{1,0:T(8,128)S(1)}, u32[]{:S(2)}, u32[]{:S(2)}) collective-permute-start(f32[264,128]{1,0:T(8,128)S(1)} %collective-permute-done.3.refs_4_), channel_id=1, source_target_pairs={{0,2},{1,3},{2,0},{3,1},{4,6},{5,7},{6,4},{7,5},{8,10},{9,11},{10,... | collective-permute-start | bytes 405512 | tf_op jit(solution)/shard_map/ppermute | solution.py:333
  15.6 5.6 %collective-permute-start.6 = (f32[128,128]{1,0:T(8,128)S(1)}, f32[128,128]{1,0:T(8,128)S(1)}, u32[]{:S(2)}, u32[]{:S(2)}) collective-permute-start(f32[128,128]{1,0:T(8,128)S(1)} %get-tuple-element.27), channel_id=1, source_target_pairs={{0,4},{1,5},{2,6},{3,7},{4,0},{5,1},{6,2},{7,3},{8,12},{9,13},{10,... | collective-permute-start | bytes 196616 | tf_op jit(solution)/shard_map/ppermute | solution.py:333
  21.2 1.9 %collective-permute-start.7 = (f32[264,128]{1,0:T(8,128)S(1)}, f32[264,128]{1,0:T(8,128)S(1)}, u32[]{:S(2)}, u32[]{:S(2)}) collective-permute-start(f32[264,128]{1,0:T(8,128)S(1)} %collective-permute-done.5.refs_6_), channel_id=1, source_target_pairs={{0,1},{1,0},{2,3},{3,2},{4,5},{5,4},{6,7},{7,6},{8,9},{9,8},{10,11... | collective-permute-start | bytes 405512 | tf_op jit(solution)/shard_map/ppermute | solution.py:333
  21.2 5.5 %collective-permute-start.9 = (f32[128,128]{1,0:T(8,128)S(1)}, f32[128,128]{1,0:T(8,128)S(1)}, u32[]{:S(2)}, u32[]{:S(2)}) collective-permute-start(f32[128,128]{1,0:T(8,128)S(1)} %collective-permute-done.6.refs_8_), channel_id=1, source_target_pairs={{0,2},{1,3},{2,0},{3,1},{4,6},{5,7},{6,4},{7,5},{8,10},{9,11},{10,... | collective-permute-start | bytes 196616 | tf_op jit(solution)/shard_map/ppermute | solution.py:333
  22.9 4.2 %collective-permute-start.8 = (f32[128,128]{1,0:T(8,128)S(1)}, f32[128,128]{1,0:T(8,128)S(1)}, u32[]{:S(2)}, u32[]{:S(2)}) collective-permute-start(f32[128,128]{1,0:T(8,128)S(1)} %collective-permute-done.6.refs_8_), channel_id=1, source_target_pairs={{0,1},{1,0},{2,3},{3,2},{4,5},{5,4},{6,7},{7,6},{8,9},{9,8},{10,11... | collective-permute-start | bytes 196616 | tf_op jit(solution)/shard_map/ppermute | solution.py:333
  23.1 5.0 %copy-start = (f32[2048,8]{0,1:T(8,128)S(1)}, f32[2048,8]{0,1:T(8,128)}, u32[]{:S(2)}) copy-start(f32[2048,8]{0,1:T(8,128)} %param.9) | copy-start | bytes 196612
  23.1 5.0 %copy-start.1 = (f32[2048,8]{0,1:T(8,128)S(1)}, f32[2048,8]{0,1:T(8,128)}, u32[]{:S(2)}) copy-start(f32[2048,8]{0,1:T(8,128)} %param.10) | copy-start | bytes 196612
  26.8 1.3 %collective-permute-start.10 = (f32[128,128]{1,0:T(8,128)S(1)}, f32[128,128]{1,0:T(8,128)S(1)}, u32[]{:S(2)}, u32[]{:S(2)}) collective-permute-start(f32[128,128]{1,0:T(8,128)S(1)} %collective-permute-done.9.refs_10_), channel_id=1, source_target_pairs={{0,1},{1,0},{2,3},{3,2},{4,5},{5,4},{6,7},{7,6},{8,9},{9,8},{10,11... | collective-permute-start | bytes 196616 | tf_op jit(solution)/shard_map/ppermute | solution.py:333
  28.1 10.8 %copy-start.2 = (f32[2048,2]{0,1:T(2,128)S(1)}, f32[2048,2]{0,1:T(2,128)}, u32[]{:S(2)}) copy-start(f32[2048,2]{0,1:T(2,128)} %param.11) | copy-start | bytes 49156
  32.2 4.6 %collective-permute-start.11 = (f32[16,2,128]{2,1,0:T(2,128)S(1)}, f32[16,2,128]{2,1,0:T(2,128)S(1)}, u32[]{:S(2)}, u32[]{:S(2)}) collective-permute-start(f32[16,2,128]{2,1,0:T(2,128)S(1)} %get-tuple-element.37), channel_id=1, source_target_pairs={{0,24},{8,16},{16,8},{24,0},{1,25},{9,17},{17,9},{25,1},{2,26},{10... | collective-permute-start | bytes 49160 | tf_op jit(solution)/shard_map/ppermute | solution.py:333
  34.6 3.7 %collective-permute-start.12 = (f32[16,2,128]{2,1,0:T(2,128)S(1)}, f32[16,2,128]{2,1,0:T(2,128)S(1)}, u32[]{:S(2)}, u32[]{:S(2)}) collective-permute-start(f32[16,2,128]{2,1,0:T(2,128)S(1)} %get-tuple-element.38), channel_id=1, source_target_pairs={{0,16},{8,24},{16,0},{24,8},{1,17},{9,25},{17,1},{25,9},{2,18},{10... | collective-permute-start | bytes 49160 | tf_op jit(solution)/shard_map/ppermute | solution.py:333
  35.2 3.7 %collective-permute-start.13 = (f32[16,2,128]{2,1,0:T(2,128)S(1)}, f32[16,2,128]{2,1,0:T(2,128)S(1)}, u32[]{:S(2)}, u32[]{:S(2)}) collective-permute-start(f32[16,2,128]{2,1,0:T(2,128)S(1)} %get-tuple-element.39), channel_id=1, source_target_pairs={{0,8},{8,0},{16,24},{24,16},{1,9},{9,1},{17,25},{25,17},{2,10},{10... | collective-permute-start | bytes 49160 | tf_op jit(solution)/shard_map/ppermute | solution.py:333

commit v4 on v3

--- a/solution.py
+++ b/solution.py
@@ -48,11 +48,19 @@
 def stacked(first, second, axis):
     fh, fl = split(first)
     sh, sl = split(second)
-    return jnp.concatenate([fh, sh, fl, sl, fh, sh], axis)
+    return jnp.concatenate([fh, sh], axis), jnp.concatenate([fl, sl], axis)
 
 
 def times(left, right):
     return jnp.dot(left, right, preferred_element_type=exact)
+
+
+def left_product(table, columns):
+    n = table.shape[0] // 2
+    high = jnp.concatenate([column[0] for column in columns], 1)
+    low = jnp.concatenate([column[1] for column in columns], 1)
+    both = times(table[...], high)
+    return both[:n] + both[n:] + times(table[:n], low)
 
 
 def turned(re, im, cos, sin):
@@ -101,48 +109,48 @@
     return [(odd if r % 2 else even)[r // 2] for r in range(n)]
 
 
-def pack_kernel(half, *refs):
-    sources, (out, first_out, noise_out), held, landed, done = refs[:6], refs[6:9], refs[9:11], refs[11:15], refs[15]
+def pack_kernel(half, first, *refs):
+    sources, out, sent, held, landed, done = refs[:6], refs[6], refs[7], refs[8:10], refs[10:14], refs[14]
     targets = (*landed, *held)
     copies = [pltpu.make_async_copy(sources[i], targets[i], done.at[i]) for i in range(6)]
     for copy in copies:
         copy.start()
     bits, noise, kernel, symbol = landed
-    first = first_out.shape[0]
     copies[0].wait()
-    signs = (2 * bits[...] - 1).astype(exact).T
-    out[:lanes] = signs
-    first_out[:lanes] = signs
+    out[:lanes] = (2 * bits[...] - 1).astype(exact).T
     copies[1].wait()
-    noise = noise[...].T
-    out[first:] = noise
-    noise_out[...] = noise
+    out[first:] = noise[...].T
     copies[2].wait()
     copies[3].wait()
     depth = kernel.shape[0]
+    for a in range(half):
+        at = lanes + a * depth
+        out[at : at + depth] = kernel[:, a]
+        at += half * depth
+        out[at : at + depth] = symbol[:, a]
     middle = jnp.concatenate([kernel[0, half : half + 1], symbol[0, half : half + 1]], 0)
-    for target in (out, first_out):
-        for a in range(half):
-            at = lanes + a * depth
-            target[at : at + depth] = kernel[:, a]
-            at += half * depth
-            target[at : at + depth] = symbol[:, a]
-        target[first - lead : first] = jnp.concatenate([middle] * (lead // 2), 0)
+    out[first - lead : first] = jnp.concatenate([middle] * (lead // 2), 0)
+    sent[:first] = out[:first]
+    share = lanes // 2
+    side = lax.rem(lax.axis_index("probe"), 2)
+    sent[first:] = out[pl.ds(pl.multiple_of(first + side * share, lead), share)]
     copies[4].wait()
     copies[5].wait()
 
 
-def row_spectrum(signs, r, sign_right, left, w):
-    columns = []
-    for x in signs:
-        x = x[:lanes].astype(near)
-        section = times(jnp.concatenate([x, x], 1), sign_right)
-        columns.append(stacked(*turned(section[:, :lanes], section[:, lanes:], *w), 0))
-    done = times(left, jnp.concatenate(columns, 1))
+def row_spectra(signs, rows, sign_right, left, w, big_turn):
+    lined = [jnp.concatenate([x[:lanes].astype(near)] * 2, 1) for x in signs]
+    section = times(jnp.concatenate(lined, 0), sign_right)
     out = []
-    for k, turn in enumerate(r):
-        at = slice(k * lanes, (k + 1) * lanes)
-        out.append(turned(done[:lanes, at], done[lanes:, at], turn[:, :lanes], turn[:, lanes:]))
+    for j in range(0, len(signs), 2):
+        columns = []
+        for k in (j, j + 1):
+            at = slice(k * lanes, (k + 1) * lanes)
+            columns.append(stacked(*turned(section[at, :lanes], section[at, lanes:], *w), 0))
+        done = left_product(left, columns)
+        for k in range(2):
+            at, r = slice(k * lanes, (k + 1) * lanes), rows[j + k]
+            out.append(turned(done[:lanes, at], done[lanes:, at], big_turn[r, :, :lanes], big_turn[r, :, lanes:]))
     return out
 
 
@@ -151,14 +159,20 @@
     return jnp.concatenate([jnp.concatenate([c_high, s_high], 1), jnp.concatenate([c_low, s_low], 1)], 0)
 
 
+def early_slots(rows):
+    return [0, 1, *range(2, rows - 2, 2)]
+
+
 def early_kernel(rows, *refs):
-    early = rows - 2
-    blocks = refs[:early]
-    dft, turns, found, left, big_turn = refs[early:]
+    early = early_slots(rows)
+    blocks = refs[: len(early)]
+    dft, turns, found, left, big_turn = refs[len(early) :]
     me = lax.axis_index("seq")
     c_high, s_high, c_low, s_low = (dft[k] for k in range(4))
-    left[:lanes] = jnp.concatenate([c_high, -s_high, c_high, -s_high, c_low, -s_low], 1)
-    left[lanes:] = jnp.concatenate([s_high, c_high, s_high, c_high, s_low, c_low], 1)
+    left[:lanes] = jnp.concatenate([c_high, -s_high], 1)
+    left[lanes : 2 * lanes] = jnp.concatenate([s_high, c_high], 1)
+    left[2 * lanes : 3 * lanes] = jnp.concatenate([c_low, -s_low], 1)
+    left[3 * lanes :] = jnp.concatenate([s_low, c_low], 1)
     for t in range(0, lanes, lead):
         at = slice(t, t + lead)
         one = turns[1, at, :lanes], turns[1, at, lanes:]
@@ -169,26 +183,25 @@
             big_turn[r, at, :lanes] = powers[r][0]
             big_turn[r, at, lanes:] = powers[r][1]
     w = turns[0, :, :lanes], turns[0, :, lanes:]
-    for j in range(0, early, 2):
-        turn = [big_turn[me ^ j], big_turn[me ^ (j + 1)]]
-        for k, x in enumerate(row_spectrum(blocks[j : j + 2], turn, sign_table(dft), left[...], w)):
-            found[j + k, 0], found[j + k, 1] = x
+    at = [me ^ j for j in early]
+    for k, x in enumerate(row_spectra(blocks, at, sign_table(dft), left, w, big_turn)):
+        found[k, 0], found[k, 1] = x
 
 
 def inverse_kernel(rows, *refs):
     blocks = refs[:rows]
     found, left, dft, turns, big_turn, spectrum, precond, circulant, kernel, symbol, ends, work = refs[rows:]
-    half, early = rows // 2, rows - 2
+    half, early = rows // 2, early_slots(rows)
     depth = lanes // rows
     samples = rows * lanes * lanes
     me = lax.axis_index("seq")
     w = turns[0, :, :lanes], turns[0, :, lanes:]
-    for j in range(early):
-        work[me ^ j, 0, 0], work[me ^ j, 0, 1] = found[j, 0], found[j, 1]
-    for j in range(early, rows, 2):
-        turn = [big_turn[me ^ j], big_turn[me ^ (j + 1)]]
-        for k, x in enumerate(row_spectrum(blocks[j : j + 2], turn, sign_table(dft), left[...], w)):
-            work[me ^ (j + k), 0, 0], work[me ^ (j + k), 0, 1] = x
+    for k, j in enumerate(early):
+        work[me ^ j, 0, 0], work[me ^ j, 0, 1] = found[k, 0], found[k, 1]
+    late = [j for j in range(rows) if j not in early]
+    at = [me ^ j for j in late]
+    for r, x in zip(at, row_spectra([blocks[j] for j in late], at, sign_table(dft), left, w, big_turn)):
+        work[r, 0, 0], work[r, 0, 1] = x
     for t in range(0, lanes, lead):
         at = slice(t, t + lead)
         out = small_dft([(work[r, 0, 0, at], work[r, 0, 1, at]) for r in range(rows)], -1)
@@ -223,18 +236,23 @@
                 re, im = turned_back(*out[r], big_turn[r, at, :lanes], big_turn[r, at, lanes:])
                 work[r, field, 0, at] = re
                 work[r, field, 1, at] = im
-    back_right = jnp.concatenate([dft[k] for k in (0, 1, 0, 1, 2, 3)], 0)
+    c_high, s_high, c_low, s_low = (dft[k] for k in range(4))
+    back_right = jnp.concatenate([jnp.concatenate([c_high, s_high], 0), jnp.concatenate([c_low, s_low], 0)], 1)
+    highs, lows = [], []
     for r in range(rows):
         columns = [stacked(work[r, field, 1], work[r, field, 0], 0) for field in range(2)]
-        done = times(left[...], jnp.concatenate(columns, 1))
-        lined = []
+        done = left_product(left, columns)
         for field in range(2):
             at = slice(field * lanes, (field + 1) * lanes)
-            lined.append(stacked(*turned_back(done[lanes:, at], done[:lanes, at], *w), 1))
-        done = times(jnp.concatenate(lined, 0), back_right)
+            high, low = stacked(*turned_back(done[lanes:, at], done[:lanes, at], *w), 1)
+            highs.append(high)
+            lows.append(low)
+    both = times(jnp.concatenate(highs, 0), back_right)
+    done = both[:, :lanes] + both[:, lanes:] + times(jnp.concatenate(lows, 0), back_right[:, :lanes])
+    for r in range(rows):
         sign = 1.0 if r % 2 == 0 else -1.0
-        precond[r] = done[:lanes] + sign * middle
-        circulant[r] = done[lanes:] + sign * middle_image
+        precond[r] = done[2 * r * lanes : (2 * r + 1) * lanes] + sign * middle
+        circulant[r] = done[(2 * r + 1) * lanes : (2 * r + 2) * lanes] + sign * middle_image
 
 
 def whole_sum(x):
@@ -243,54 +261,71 @@
 
 def adjoint_kernel(rows, probes, *refs):
     signs = [refs[j].at[:lanes] for j in range(rows)]
-    near_noises = [refs[j].at[refs[j].shape[0] - lanes :] for j in range(rows // 2)]
-    noises = (*near_noises, *refs[rows : rows + rows // 2])
-    refs = refs[rows + rows // 2 :]
+    share = lanes // 2
+    own_noises = [refs[j].at[refs[j].shape[0] - lanes :] for j in range(2)]
+    held = [refs[j].at[refs[j].shape[0] - share :] for j in range(2, rows)]
+    others = [refs[rows + k].at[at : at + share] for at in (0, share) for k in (0, 1)] + list(refs[rows + 2 : rows + 4])
+    refs = refs[rows + 4 :]
+    noise = refs[-1]
+    refs = refs[:-1]
+    side = lax.rem(lax.axis_index("probe"), 2) * share
+    for j in range(rows - 2):
+        noise[j, pl.ds(pl.multiple_of(side, share), share)] = held[j][...]
+        noise[j, pl.ds(pl.multiple_of(share - side, share), share)] = others[j][...]
+    noises = (*own_noises, *(noise.at[j] for j in range(rows - 2)))
     precond, circulant, spectrum, kernel, symbol, left, dft, turns, big_turn, residual_out = refs[:10]
     outs = refs[10 : 10 + probes]
-    image, field, work, shares = refs[10 + probes :]
+    image, work, shares = refs[10 + probes :]
     depth = lanes // rows
     samples = rows * lanes * lanes
     me = lax.axis_index("seq")
+    c_high, s_high, c_low, s_low = (dft[k] for k in range(4))
+    wide_high, wide_low = jnp.concatenate([c_high, s_high], 1), jnp.concatenate([c_low, s_low], 1)
+    twice_high = jnp.concatenate([wide_high, wide_high], 0)
+    w = turns[0, :, :lanes], turns[0, :, lanes:]
+    own = pl.multiple_of(me * depth, depth)
+    parts = [left[pl.ds(pl.multiple_of(k * lanes + own, depth), depth)] for k in range(4)]
+    block = jnp.concatenate(parts, 0)
+
+    def own_spectra(fields, k):
+        highs, lows = zip(*(split(x) for x in fields))
+        highs, lows = jnp.concatenate(highs, 0), jnp.concatenate(lows, 0)
+        section = times(jnp.concatenate([highs, lows], 1), twice_high) + times(highs, wide_low)
+        for j in range(0, rows, 2):
+            columns = []
+            for i in (j, j + 1):
+                at = slice(i * lanes, (i + 1) * lanes)
+                columns.append(stacked(*turned(section[at, :lanes], section[at, lanes:], *w), 0))
+            done = left_product(block, columns)
+            for i in range(2):
+                at, r = slice(i * lanes, (i + 1) * lanes), me ^ (j + i)
+                gc, gs = big_turn[r, pl.ds(own, depth), :lanes], big_turn[r, pl.ds(own, depth), lanes:]
+                work[r, k, 0], work[r, k, 1] = turned(done[:depth, at], done[depth:, at], gc, gs)
+
     numerator = jnp.zeros((lanes, lanes), exact)
     curvature = jnp.zeros((lanes, lanes), exact)
+    fields = []
     for j in range(rows):
         p = precond[me ^ j]
-        ki = circulant[me ^ j] + noises[j][...] * p
+        noisy = noises[j][...] * p
+        ki = circulant[me ^ j] + noisy
         image[j] = ki
+        fields.append(noisy)
         numerator += signs[j][...] * p
         curvature += p * ki
     numerator, curvature = whole_sum(numerator), whole_sum(curvature)
+    own_spectra(fields, 0)
     step_size = numerator / curvature
     cross = jnp.zeros((lanes, lanes), exact)
+    fields = []
     for j in range(rows):
         residual = signs[j][...] - step_size * image[j]
         cross += residual * image[j]
-        field[j] = residual
+        fields.append(noises[j][...] * residual)
+        if j == 0:
+            residual_out[...] = residual.T
     weight = -2.0 * whole_sum(cross)
-    residual_out[...] = field[0].T
-    wc, ws = turns[0, :, :lanes], turns[0, :, lanes:]
-    own = pl.multiple_of(me * depth, depth)
-    real_right = jnp.concatenate([jnp.concatenate([dft[k], dft[k + 1]], 1) for k in (0, 0, 2)], 0)
-    block = jnp.concatenate([left[pl.ds(own, depth)], left[pl.ds(pl.multiple_of(lanes + own, depth), depth)]], 0)
-    for j in range(rows):
-        r = me ^ j
-        lined = []
-        for x in (precond[r], field[j]):
-            high, low = split(noises[j][...] * x)
-            lined.append(jnp.concatenate([high, low, high], 1))
-        section = times(jnp.concatenate(lined, 0), real_right)
-        columns = []
-        for k in range(2):
-            at = slice(k * lanes, (k + 1) * lanes)
-            columns.append(stacked(*turned(section[at, :lanes], section[at, lanes:], wc, ws), 0))
-        done = times(block, jnp.concatenate(columns, 1))
-        gc, gs = big_turn[r, pl.ds(own, depth), :lanes], big_turn[r, pl.ds(own, depth), lanes:]
-        for k in range(2):
-            at = slice(k * lanes, (k + 1) * lanes)
-            re, im = turned(done[:depth, at], done[depth:, at], gc, gs)
-            work[r, k, 0] = re
-            work[r, k, 1] = im
+    own_spectra(fields, 1)
     noisy = small_dft([(work[r, 0, 0], work[r, 0, 1]) for r in range(rows)], -1)
     noisy_residual = small_dft([(work[r, 1, 0], work[r, 1, 1]) for r in range(rows)], -1)
     for a in range(rows):
@@ -317,7 +352,7 @@
 def call(kernel, outs, scratch, *operands):
     whole = pl.BlockSpec(memory_space=pltpu.VMEM)
     typed = [out if isinstance(out[0], tuple) else (out, exact) for out in outs]
-    shapes = tuple(jax.ShapeDtypeStruct(shape, dtype) for shape, dtype in typed)
+    shapes = tuple(pltpu.VMEM(shape, dtype) for shape, dtype in typed)
     return pl.pallas_call(
         kernel,
         out_shape=shapes,
@@ -343,6 +378,10 @@
 
 def other_core(x):
     return swapped(x, "seq", 1)
+
+
+def across_x(x):
+    return swapped(x, "probe", 1)
 
 
 def next_chip(x):
@@ -363,15 +402,16 @@
     square = (lanes, lanes)
     dft, turns = tables(rows)
     first = lanes + 2 * half * depth + lead
-    block, mine, noise, dft, turns = pl.pallas_call(
-        functools.partial(pack_kernel, half),
+    block, sent, dft, turns = pl.pallas_call(
+        functools.partial(pack_kernel, half, first),
         out_shape=(
-            *(pltpu.VMEM((n, lanes), exact) for n in (first + lanes, first, lanes)),
+            pltpu.VMEM((first + lanes, lanes), exact),
+            pltpu.VMEM((first + lanes // 2, lanes), exact),
             pltpu.VMEM(dft.shape, near),
             pltpu.VMEM(turns.shape, exact),
         ),
         in_specs=[pl.BlockSpec(memory_space=pl.ANY)] * 6,
-        out_specs=(pl.BlockSpec(memory_space=pltpu.VMEM),) * 5,
+        out_specs=(pl.BlockSpec(memory_space=pltpu.VMEM),) * 4,
         scratch_shapes=[
             pltpu.VMEM(square, jnp.int32),
             pltpu.VMEM(square, exact),
@@ -380,22 +420,22 @@
             pltpu.SemaphoreType.DMA((6,)),
         ],
     )(probe_bits.reshape(square), noise_var.reshape(square), kernel, symbols, dft, turns)
-    far = beyond_middle(mine)
-    neighbour = next_chip(block)
-    blocks = [block, other_core(block), neighbour, other_core(neighbour), far, other_core(far)]
+    far = beyond_middle(sent)
+    neighbour = next_chip(sent)
     passed_on = next_chip(far)
-    far_noise = beyond_middle(after(noise, far))
-    passed_noise = next_chip(far_noise)
+    early = [block, other_core(block), neighbour, far]
     found, left, big_turn = call(
         functools.partial(early_kernel, rows),
-        [(rows - 2, 2, *square), ((2 * lanes, 6 * lanes), near), (rows, lanes, 2 * lanes)],
+        [(len(early), 2, *square), ((4 * lanes, 2 * lanes), near), (rows, lanes, 2 * lanes)],
         [],
-        *blocks,
+        *early,
         dft,
         turns,
     )
-    last = after(passed_on, found, far_noise)
-    blocks += [last, other_core(last)]
+    halves = across_x(jnp.concatenate([neighbour[first:], far[first:]], 0))
+    blocks = early[:2]
+    for x, earlier in ((neighbour, found), (far, found), (passed_on, halves)):
+        blocks += [x, other_core(after(x, earlier))]
     field = (rows, *square)
     spectrum, precond, circulant = call(
         functools.partial(inverse_kernel, rows),
@@ -408,13 +448,14 @@
         turns,
         big_turn,
     )
-    passed_noise = after(passed_noise, precond)
-    noises = [far_noise, other_core(far_noise), passed_noise, other_core(passed_noise)]
+    passed_half = next_chip(halves[lanes // 2 :])
+    last = after(passed_half, precond)
+    noises = [halves, other_core(halves), last, other_core(last)]
     share = (depth, width, lanes)
     residual, *parts = call(
         functools.partial(adjoint_kernel, rows, probes),
         [square] + [share] * probes,
-        [field, field, (rows, 2, 2, depth, lanes), (rows, depth, lanes)],
+        [field, (rows, 2, 2, depth, lanes), (rows, depth, lanes), (rows - 2, *square)],
         *blocks,
         *noises,
         precond,
@@ -427,8 +468,9 @@
         turns,
         big_turn,
     )
-    arrived = [swapped(parts[d], "probe", d) for d in reversed(range(1, probes))]
-    total = before + sum(arrived, parts[0]) / probes
+    arrived = [swapped(parts[d], "probe", d) for d in range(1, probes)]
+    total = lax.optimization_barrier(parts[0] + arrived.pop())
+    total = before + sum(arrived, total) / probes
     total = total.transpose(1, 0, 2).reshape(width, depth * lanes).T
     return residual.reshape(probe_bits.shape), total
 

time: 39.7 us -> 34.9 us (0.88)
  Pallas kernels: 9.93 us -> 6.86 us
  starting transfers between devices: 16.2 us -> 14 us
  local copies, waits for them, and re-layouts: 0.01 us -> 0.65 us
    pallas_call x3, Pallas kernels: 8.72 us -> 5.65 us  [call(): pl.pallas_call(kernel, out_shape=shapes, in_specs=[whole] * len(operands)...]
    ppermute x14, starting transfers between devices: 16.2 us -> 14 us  [swapped(): lax.ppermute(x, axis, [(i, i ^ d) for i in range(lax.axis_size(axis))])]
    unnamed x6 -> x7, local copies, waits for them, and re-layouts: 0.01 us -> 0.65 us
  transfers between devices with their start and end apart: 14 -> 14, of which waited for: 7 -> 7; matrix products, arithmetic and copies ran while one was open for 0% -> 2% of each run, Pallas kernels for 12% -> 10%
where the time goes in v4:
time: 34.9 us; the launch traced here: 34.8 us
  starting transfers between devices  14 us (40%)
  waiting for transfers between devices  11.9 us (34%)
  Pallas kernels  6.86 us (20%)
  between operations  0.72 us (2%)
  local copies, waits for them, and re-layouts  0.65 us (2%)
  other arithmetic  0.64 us (2%)
    ppermute x14, starting transfers between devices, swapped(): lax.ppermute(x, axis, [(i, i ^ d) for i in range(lax.axis_size(axis))])  14 us
    ppermute x14, waiting for transfers between devices, swapped(): lax.ppermute(x, axis, [(i, i ^ d) for i in range(lax.axis_size(axis))])  11.9 us
    pallas_call x3, Pallas kernels, call(): pl.pallas_call(kernel, out_shape=shapes, in_specs=[whole] * len(operands)...  5.65 us
    pallas_call x1, Pallas kernels, gathered_shards(): pl.pallas_call(functools.partial(pack_kernel, half, first), out_shape=(pl...  1.21 us
  transfers between devices with their start and end apart: 14, of which 7 were waited for; matrix products, arithmetic and copies ran while one was open for 2% of the time, Pallas kernels for 10%

profile of v4, /device:TPU:0, one launch (start us, length us, event | category | flops | bytes accessed | tf_op | source)
XLA Modules:
  0.0 34.8 jit_solution(14079420465223653409)
XLA Ops:
  0.6 1.2 %shard_map.86 = (f32[392,128]{1,0:T(8,128)S(1)}, f32[328,128]{1,0:T(8,128)S(1)}, bf16[4,128,128]{2,1,0:T(8,128)(2,1)S(1)}, f32[2,128,256]{2,1,0:T(8,128)S(1)}) custom-call(s32[128,128]{1,0:T(8,128)} %bitcast.32, f32[128,128]{1,0:T(8,128)} %bitcast.33, f32[16,8,128]{2,1,0:T(8,128)} %bitcast.28, f32[16,8,128]{2,1,0:T(8,128)} %bitcast.30, ...), custom_call_target="tpu_custom_call" | custom-call | tf_op jit(solution)/shard_map/pallas_call | solution.py:405
  1.8 4.1 %collective-permute-start.2 = (f32[328,128]{1,0:T(8,128)S(1)}, f32[328,128]{1,0:T(8,128)S(1)}, u32[]{:S(2)}, u32[]{:S(2)}) collective-permute-start(f32[328,128]{1,0:T(8,128)S(1)} %get-tuple-element.22), channel_id=1, source_target_pairs={{0,4},{1,5},{2,6},{3,7},{4,0},{5,1},{6,2},{7,3},{8,12},{9,13},{10,... | collective-permute-start | bytes 503816 | tf_op jit(solution)/shard_map/ppermute | solution.py:368
  5.9 1.6 %collective-permute-start.1 = (f32[328,128]{1,0:T(8,128)S(1)}, f32[328,128]{1,0:T(8,128)S(1)}, u32[]{:S(2)}, u32[]{:S(2)}) collective-permute-start(f32[328,128]{1,0:T(8,128)S(1)} %get-tuple-element.22), channel_id=1, source_target_pairs={{0,2},{1,3},{2,0},{3,1},{4,6},{5,7},{6,4},{7,5},{8,10},{9,11},{10,... | collective-permute-start | bytes 503816 | tf_op jit(solution)/shard_map/ppermute | solution.py:368
  7.5 0.0 collective-permute-start
  7.5 6.4 %collective-permute-done.2.refs_3_.refs_4_ = f32[328,128]{1,0:T(8,128)S(1)} collective-permute-done((f32[328,128]{1,0:T(8,128)S(1)}, f32[328,128]{1,0:T(8,128)S(1)}, u32[]{:S(2)}, u32[]{:S(2)}) %collective-permute-start.2) | collective-permute-done | bytes 167968 | tf_op jit(solution)/shard_map/ppermute | solution.py:368
  13.9 0.6 %collective-permute-start.5 = (f32[328,128]{1,0:T(8,128)S(1)}, f32[328,128]{1,0:T(8,128)S(1)}, u32[]{:S(2)}, u32[]{:S(2)}) collective-permute-start(f32[328,128]{1,0:T(8,128)S(1)} %collective-permute-done.2.refs_3_.refs_4_), channel_id=1, source_target_pairs={{0,2},{1,3},{2,0},{3,1},{4,6},{5,7},{6,4},{7,5},{8,10},{9,11},{10,... | collective-permute-start | bytes 503816 | tf_op jit(solution)/shard_map/ppermute | solution.py:368
  14.6 0.0 collective-permute-done.1.refs_2_
  14.6 1.6 %collective-permute-start.6 = (f32[128,128]{1,0:T(8,128)S(1)}, f32[128,128]{1,0:T(8,128)S(1)}, u32[]{:S(2)}, u32[]{:S(2)}) collective-permute-start(f32[128,128]{1,0:T(8,128)S(1)} %pad_maximum_fusion), channel_id=1, source_target_pairs={{0,8},{8,0},{16,24},{24,16},{1,9},{9,1},{17,25},{25,17},{2,10},{10... | collective-permute-start | bytes 196616 | tf_op jit(solution)/shard_map/ppermute | solution.py:368
  16.1 0.0 collective-permute-done.refs_1_
  16.1 0.6 %shard_map.87 = (f32[4,2,128,128]{3,2,1,0:T(8,128)S(1)}, bf16[512,256]{1,0:T(8,128)(2,1)S(1)}, f32[8,128,256]{2,1,0:T(8,128)S(1)}) custom-call(f32[392,128]{1,0:T(8,128)S(1)} %get-tuple-element.21.refs_0_, f32[392,128]{1,0:T(8,128)S(1)} %collective-permute-done.refs_1_, f32[328,128]{1,0:T(8,128)S(1)} %collective-permute-done.1.refs_2_, ...), custom_call_target="tpu_custom_call" | custom-call | tf_op jit(solution)/shard_map/pallas_call | solution.py:356
  16.8 0.1 collective-permute-start.4
  16.9 0.5 %collective-permute-start.3 = (f32[328,128]{1,0:T(8,128)S(1)}, f32[328,128]{1,0:T(8,128)S(1)}, u32[]{:S(2)}, u32[]{:S(2)}) collective-permute-start(f32[328,128]{1,0:T(8,128)S(1)} %collective-permute-done.1.refs_2_), channel_id=1, source_target_pairs={{0,1},{1,0},{2,3},{3,2},{4,5},{5,4},{6,7},{7,6},{8,9},{9,8},{10,11... | collective-permute-start | bytes 503816 | tf_op jit(solution)/shard_map/ppermute | solution.py:368
  17.4 1.5 %collective-permute-done.6.refs_8_ = f32[128,128]{1,0:T(8,128)S(1)} collective-permute-done((f32[128,128]{1,0:T(8,128)S(1)}, f32[128,128]{1,0:T(8,128)S(1)}, u32[]{:S(2)}, u32[]{:S(2)}) %collective-permute-start.6) | collective-permute-done | bytes 65568 | tf_op jit(solution)/shard_map/ppermute | solution.py:368
  18.9 0.4 %collective-permute-done.5.refs_6_ = f32[328,128]{1,0:T(8,128)S(1)} collective-permute-done((f32[328,128]{1,0:T(8,128)S(1)}, f32[328,128]{1,0:T(8,128)S(1)}, u32[]{:S(2)}, u32[]{:S(2)}) %collective-permute-start.5) | collective-permute-done | bytes 167968 | tf_op jit(solution)/shard_map/ppermute | solution.py:368
  19.3 0.0 collective-permute-start.7
  19.3 1.5 %collective-permute-start.9 = (f32[64,128]{1,0:T(8,128)S(1)}, f32[64,128]{1,0:T(8,128)S(1)}, u32[]{:S(2)}, u32[]{:S(2)}) collective-permute-start(f32[64,128]{1,0:T(8,128)S(1)} %slice.14), channel_id=1, source_target_pairs={{0,2},{1,3},{2,0},{3,1},{4,6},{5,7},{6,4},{7,5},{8,10},{9,11},{10,... | collective-permute-start | bytes 98312 | tf_op jit(solution)/shard_map/ppermute | solution.py:368
  20.8 0.2 collective-permute-start.8
  21.0 0.0 collective-permute-done.4.refs_5_
  21.0 0.0 collective-permute-done.3.refs_3_
  21.0 0.0 collective-permute-done.7.refs_7_
  21.0 0.0 copy-start
  21.0 0.0 copy-start.1
  21.0 2.9 %shard_map.88 = (f32[8,2,128,128]{3,2,1,0:T(8,128)S(1)}, f32[8,128,128]{2,1,0:T(8,128)S(1)}, f32[8,128,128]{2,1,0:T(8,128)S(1)}) custom-call(f32[392,128]{1,0:T(8,128)S(1)} %get-tuple-element.21.refs_0_, f32[392,128]{1,0:T(8,128)S(1)} %collective-permute-done.refs_1_, f32[328,128]{1,0:T(8,128)S(1)} %collective-permute-done.1.refs_2_, ...), custom_call_target="tpu_custom_call" | custom-call | tf_op jit(solution)/shard_map/pallas_call | solution.py:356
  24.0 0.0 collective-permute-done.9.refs_10_
  24.0 0.3 %collective-permute-start.10 = (f32[64,128]{1,0:T(8,128)S(1)}, f32[64,128]{1,0:T(8,128)S(1)}, u32[]{:S(2)}, u32[]{:S(2)}) collective-permute-start(f32[64,128]{1,0:T(8,128)S(1)} %collective-permute-done.9.refs_10_), channel_id=1, source_target_pairs={{0,1},{1,0},{2,3},{3,2},{4,5},{5,4},{6,7},{7,6},{8,9},{9,8},{10,11... | collective-permute-start | bytes 98312 | tf_op jit(solution)/shard_map/ppermute | solution.py:368
  24.4 0.0 collective-permute-done.8.refs_9_
  24.4 0.9 %collective-permute-done.10.refs_11_ = f32[64,128]{1,0:T(8,128)S(1)} collective-permute-done((f32[64,128]{1,0:T(8,128)S(1)}, f32[64,128]{1,0:T(8,128)S(1)}, u32[]{:S(2)}, u32[]{:S(2)}) %collective-permute-start.10) | collective-permute-done | bytes 32800 | tf_op jit(solution)/shard_map/ppermute | solution.py:368
  25.3 0.0 copy-done
  25.3 0.0 copy-done.1
  25.3 2.1 %shard_map.89 = (f32[128,128]{1,0:T(8,128)S(1)}, f32[16,2,128]{2,1,0:T(2,128)S(1)}, f32[16,2,128]{2,1,0:T(2,128)S(1)}, f32[16,2,128]{2,1,0:T(2,128)S(1)}, f32[16,2,128]{2,1,0:T(2,128)S(1)}) custom-call(f32[392,128]{1,0:T(8,128)S(1)} %get-tuple-element.21.refs_0_, f32[392,128]{1,0:T(8,128)S(1)} %collective-permute-done.refs_1_, ...), custom_call_target="tpu_custom_call" | custom-call | tf_op jit(solution)/shard_map/pallas_call | solution.py:356
  27.3 2.5 %collective-permute-start.11 = (f32[16,2,128]{2,1,0:T(2,128)S(1)}, f32[16,2,128]{2,1,0:T(2,128)S(1)}, u32[]{:S(2)}, u32[]{:S(2)}) collective-permute-start(f32[16,2,128]{2,1,0:T(2,128)S(1)} %get-tuple-element.37), channel_id=1, source_target_pairs={{0,24},{8,16},{16,8},{24,0},{1,25},{9,17},{17,9},{25,1},{2,26},{10... | collective-permute-start | bytes 49160 | tf_op jit(solution)/shard_map/ppermute | solution.py:368
  29.9 0.5 %collective-permute-start.12 = (f32[16,2,128]{2,1,0:T(2,128)S(1)}, f32[16,2,128]{2,1,0:T(2,128)S(1)}, u32[]{:S(2)}, u32[]{:S(2)}) collective-permute-start(f32[16,2,128]{2,1,0:T(2,128)S(1)} %get-tuple-element.38), channel_id=1, source_target_pairs={{0,8},{8,0},{16,24},{24,16},{1,9},{9,1},{17,25},{25,17},{2,10},{10... | collective-permute-start | bytes 49160 | tf_op jit(solution)/shard_map/ppermute | solution.py:368
  30.4 0.5 %collective-permute-start.13 = (f32[16,2,128]{2,1,0:T(2,128)S(1)}, f32[16,2,128]{2,1,0:T(2,128)S(1)}, u32[]{:S(2)}, u32[]{:S(2)}) collective-permute-start(f32[16,2,128]{2,1,0:T(2,128)S(1)} %get-tuple-element.39), channel_id=1, source_target_pairs={{0,16},{8,24},{16,0},{24,8},{1,17},{9,25},{17,1},{25,9},{2,18},{10... | collective-permute-start | bytes 49160 | tf_op jit(solution)/shard_map/ppermute | solution.py:368
  30.9 0.6 %copy.9 = f32[1,1,16384]{2,1,0:T(1,128)} copy(f32[1,1,16384]{2,1,0:T(1,128)S(1)} %bitcast.27) | data formatting | bytes 131072
  31.5 0.5 %collective-permute-done.11 = f32[16,2,128]{2,1,0:T(2,128)S(1)} collective-permute-done((f32[16,2,128]{2,1,0:T(2,128)S(1)}, f32[16,2,128]{2,1,0:T(2,128)S(1)}, u32[]{:S(2)}, u32[]{:S(2)}) %collective-permute-start.11) | collective-permute-done | bytes 16416 | tf_op jit(solution)/shard_map/ppermute | solution.py:368
  32.0 0.0 copy-start.2
  32.1 1.5 %collective-permute-done.12 = f32[16,2,128]{2,1,0:T(2,128)S(1)} collective-permute-done((f32[16,2,128]{2,1,0:T(2,128)S(1)}, f32[16,2,128]{2,1,0:T(2,128)S(1)}, u32[]{:S(2)}, u32[]{:S(2)}) %collective-permute-start.12) | collective-permute-done | bytes 16416 | tf_op jit(solution)/shard_map/ppermute | solution.py:368
  33.6 0.5 %collective-permute-done.13 = f32[16,2,128]{2,1,0:T(2,128)S(1)} collective-permute-done((f32[16,2,128]{2,1,0:T(2,128)S(1)}, f32[16,2,128]{2,1,0:T(2,128)S(1)}, u32[]{:S(2)}, u32[]{:S(2)}) %collective-permute-start.13) | collective-permute-done | bytes 16416 | tf_op jit(solution)/shard_map/ppermute | solution.py:368
  34.1 0.0 copy-done.2
  34.1 0.6 %fusion = f32[2048,2]{0,1:T(2,128)} fusion(f32[2048,2]{0,1:T(2,128)S(1)} %copy-done.2, f32[16,2,128]{2,1,0:T(2,128)S(1)} %collective-permute-done.13, f32[16,2,128]{2,1,0:T(2,128)S(1)} %add.12, f32[16,2,128]{2,1,0:T(2,128)S(1)} %collective-permute-done.12), kind=kLoop, calls=%fused_computation.2 | loop fusion | flops 16384 | bytes 81920 | tf_op jit(solution)/shard_map/transpose | solution.py:474
  (5 shorter events, 0.0 us)
Async XLA Ops:
  1.8 12.1 %collective-permute-start.2 = (f32[328,128]{1,0:T(8,128)S(1)}, f32[328,128]{1,0:T(8,128)S(1)}, u32[]{:S(2)}, u32[]{:S(2)}) collective-permute-start(f32[328,128]{1,0:T(8,128)S(1)} %get-tuple-element.22), channel_id=1, source_target_pairs={{0,4},{1,5},{2,6},{3,7},{4,0},{5,1},{6,2},{7,3},{8,12},{9,13},{10,... | collective-permute-start | bytes 503816 | tf_op jit(solution)/shard_map/ppermute | solution.py:368
  5.9 8.6 %collective-permute-start.1 = (f32[328,128]{1,0:T(8,128)S(1)}, f32[328,128]{1,0:T(8,128)S(1)}, u32[]{:S(2)}, u32[]{:S(2)}) collective-permute-start(f32[328,128]{1,0:T(8,128)S(1)} %get-tuple-element.22), channel_id=1, source_target_pairs={{0,2},{1,3},{2,0},{3,1},{4,6},{5,7},{6,4},{7,5},{8,10},{9,11},{10,... | collective-permute-start | bytes 503816 | tf_op jit(solution)/shard_map/ppermute | solution.py:368
  7.5 8.6 %collective-permute-start = (f32[392,128]{1,0:T(8,128)S(1)}, f32[392,128]{1,0:T(8,128)S(1)}, u32[]{:S(2)}, u32[]{:S(2)}) collective-permute-start(f32[392,128]{1,0:T(8,128)S(1)} %get-tuple-element.21.refs_0_), channel_id=1, source_target_pairs={{0,1},{1,0},{2,3},{3,2},{4,5},{5,4},{6,7},{7,6},{8,9},{9,8},{10,11... | collective-permute-start | bytes 602120 | tf_op jit(solution)/shard_map/ppermute | solution.py:368
  13.9 5.4 %collective-permute-start.5 = (f32[328,128]{1,0:T(8,128)S(1)}, f32[328,128]{1,0:T(8,128)S(1)}, u32[]{:S(2)}, u32[]{:S(2)}) collective-permute-start(f32[328,128]{1,0:T(8,128)S(1)} %collective-permute-done.2.refs_3_.refs_4_), channel_id=1, source_target_pairs={{0,2},{1,3},{2,0},{3,1},{4,6},{5,7},{6,4},{7,5},{8,10},{9,11},{10,... | collective-permute-start | bytes 503816 | tf_op jit(solution)/shard_map/ppermute | solution.py:368
  14.6 4.3 %collective-permute-start.6 = (f32[128,128]{1,0:T(8,128)S(1)}, f32[128,128]{1,0:T(8,128)S(1)}, u32[]{:S(2)}, u32[]{:S(2)}) collective-permute-start(f32[128,128]{1,0:T(8,128)S(1)} %pad_maximum_fusion), channel_id=1, source_target_pairs={{0,8},{8,0},{16,24},{24,16},{1,9},{9,1},{17,25},{25,17},{2,10},{10... | collective-permute-start | bytes 196616 | tf_op jit(solution)/shard_map/ppermute | solution.py:368
  16.8 4.2 %collective-permute-start.4 = (f32[328,128]{1,0:T(8,128)S(1)}, f32[328,128]{1,0:T(8,128)S(1)}, u32[]{:S(2)}, u32[]{:S(2)}) collective-permute-start(f32[328,128]{1,0:T(8,128)S(1)} %collective-permute-done.2.refs_3_.refs_4_), channel_id=1, source_target_pairs={{0,1},{1,0},{2,3},{3,2},{4,5},{5,4},{6,7},{7,6},{8,9},{9,8},{10,11... | collective-permute-start | bytes 503816 | tf_op jit(solution)/shard_map/ppermute | solution.py:368
  16.9 4.1 %collective-permute-start.3 = (f32[328,128]{1,0:T(8,128)S(1)}, f32[328,128]{1,0:T(8,128)S(1)}, u32[]{:S(2)}, u32[]{:S(2)}) collective-permute-start(f32[328,128]{1,0:T(8,128)S(1)} %collective-permute-done.1.refs_2_), channel_id=1, source_target_pairs={{0,1},{1,0},{2,3},{3,2},{4,5},{5,4},{6,7},{7,6},{8,9},{9,8},{10,11... | collective-permute-start | bytes 503816 | tf_op jit(solution)/shard_map/ppermute | solution.py:368
  19.3 1.7 %collective-permute-start.7 = (f32[328,128]{1,0:T(8,128)S(1)}, f32[328,128]{1,0:T(8,128)S(1)}, u32[]{:S(2)}, u32[]{:S(2)}) collective-permute-start(f32[328,128]{1,0:T(8,128)S(1)} %collective-permute-done.5.refs_6_), channel_id=1, source_target_pairs={{0,1},{1,0},{2,3},{3,2},{4,5},{5,4},{6,7},{7,6},{8,9},{9,8},{10,11... | collective-permute-start | bytes 503816 | tf_op jit(solution)/shard_map/ppermute | solution.py:368
  19.3 4.7 %collective-permute-start.9 = (f32[64,128]{1,0:T(8,128)S(1)}, f32[64,128]{1,0:T(8,128)S(1)}, u32[]{:S(2)}, u32[]{:S(2)}) collective-permute-start(f32[64,128]{1,0:T(8,128)S(1)} %slice.14), channel_id=1, source_target_pairs={{0,2},{1,3},{2,0},{3,1},{4,6},{5,7},{6,4},{7,5},{8,10},{9,11},{10,... | collective-permute-start | bytes 98312 | tf_op jit(solution)/shard_map/ppermute | solution.py:368
  20.8 3.6 %collective-permute-start.8 = (f32[128,128]{1,0:T(8,128)S(1)}, f32[128,128]{1,0:T(8,128)S(1)}, u32[]{:S(2)}, u32[]{:S(2)}) collective-permute-start(f32[128,128]{1,0:T(8,128)S(1)} %collective-permute-done.6.refs_8_), channel_id=1, source_target_pairs={{0,1},{1,0},{2,3},{3,2},{4,5},{5,4},{6,7},{7,6},{8,9},{9,8},{10,11... | collective-permute-start | bytes 196616 | tf_op jit(solution)/shard_map/ppermute | solution.py:368
  21.0 4.3 %copy-start = (f32[2048,8]{0,1:T(8,128)S(1)}, f32[2048,8]{0,1:T(8,128)}, u32[]{:S(2)}) copy-start(f32[2048,8]{0,1:T(8,128)} %param.9) | copy-start | bytes 196612
  21.0 4.3 %copy-start.1 = (f32[2048,8]{0,1:T(8,128)S(1)}, f32[2048,8]{0,1:T(8,128)}, u32[]{:S(2)}) copy-start(f32[2048,8]{0,1:T(8,128)} %param.10) | copy-start | bytes 196612
  24.0 1.3 %collective-permute-start.10 = (f32[64,128]{1,0:T(8,128)S(1)}, f32[64,128]{1,0:T(8,128)S(1)}, u32[]{:S(2)}, u32[]{:S(2)}) collective-permute-start(f32[64,128]{1,0:T(8,128)S(1)} %collective-permute-done.9.refs_10_), channel_id=1, source_target_pairs={{0,1},{1,0},{2,3},{3,2},{4,5},{5,4},{6,7},{7,6},{8,9},{9,8},{10,11... | collective-permute-start | bytes 98312 | tf_op jit(solution)/shard_map/ppermute | solution.py:368
  27.3 4.7 %collective-permute-start.11 = (f32[16,2,128]{2,1,0:T(2,128)S(1)}, f32[16,2,128]{2,1,0:T(2,128)S(1)}, u32[]{:S(2)}, u32[]{:S(2)}) collective-permute-start(f32[16,2,128]{2,1,0:T(2,128)S(1)} %get-tuple-element.37), channel_id=1, source_target_pairs={{0,24},{8,16},{16,8},{24,0},{1,25},{9,17},{17,9},{25,1},{2,26},{10... | collective-permute-start | bytes 49160 | tf_op jit(solution)/shard_map/ppermute | solution.py:368
  29.9 3.7 %collective-permute-start.12 = (f32[16,2,128]{2,1,0:T(2,128)S(1)}, f32[16,2,128]{2,1,0:T(2,128)S(1)}, u32[]{:S(2)}, u32[]{:S(2)}) collective-permute-start(f32[16,2,128]{2,1,0:T(2,128)S(1)} %get-tuple-element.38), channel_id=1, source_target_pairs={{0,8},{8,0},{16,24},{24,16},{1,9},{9,1},{17,25},{25,17},{2,10},{10... | collective-permute-start | bytes 49160 | tf_op jit(solution)/shard_map/ppermute | solution.py:368
  30.4 3.7 %collective-permute-start.13 = (f32[16,2,128]{2,1,0:T(2,128)S(1)}, f32[16,2,128]{2,1,0:T(2,128)S(1)}, u32[]{:S(2)}, u32[]{:S(2)}) collective-permute-start(f32[16,2,128]{2,1,0:T(2,128)S(1)} %get-tuple-element.39), channel_id=1, source_target_pairs={{0,16},{8,24},{16,0},{24,8},{1,17},{9,25},{17,1},{25,9},{2,18},{10... | collective-permute-start | bytes 49160 | tf_op jit(solution)/shard_map/ppermute | solution.py:368
  32.0 2.1 %copy-start.2 = (f32[2048,2]{0,1:T(2,128)S(1)}, f32[2048,2]{0,1:T(2,128)}, u32[]{:S(2)}) copy-start(f32[2048,2]{0,1:T(2,128)} %param.11) | copy-start | bytes 49156

commit v5 on v4

--- a/solution.py
+++ b/solution.py
@@ -259,73 +259,115 @@
     return jnp.sum(jnp.sum(x, axis=0, keepdims=True), axis=1, keepdims=True)
 
 
-def adjoint_kernel(rows, probes, *refs):
-    signs = [refs[j].at[:lanes] for j in range(rows)]
-    share = lanes // 2
-    own_noises = [refs[j].at[refs[j].shape[0] - lanes :] for j in range(2)]
-    held = [refs[j].at[refs[j].shape[0] - share :] for j in range(2, rows)]
-    others = [refs[rows + k].at[at : at + share] for at in (0, share) for k in (0, 1)] + list(refs[rows + 2 : rows + 4])
-    refs = refs[rows + 4 :]
-    noise = refs[-1]
-    refs = refs[:-1]
-    side = lax.rem(lax.axis_index("probe"), 2) * share
-    for j in range(rows - 2):
-        noise[j, pl.ds(pl.multiple_of(side, share), share)] = held[j][...]
-        noise[j, pl.ds(pl.multiple_of(share - side, share), share)] = others[j][...]
-    noises = (*own_noises, *(noise.at[j] for j in range(rows - 2)))
-    precond, circulant, spectrum, kernel, symbol, left, dft, turns, big_turn, residual_out = refs[:10]
-    outs = refs[10 : 10 + probes]
-    image, work, shares = refs[10 + probes :]
+def folded(x):
+    return sum(x[t : t + lead] for t in range(0, x.shape[0], lead))
+
+
+def own_spectra(fields, at, left, dft, turns, big_turn):
+    rows = big_turn.shape[0]
     depth = lanes // rows
-    samples = rows * lanes * lanes
-    me = lax.axis_index("seq")
+    own = pl.multiple_of(lax.axis_index("seq") * depth, depth)
     c_high, s_high, c_low, s_low = (dft[k] for k in range(4))
     wide_high, wide_low = jnp.concatenate([c_high, s_high], 1), jnp.concatenate([c_low, s_low], 1)
     twice_high = jnp.concatenate([wide_high, wide_high], 0)
     w = turns[0, :, :lanes], turns[0, :, lanes:]
-    own = pl.multiple_of(me * depth, depth)
     parts = [left[pl.ds(pl.multiple_of(k * lanes + own, depth), depth)] for k in range(4)]
     block = jnp.concatenate(parts, 0)
-
-    def own_spectra(fields, k):
-        highs, lows = zip(*(split(x) for x in fields))
-        highs, lows = jnp.concatenate(highs, 0), jnp.concatenate(lows, 0)
-        section = times(jnp.concatenate([highs, lows], 1), twice_high) + times(highs, wide_low)
-        for j in range(0, rows, 2):
-            columns = []
-            for i in (j, j + 1):
-                at = slice(i * lanes, (i + 1) * lanes)
-                columns.append(stacked(*turned(section[at, :lanes], section[at, lanes:], *w), 0))
-            done = left_product(block, columns)
-            for i in range(2):
-                at, r = slice(i * lanes, (i + 1) * lanes), me ^ (j + i)
-                gc, gs = big_turn[r, pl.ds(own, depth), :lanes], big_turn[r, pl.ds(own, depth), lanes:]
-                work[r, k, 0], work[r, k, 1] = turned(done[:depth, at], done[depth:, at], gc, gs)
-
-    numerator = jnp.zeros((lanes, lanes), exact)
-    curvature = jnp.zeros((lanes, lanes), exact)
+    highs, lows = zip(*(split(x) for x in fields))
+    highs, lows = jnp.concatenate(highs, 0), jnp.concatenate(lows, 0)
+    section = times(jnp.concatenate([highs, lows], 1), twice_high) + times(highs, wide_low)
+    out = []
+    for j in range(0, len(fields), 2):
+        columns = []
+        for i in (j, j + 1):
+            here = slice(i * lanes, (i + 1) * lanes)
+            columns.append(stacked(*turned(section[here, :lanes], section[here, lanes:], *w), 0))
+        done = left_product(block, columns)
+        for i in range(2):
+            here, r = slice(i * lanes, (i + 1) * lanes), at[j + i]
+            gc, gs = big_turn[r, pl.ds(own, depth), :lanes], big_turn[r, pl.ds(own, depth), lanes:]
+            out.append(turned(done[:depth, here], done[depth:, here], gc, gs))
+    return out
+
+
+def whole_noise(target, held, other):
+    share = lanes // 2
+    side = lax.rem(lax.axis_index("probe"), 2) * share
+    target[pl.ds(pl.multiple_of(side, share), share)] = held[held.shape[0] - share :]
+    target[pl.ds(pl.multiple_of(share - side, share), share)] = other[...]
+
+
+def images(slots, signs, noises, precond, circulant, image, sums):
+    me = lax.axis_index("seq")
+    fields = []
+    numerator, curvature = sums
+    for k, j in enumerate(slots):
+        p = precond[me ^ j]
+        noisy = noises[k][...] * p
+        ki = circulant[me ^ j] + noisy
+        image[k] = ki
+        fields.append(noisy)
+        numerator += folded(signs[k][:lanes] * p)
+        curvature += folded(p * ki)
+    return fields, (numerator, curvature)
+
+
+def near_kernel(rows, *refs):
+    n = rows - 2
+    blocks, others = refs[:n], refs[n : n + 2]
+    precond, circulant, left, dft, turns, big_turn, image, noise, found, sums = refs[n + 2 :]
+    share = lanes // 2
+    for j in range(2):
+        noise[j] = blocks[j][blocks[j].shape[0] - lanes :]
+    for j in range(2, n):
+        whole_noise(noise.at[j], blocks[j], others[j % 2].at[(j - 2) // 2 * share : j // 2 * share])
+    zero = jnp.zeros((lead, lanes), exact)
+    noises = [noise.at[j] for j in range(n)]
+    fields, totals = images(range(n), blocks, noises, precond, circulant, image, (zero, zero))
+    sums[0], sums[1] = totals
+    at = [lax.axis_index("seq") ^ j for j in range(n)]
+    for j, x in enumerate(own_spectra(fields, at, left, dft, turns, big_turn)):
+        found[j, 0], found[j, 1] = x
+
+
+def adjoint_kernel(rows, probes, *refs):
+    n = rows - 2
+    signs = [refs[j].at[:lanes] for j in range(rows)]
+    blocks, others = refs[:rows], refs[rows : rows + 2]
+    near_image, near_noise, near_found, near_sums = refs[rows + 2 : rows + 6]
+    refs = refs[rows + 6 :]
+    precond, circulant, spectrum, kernel, symbol, left, dft, turns, big_turn, residual_out = refs[:10]
+    outs = refs[10 : 10 + probes]
+    image, noise, work, shares = refs[10 + probes :]
+    depth = lanes // rows
+    samples = rows * lanes * lanes
+    me = lax.axis_index("seq")
+    own = pl.multiple_of(me * depth, depth)
+    at = [me ^ j for j in range(rows)]
+    for j in range(n):
+        work[at[j], 0, 0], work[at[j], 0, 1] = near_found[j, 0], near_found[j, 1]
+    for k in range(2):
+        whole_noise(noise.at[k], blocks[n + k], others[k])
+    last_noises = [noise.at[k] for k in range(2)]
+    sums = (near_sums[0], near_sums[1])
+    fields, sums = images(range(n, rows), blocks[n:], last_noises, precond, circulant, image, sums)
+    noises = [near_noise.at[j] for j in range(n)] + last_noises
+    image = [near_image.at[j] for j in range(n)] + [image.at[k] for k in range(2)]
+    numerator, curvature = whole_sum(sums[0]), whole_sum(sums[1])
+    for j, x in zip(range(n, rows), own_spectra(fields, at[n:], left, dft, turns, big_turn)):
+        work[at[j], 0, 0], work[at[j], 0, 1] = x
+    step_size = numerator / curvature
+    cross = jnp.zeros((lead, lanes), exact)
     fields = []
     for j in range(rows):
-        p = precond[me ^ j]
-        noisy = noises[j][...] * p
-        ki = circulant[me ^ j] + noisy
-        image[j] = ki
-        fields.append(noisy)
-        numerator += signs[j][...] * p
-        curvature += p * ki
-    numerator, curvature = whole_sum(numerator), whole_sum(curvature)
-    own_spectra(fields, 0)
-    step_size = numerator / curvature
-    cross = jnp.zeros((lanes, lanes), exact)
-    fields = []
-    for j in range(rows):
-        residual = signs[j][...] - step_size * image[j]
-        cross += residual * image[j]
+        residual = signs[j][...] - step_size * image[j][...]
+        cross += folded(residual * image[j][...])
         fields.append(noises[j][...] * residual)
         if j == 0:
             residual_out[...] = residual.T
     weight = -2.0 * whole_sum(cross)
-    own_spectra(fields, 1)
+    for r, x in zip(at, own_spectra(fields, at, left, dft, turns, big_turn)):
+        work[r, 1, 0], work[r, 1, 1] = x
     noisy = small_dft([(work[r, 0, 0], work[r, 0, 1]) for r in range(rows)], -1)
     noisy_residual = small_dft([(work[r, 1, 0], work[r, 1, 1]) for r in range(rows)], -1)
     for a in range(rows):
@@ -390,6 +432,38 @@
 
 def beyond_middle(x):
     return swapped(x, "seq", 4)
+
+
+def adjoint_calls(
+    rows, probes, blocks, noises, precond, circulant, spectrum, kernel, symbols, left, dft, turns, big_turn
+):
+    square = (lanes, lanes)
+    depth, width, n = lanes // rows, rows // probes, rows - 2
+    tables_held = (left, dft, turns, big_turn)
+    near_parts = call(
+        functools.partial(near_kernel, rows),
+        [(n, *square), (n, *square), (n, 2, depth, lanes), (2, lead, lanes)],
+        [],
+        *blocks[:n],
+        *noises[:2],
+        precond,
+        circulant,
+        *tables_held,
+    )
+    return call(
+        functools.partial(adjoint_kernel, rows, probes),
+        [square] + [(depth, width, lanes)] * probes,
+        [(2, *square), (2, *square), (rows, 2, 2, depth, lanes), (rows, depth, lanes)],
+        *blocks,
+        *noises[2:],
+        *near_parts,
+        precond,
+        circulant,
+        spectrum,
+        kernel,
+        symbols,
+        *tables_held,
+    )
 
 
 def gathered_shards(probe_bits, noise_var, kernel_spectrum, symbol, grad_prev):
@@ -451,22 +525,8 @@
     passed_half = next_chip(halves[lanes // 2 :])
     last = after(passed_half, precond)
     noises = [halves, other_core(halves), last, other_core(last)]
-    share = (depth, width, lanes)
-    residual, *parts = call(
-        functools.partial(adjoint_kernel, rows, probes),
-        [square] + [share] * probes,
-        [field, (rows, 2, 2, depth, lanes), (rows, depth, lanes), (rows - 2, *square)],
-        *blocks,
-        *noises,
-        precond,
-        circulant,
-        spectrum,
-        kernel,
-        symbols,
-        left,
-        dft,
-        turns,
-        big_turn,
+    residual, *parts = adjoint_calls(
+        rows, probes, blocks, noises, precond, circulant, spectrum, kernel, symbols, left, dft, turns, big_turn
     )
     arrived = [swapped(parts[d], "probe", d) for d in range(1, probes)]
     total = lax.optimization_barrier(parts[0] + arrived.pop())

time: 34.9 us -> 34.2 us (0.980)
  waiting for transfers between devices: 11.9 us -> 11.2 us
    ppermute x14, waiting for transfers between devices: 11.9 us -> 11.2 us  [swapped(): lax.ppermute(x, axis, [(i, i ^ d) for i in range(lax.axis_size(axis))])]
    pallas_call x3 -> x4, Pallas kernels: 5.65 us -> 5.62 us  [call(): pl.pallas_call(kernel, out_shape=shapes, in_specs=[whole] * len(operands)...]
  transfers between devices with their start and end apart: 14 -> 14, of which waited for: 7 -> 7; matrix products, arithmetic and copies ran while one was open for 2% -> 2% of each run, Pallas kernels for 10% -> 13%
where the time goes in v5:
time: 34.2 us; the launch traced here: 34.1 us
  starting transfers between devices  14 us (41%)
  waiting for transfers between devices  11.2 us (33%)
  Pallas kernels  6.83 us (20%)
  between operations  0.7 us (2%)
  local copies, waits for them, and re-layouts  0.65 us (2%)
  other arithmetic  0.64 us (2%)
    ppermute x14, starting transfers between devices, swapped(): lax.ppermute(x, axis, [(i, i ^ d) for i in range(lax.axis_size(axis))])  14 us
    ppermute x14, waiting for transfers between devices, swapped(): lax.ppermute(x, axis, [(i, i ^ d) for i in range(lax.axis_size(axis))])  11.2 us
    pallas_call x4, Pallas kernels, call(): pl.pallas_call(kernel, out_shape=shapes, in_specs=[whole] * len(operands)...  5.62 us
    pallas_call x1, Pallas kernels, gathered_shards(): pl.pallas_call(functools.partial(pack_kernel, half, first), out_shape=(pl...  1.21 us
  transfers between devices with their start and end apart: 14, of which 7 were waited for; matrix products, arithmetic and copies ran while one was open for 2% of the time, Pallas kernels for 13%

profile of v5, /device:TPU:0, one launch (start us, length us, event | category | flops | bytes accessed | tf_op | source)
XLA Modules:
  0.0 34.1 jit_solution(9919677738940100622)
XLA Ops:
  0.6 1.2 %shard_map.86 = (f32[392,128]{1,0:T(8,128)S(1)}, f32[328,128]{1,0:T(8,128)S(1)}, bf16[4,128,128]{2,1,0:T(8,128)(2,1)S(1)}, f32[2,128,256]{2,1,0:T(8,128)S(1)}) custom-call(s32[128,128]{1,0:T(8,128)} %bitcast.32, f32[128,128]{1,0:T(8,128)} %bitcast.33, f32[16,8,128]{2,1,0:T(8,128)} %bitcast.28, f32[16,8,128]{2,1,0:T(8,128)} %bitcast.30, ...), custom_call_target="tpu_custom_call" | custom-call | tf_op jit(solution)/shard_map/pallas_call | solution.py:479
  1.8 4.1 %collective-permute-start.2 = (f32[328,128]{1,0:T(8,128)S(1)}, f32[328,128]{1,0:T(8,128)S(1)}, u32[]{:S(2)}, u32[]{:S(2)}) collective-permute-start(f32[328,128]{1,0:T(8,128)S(1)} %get-tuple-element.26), channel_id=1, source_target_pairs={{0,4},{1,5},{2,6},{3,7},{4,0},{5,1},{6,2},{7,3},{8,12},{9,13},{10,... | collective-permute-start | bytes 503816 | tf_op jit(solution)/shard_map/ppermute | solution.py:410
  5.9 1.6 %collective-permute-start.1 = (f32[328,128]{1,0:T(8,128)S(1)}, f32[328,128]{1,0:T(8,128)S(1)}, u32[]{:S(2)}, u32[]{:S(2)}) collective-permute-start(f32[328,128]{1,0:T(8,128)S(1)} %get-tuple-element.26), channel_id=1, source_target_pairs={{0,2},{1,3},{2,0},{3,1},{4,6},{5,7},{6,4},{7,5},{8,10},{9,11},{10,... | collective-permute-start | bytes 503816 | tf_op jit(solution)/shard_map/ppermute | solution.py:410
  7.5 0.0 collective-permute-start
  7.5 6.4 %collective-permute-done.2.refs_3_.refs_4_ = f32[328,128]{1,0:T(8,128)S(1)} collective-permute-done((f32[328,128]{1,0:T(8,128)S(1)}, f32[328,128]{1,0:T(8,128)S(1)}, u32[]{:S(2)}, u32[]{:S(2)}) %collective-permute-start.2) | collective-permute-done | bytes 167968 | tf_op jit(solution)/shard_map/ppermute | solution.py:410
  13.9 0.6 %collective-permute-start.5 = (f32[328,128]{1,0:T(8,128)S(1)}, f32[328,128]{1,0:T(8,128)S(1)}, u32[]{:S(2)}, u32[]{:S(2)}) collective-permute-start(f32[328,128]{1,0:T(8,128)S(1)} %collective-permute-done.2.refs_3_.refs_4_), channel_id=1, source_target_pairs={{0,2},{1,3},{2,0},{3,1},{4,6},{5,7},{6,4},{7,5},{8,10},{9,11},{10,... | collective-permute-start | bytes 503816 | tf_op jit(solution)/shard_map/ppermute | solution.py:410
  14.6 0.0 collective-permute-done.1.refs_2_
  14.6 1.6 %collective-permute-start.6 = (f32[128,128]{1,0:T(8,128)S(1)}, f32[128,128]{1,0:T(8,128)S(1)}, u32[]{:S(2)}, u32[]{:S(2)}) collective-permute-start(f32[128,128]{1,0:T(8,128)S(1)} %pad_maximum_fusion), channel_id=1, source_target_pairs={{0,8},{8,0},{16,24},{24,16},{1,9},{9,1},{17,25},{25,17},{2,10},{10... | collective-permute-start | bytes 196616 | tf_op jit(solution)/shard_map/ppermute | solution.py:410
  16.1 0.0 collective-permute-done.refs_1_
  16.1 0.6 %shard_map.87 = (f32[4,2,128,128]{3,2,1,0:T(8,128)S(1)}, bf16[512,256]{1,0:T(8,128)(2,1)S(1)}, f32[8,128,256]{2,1,0:T(8,128)S(1)}) custom-call(f32[392,128]{1,0:T(8,128)S(1)} %get-tuple-element.25.refs_0_, f32[392,128]{1,0:T(8,128)S(1)} %collective-permute-done.refs_1_, f32[328,128]{1,0:T(8,128)S(1)} %collective-permute-done.1.refs_2_, ...), custom_call_target="tpu_custom_call" | custom-call | tf_op jit(solution)/shard_map/pallas_call | solution.py:398
  16.8 0.1 collective-permute-start.3
  16.9 0.5 %collective-permute-start.4 = (f32[328,128]{1,0:T(8,128)S(1)}, f32[328,128]{1,0:T(8,128)S(1)}, u32[]{:S(2)}, u32[]{:S(2)}) collective-permute-start(f32[328,128]{1,0:T(8,128)S(1)} %collective-permute-done.2.refs_3_.refs_4_), channel_id=1, source_target_pairs={{0,1},{1,0},{2,3},{3,2},{4,5},{5,4},{6,7},{7,6},{8,9},{9,8},{10,11... | collective-permute-start | bytes 503816 | tf_op jit(solution)/shard_map/ppermute | solution.py:410
  17.4 1.5 %collective-permute-done.6.refs_6_ = f32[128,128]{1,0:T(8,128)S(1)} collective-permute-done((f32[128,128]{1,0:T(8,128)S(1)}, f32[128,128]{1,0:T(8,128)S(1)}, u32[]{:S(2)}, u32[]{:S(2)}) %collective-permute-start.6) | collective-permute-done | bytes 65568 | tf_op jit(solution)/shard_map/ppermute | solution.py:410
  18.9 0.4 %collective-permute-done.5.refs_6_ = f32[328,128]{1,0:T(8,128)S(1)} collective-permute-done((f32[328,128]{1,0:T(8,128)S(1)}, f32[328,128]{1,0:T(8,128)S(1)}, u32[]{:S(2)}, u32[]{:S(2)}) %collective-permute-start.5) | collective-permute-done | bytes 167968 | tf_op jit(solution)/shard_map/ppermute | solution.py:410
  19.3 0.0 collective-permute-start.7
  19.3 1.5 %collective-permute-start.8 = (f32[64,128]{1,0:T(8,128)S(1)}, f32[64,128]{1,0:T(8,128)S(1)}, u32[]{:S(2)}, u32[]{:S(2)}) collective-permute-start(f32[64,128]{1,0:T(8,128)S(1)} %slice.14), channel_id=1, source_target_pairs={{0,2},{1,3},{2,0},{3,1},{4,6},{5,7},{6,4},{7,5},{8,10},{9,11},{10,... | collective-permute-start | bytes 98312 | tf_op jit(solution)/shard_map/ppermute | solution.py:410
  20.8 0.2 collective-permute-start.10
  21.0 0.0 collective-permute-done.3.refs_3_
  21.0 0.0 collective-permute-done.4.refs_5_
  21.0 0.0 collective-permute-done.7.refs_7_
  21.0 3.0 %shard_map.88 = (f32[8,2,128,128]{3,2,1,0:T(8,128)S(1)}, f32[8,128,128]{2,1,0:T(8,128)S(1)}, f32[8,128,128]{2,1,0:T(8,128)S(1)}) custom-call(f32[392,128]{1,0:T(8,128)S(1)} %get-tuple-element.25.refs_0_, f32[392,128]{1,0:T(8,128)S(1)} %collective-permute-done.refs_1_, f32[328,128]{1,0:T(8,128)S(1)} %collective-permute-done.1.refs_2_, ...), custom_call_target="tpu_custom_call" | custom-call | tf_op jit(solution)/shard_map/pallas_call | solution.py:398
  24.0 0.0 collective-permute-done.8.refs_8_
  24.0 0.3 %collective-permute-start.9 = (f32[64,128]{1,0:T(8,128)S(1)}, f32[64,128]{1,0:T(8,128)S(1)}, u32[]{:S(2)}, u32[]{:S(2)}) collective-permute-start(f32[64,128]{1,0:T(8,128)S(1)} %collective-permute-done.8.refs_8_), channel_id=1, source_target_pairs={{0,1},{1,0},{2,3},{3,2},{4,5},{5,4},{6,7},{7,6},{8,9},{9,8},{10,11... | collective-permute-start | bytes 98312 | tf_op jit(solution)/shard_map/ppermute | solution.py:410
  24.4 0.0 collective-permute-done.10.refs_7_
  24.4 0.0 copy-start
  24.4 0.0 copy-start.1
  24.4 0.7 %shard_map.89 = (f32[6,128,128]{2,1,0:T(8,128)S(1)}, f32[6,128,128]{2,1,0:T(8,128)S(1)}, f32[6,2,16,128]{3,2,1,0:T(8,128)S(1)}, f32[2,8,128]{2,1,0:T(8,128)S(1)}) custom-call(f32[392,128]{1,0:T(8,128)S(1)} %get-tuple-element.25.refs_0_, f32[392,128]{1,0:T(8,128)S(1)} %collective-permute-done.refs_1_, f32[328,128]{1,0:T(8,128)S(1)} %collective-permute-done.1.refs_2_, ...), custom_call_target="tpu_custom_call" | custom-call | tf_op jit(solution)/shard_map/pallas_call | solution.py:398
  25.1 0.3 collective-permute-done.9.refs_9_
  25.3 0.0 copy-done
  25.3 0.0 copy-done.1
  25.3 1.3 %shard_map.90 = (f32[128,128]{1,0:T(8,128)S(1)}, f32[16,2,128]{2,1,0:T(2,128)S(1)}, f32[16,2,128]{2,1,0:T(2,128)S(1)}, f32[16,2,128]{2,1,0:T(2,128)S(1)}, f32[16,2,128]{2,1,0:T(2,128)S(1)}) custom-call(f32[392,128]{1,0:T(8,128)S(1)} %get-tuple-element.25.refs_0_, f32[392,128]{1,0:T(8,128)S(1)} %collective-permute-done.refs_1_, ...), custom_call_target="tpu_custom_call" | custom-call | tf_op jit(solution)/shard_map/pallas_call | solution.py:398
  26.6 2.5 %collective-permute-start.11 = (f32[16,2,128]{2,1,0:T(2,128)S(1)}, f32[16,2,128]{2,1,0:T(2,128)S(1)}, u32[]{:S(2)}, u32[]{:S(2)}) collective-permute-start(f32[16,2,128]{2,1,0:T(2,128)S(1)} %get-tuple-element.45), channel_id=1, source_target_pairs={{0,24},{8,16},{16,8},{24,0},{1,25},{9,17},{17,9},{25,1},{2,26},{10... | collective-permute-start | bytes 49160 | tf_op jit(solution)/shard_map/ppermute | solution.py:410
  29.2 0.5 %collective-permute-start.12 = (f32[16,2,128]{2,1,0:T(2,128)S(1)}, f32[16,2,128]{2,1,0:T(2,128)S(1)}, u32[]{:S(2)}, u32[]{:S(2)}) collective-permute-start(f32[16,2,128]{2,1,0:T(2,128)S(1)} %get-tuple-element.46), channel_id=1, source_target_pairs={{0,8},{8,0},{16,24},{24,16},{1,9},{9,1},{17,25},{25,17},{2,10},{10... | collective-permute-start | bytes 49160 | tf_op jit(solution)/shard_map/ppermute | solution.py:410
  29.7 0.5 %collective-permute-start.13 = (f32[16,2,128]{2,1,0:T(2,128)S(1)}, f32[16,2,128]{2,1,0:T(2,128)S(1)}, u32[]{:S(2)}, u32[]{:S(2)}) collective-permute-start(f32[16,2,128]{2,1,0:T(2,128)S(1)} %get-tuple-element.47), channel_id=1, source_target_pairs={{0,16},{8,24},{16,0},{24,8},{1,17},{9,25},{17,1},{25,9},{2,18},{10... | collective-permute-start | bytes 49160 | tf_op jit(solution)/shard_map/ppermute | solution.py:410
  30.2 0.6 %copy.9 = f32[1,1,16384]{2,1,0:T(1,128)} copy(f32[1,1,16384]{2,1,0:T(1,128)S(1)} %bitcast.27) | data formatting | bytes 131072
  30.8 0.5 %collective-permute-done.11 = f32[16,2,128]{2,1,0:T(2,128)S(1)} collective-permute-done((f32[16,2,128]{2,1,0:T(2,128)S(1)}, f32[16,2,128]{2,1,0:T(2,128)S(1)}, u32[]{:S(2)}, u32[]{:S(2)}) %collective-permute-start.11) | collective-permute-done | bytes 16416 | tf_op jit(solution)/shard_map/ppermute | solution.py:410
  31.3 0.0 copy-start.2
  31.4 1.5 %collective-permute-done.12 = f32[16,2,128]{2,1,0:T(2,128)S(1)} collective-permute-done((f32[16,2,128]{2,1,0:T(2,128)S(1)}, f32[16,2,128]{2,1,0:T(2,128)S(1)}, u32[]{:S(2)}, u32[]{:S(2)}) %collective-permute-start.12) | collective-permute-done | bytes 16416 | tf_op jit(solution)/shard_map/ppermute | solution.py:410
  32.9 0.5 %collective-permute-done.13 = f32[16,2,128]{2,1,0:T(2,128)S(1)} collective-permute-done((f32[16,2,128]{2,1,0:T(2,128)S(1)}, f32[16,2,128]{2,1,0:T(2,128)S(1)}, u32[]{:S(2)}, u32[]{:S(2)}) %collective-permute-start.13) | collective-permute-done | bytes 16416 | tf_op jit(solution)/shard_map/ppermute | solution.py:410
  33.4 0.0 copy-done.2
  33.4 0.6 %fusion = f32[2048,2]{0,1:T(2,128)} fusion(f32[2048,2]{0,1:T(2,128)S(1)} %copy-done.2, f32[16,2,128]{2,1,0:T(2,128)S(1)} %collective-permute-done.13, f32[16,2,128]{2,1,0:T(2,128)S(1)} %add.12, f32[16,2,128]{2,1,0:T(2,128)S(1)} %collective-permute-done.12), kind=kLoop, calls=%fused_computation.2 | loop fusion | flops 16384 | bytes 81920 | tf_op jit(solution)/shard_map/transpose | solution.py:534
  (5 shorter events, 0.0 us)
Async XLA Ops:
  1.8 12.1 %collective-permute-start.2 = (f32[328,128]{1,0:T(8,128)S(1)}, f32[328,128]{1,0:T(8,128)S(1)}, u32[]{:S(2)}, u32[]{:S(2)}) collective-permute-start(f32[328,128]{1,0:T(8,128)S(1)} %get-tuple-element.26), channel_id=1, source_target_pairs={{0,4},{1,5},{2,6},{3,7},{4,0},{5,1},{6,2},{7,3},{8,12},{9,13},{10,... | collective-permute-start | bytes 503816 | tf_op jit(solution)/shard_map/ppermute | solution.py:410
  5.9 8.6 %collective-permute-start.1 = (f32[328,128]{1,0:T(8,128)S(1)}, f32[328,128]{1,0:T(8,128)S(1)}, u32[]{:S(2)}, u32[]{:S(2)}) collective-permute-start(f32[328,128]{1,0:T(8,128)S(1)} %get-tuple-element.26), channel_id=1, source_target_pairs={{0,2},{1,3},{2,0},{3,1},{4,6},{5,7},{6,4},{7,5},{8,10},{9,11},{10,... | collective-permute-start | bytes 503816 | tf_op jit(solution)/shard_map/ppermute | solution.py:410
  7.5 8.6 %collective-permute-start = (f32[392,128]{1,0:T(8,128)S(1)}, f32[392,128]{1,0:T(8,128)S(1)}, u32[]{:S(2)}, u32[]{:S(2)}) collective-permute-start(f32[392,128]{1,0:T(8,128)S(1)} %get-tuple-element.25.refs_0_), channel_id=1, source_target_pairs={{0,1},{1,0},{2,3},{3,2},{4,5},{5,4},{6,7},{7,6},{8,9},{9,8},{10,11... | collective-permute-start | bytes 602120 | tf_op jit(solution)/shard_map/ppermute | solution.py:410
  13.9 5.4 %collective-permute-start.5 = (f32[328,128]{1,0:T(8,128)S(1)}, f32[328,128]{1,0:T(8,128)S(1)}, u32[]{:S(2)}, u32[]{:S(2)}) collective-permute-start(f32[328,128]{1,0:T(8,128)S(1)} %collective-permute-done.2.refs_3_.refs_4_), channel_id=1, source_target_pairs={{0,2},{1,3},{2,0},{3,1},{4,6},{5,7},{6,4},{7,5},{8,10},{9,11},{10,... | collective-permute-start | bytes 503816 | tf_op jit(solution)/shard_map/ppermute | solution.py:410
  14.6 4.3 %collective-permute-start.6 = (f32[128,128]{1,0:T(8,128)S(1)}, f32[128,128]{1,0:T(8,128)S(1)}, u32[]{:S(2)}, u32[]{:S(2)}) collective-permute-start(f32[128,128]{1,0:T(8,128)S(1)} %pad_maximum_fusion), channel_id=1, source_target_pairs={{0,8},{8,0},{16,24},{24,16},{1,9},{9,1},{17,25},{25,17},{2,10},{10... | collective-permute-start | bytes 196616 | tf_op jit(solution)/shard_map/ppermute | solution.py:410
  16.8 4.2 %collective-permute-start.3 = (f32[328,128]{1,0:T(8,128)S(1)}, f32[328,128]{1,0:T(8,128)S(1)}, u32[]{:S(2)}, u32[]{:S(2)}) collective-permute-start(f32[328,128]{1,0:T(8,128)S(1)} %collective-permute-done.1.refs_2_), channel_id=1, source_target_pairs={{0,1},{1,0},{2,3},{3,2},{4,5},{5,4},{6,7},{7,6},{8,9},{9,8},{10,11... | collective-permute-start | bytes 503816 | tf_op jit(solution)/shard_map/ppermute | solution.py:410
  16.9 4.1 %collective-permute-start.4 = (f32[328,128]{1,0:T(8,128)S(1)}, f32[328,128]{1,0:T(8,128)S(1)}, u32[]{:S(2)}, u32[]{:S(2)}) collective-permute-start(f32[328,128]{1,0:T(8,128)S(1)} %collective-permute-done.2.refs_3_.refs_4_), channel_id=1, source_target_pairs={{0,1},{1,0},{2,3},{3,2},{4,5},{5,4},{6,7},{7,6},{8,9},{9,8},{10,11... | collective-permute-start | bytes 503816 | tf_op jit(solution)/shard_map/ppermute | solution.py:410
  19.3 1.7 %collective-permute-start.7 = (f32[328,128]{1,0:T(8,128)S(1)}, f32[328,128]{1,0:T(8,128)S(1)}, u32[]{:S(2)}, u32[]{:S(2)}) collective-permute-start(f32[328,128]{1,0:T(8,128)S(1)} %collective-permute-done.5.refs_6_), channel_id=1, source_target_pairs={{0,1},{1,0},{2,3},{3,2},{4,5},{5,4},{6,7},{7,6},{8,9},{9,8},{10,11... | collective-permute-start | bytes 503816 | tf_op jit(solution)/shard_map/ppermute | solution.py:410
  19.3 4.7 %collective-permute-start.8 = (f32[64,128]{1,0:T(8,128)S(1)}, f32[64,128]{1,0:T(8,128)S(1)}, u32[]{:S(2)}, u32[]{:S(2)}) collective-permute-start(f32[64,128]{1,0:T(8,128)S(1)} %slice.14), channel_id=1, source_target_pairs={{0,2},{1,3},{2,0},{3,1},{4,6},{5,7},{6,4},{7,5},{8,10},{9,11},{10,... | collective-permute-start | bytes 98312 | tf_op jit(solution)/shard_map/ppermute | solution.py:410
  20.8 3.6 %collective-permute-start.10 = (f32[128,128]{1,0:T(8,128)S(1)}, f32[128,128]{1,0:T(8,128)S(1)}, u32[]{:S(2)}, u32[]{:S(2)}) collective-permute-start(f32[128,128]{1,0:T(8,128)S(1)} %collective-permute-done.6.refs_6_), channel_id=1, source_target_pairs={{0,1},{1,0},{2,3},{3,2},{4,5},{5,4},{6,7},{7,6},{8,9},{9,8},{10,11... | collective-permute-start | bytes 196616 | tf_op jit(solution)/shard_map/ppermute | solution.py:410
  24.0 1.3 %collective-permute-start.9 = (f32[64,128]{1,0:T(8,128)S(1)}, f32[64,128]{1,0:T(8,128)S(1)}, u32[]{:S(2)}, u32[]{:S(2)}) collective-permute-start(f32[64,128]{1,0:T(8,128)S(1)} %collective-permute-done.8.refs_8_), channel_id=1, source_target_pairs={{0,1},{1,0},{2,3},{3,2},{4,5},{5,4},{6,7},{7,6},{8,9},{9,8},{10,11... | collective-permute-start | bytes 98312 | tf_op jit(solution)/shard_map/ppermute | solution.py:410
  24.4 0.9 %copy-start = (f32[2048,8]{0,1:T(8,128)S(1)}, f32[2048,8]{0,1:T(8,128)}, u32[]{:S(2)}) copy-start(f32[2048,8]{0,1:T(8,128)} %param.9) | copy-start | bytes 196612
  24.4 0.9 %copy-start.1 = (f32[2048,8]{0,1:T(8,128)S(1)}, f32[2048,8]{0,1:T(8,128)}, u32[]{:S(2)}) copy-start(f32[2048,8]{0,1:T(8,128)} %param.10) | copy-start | bytes 196612
  26.6 4.7 %collective-permute-start.11 = (f32[16,2,128]{2,1,0:T(2,128)S(1)}, f32[16,2,128]{2,1,0:T(2,128)S(1)}, u32[]{:S(2)}, u32[]{:S(2)}) collective-permute-start(f32[16,2,128]{2,1,0:T(2,128)S(1)} %get-tuple-element.45), channel_id=1, source_target_pairs={{0,24},{8,16},{16,8},{24,0},{1,25},{9,17},{17,9},{25,1},{2,26},{10... | collective-permute-start | bytes 49160 | tf_op jit(solution)/shard_map/ppermute | solution.py:410
  29.2 3.7 %collective-permute-start.12 = (f32[16,2,128]{2,1,0:T(2,128)S(1)}, f32[16,2,128]{2,1,0:T(2,128)S(1)}, u32[]{:S(2)}, u32[]{:S(2)}) collective-permute-start(f32[16,2,128]{2,1,0:T(2,128)S(1)} %get-tuple-element.46), channel_id=1, source_target_pairs={{0,8},{8,0},{16,24},{24,16},{1,9},{9,1},{17,25},{25,17},{2,10},{10... | collective-permute-start | bytes 49160 | tf_op jit(solution)/shard_map/ppermute | solution.py:410
  29.7 3.7 %collective-permute-start.13 = (f32[16,2,128]{2,1,0:T(2,128)S(1)}, f32[16,2,128]{2,1,0:T(2,128)S(1)}, u32[]{:S(2)}, u32[]{:S(2)}) collective-permute-start(f32[16,2,128]{2,1,0:T(2,128)S(1)} %get-tuple-element.47), channel_id=1, source_target_pairs={{0,16},{8,24},{16,0},{24,8},{1,17},{9,25},{17,1},{25,9},{2,18},{10... | collective-permute-start | bytes 49160 | tf_op jit(solution)/shard_map/ppermute | solution.py:410
  31.3 2.1 %copy-start.2 = (f32[2048,2]{0,1:T(2,128)S(1)}, f32[2048,2]{0,1:T(2,128)}, u32[]{:S(2)}) copy-start(f32[2048,2]{0,1:T(2,128)} %param.11) | copy-start | bytes 49156

commit v6 on v5

--- a/solution.py
+++ b/solution.py
@@ -202,11 +202,9 @@
     at = [me ^ j for j in late]
     for r, x in zip(at, row_spectra([blocks[j] for j in late], at, sign_table(dft), left, w, big_turn)):
         work[r, 0, 0], work[r, 0, 1] = x
-    for t in range(0, lanes, lead):
-        at = slice(t, t + lead)
-        out = small_dft([(work[r, 0, 0, at], work[r, 0, 1, at]) for r in range(rows)], -1)
-        for a in range(rows):
-            spectrum[a, 0, at], spectrum[a, 1, at] = out[a]
+    own = pl.ds(pl.multiple_of(me * depth, depth), depth)
+    for a, x in enumerate(small_dft([(work[r, 0, 0, own], work[r, 0, 1, own]) for r in range(rows)], -1)):
+        spectrum[a, 0], spectrum[a, 1] = x
     for j in range(rows):
         place = pl.multiple_of((me ^ j) * depth, depth)
         for a in range(half):
@@ -215,10 +213,12 @@
             at += half * depth
             symbol[a, pl.ds(place, depth)] = blocks[j][at : at + depth]
         ends[me ^ j] = blocks[j][lanes + 2 * half * depth : lanes + 2 * half * depth + lead]
-    middle = spectrum[half, 0, 0:1, 0:1] / ends[0, 1:2, 0:1] / samples
+    middle = sum((-1.0) ** r * work[r, 0, 0, 0:1, 0:1] for r in range(rows))
+    middle = middle / ends[0, 1:2, 0:1] / samples
     middle_image = middle * ends[0, 0:1, 0:1]
     for t in range(0, lanes, lead):
         at = slice(t, t + lead)
+        lower = small_dft([(work[r, 0, 0, at], work[r, 0, 1, at]) for r in range(rows)], -1)[:half]
         first, second = [], []
         for a in range(half):
             scale = 2.0 / samples / symbol[a, at]
@@ -227,7 +227,7 @@
                     lax.broadcasted_iota(jnp.int32, (lead, lanes), 1) == 0
                 )
                 scale = jnp.where(zero, 0.5 * scale, scale)
-            re, im = spectrum[a, 0, at] * scale, spectrum[a, 1, at] * scale
+            re, im = lower[a][0] * scale, lower[a][1] * scale
             first.append((re, im))
             second.append((re * kernel[a, at], im * kernel[a, at]))
         for field, entries in enumerate((first, second)):
@@ -347,7 +347,7 @@
     for j in range(n):
         work[at[j], 0, 0], work[at[j], 0, 1] = near_found[j, 0], near_found[j, 1]
     for k in range(2):
-        whole_noise(noise.at[k], blocks[n + k], others[k])
+        whole_noise(noise.at[k], others[k].at[: lanes // 2], others[k].at[lanes // 2 :])
     last_noises = [noise.at[k] for k in range(2)]
     sums = (near_sums[0], near_sums[1])
     fields, sums = images(range(n, rows), blocks[n:], last_noises, precond, circulant, image, sums)
@@ -374,7 +374,7 @@
         k, s = kernel[:, a], symbol[:, a]
         total = 0.0
         for part in range(2):
-            base = spectrum[a, part, pl.ds(own, depth)]
+            base = spectrum[a, part]
             ki = k * (base / s) + noisy[a][part]
             applied = k * (base - step_size * ki) + noisy_residual[a][part]
             adjoint = (
@@ -496,7 +496,7 @@
     )(probe_bits.reshape(square), noise_var.reshape(square), kernel, symbols, dft, turns)
     far = beyond_middle(sent)
     neighbour = next_chip(sent)
-    passed_on = next_chip(far)
+    passed_on = next_chip(far[:first])
     early = [block, other_core(block), neighbour, far]
     found, left, big_turn = call(
         functools.partial(early_kernel, rows),
@@ -513,7 +513,7 @@
     field = (rows, *square)
     spectrum, precond, circulant = call(
         functools.partial(inverse_kernel, rows),
-        [(rows, 2, *square), field, field],
+        [(rows, 2, depth, lanes), field, field],
         [(half, *square), (half, *square), (rows, lead, lanes), (rows, 2, 2, *square)],
         *blocks,
         found,
@@ -522,8 +522,8 @@
         turns,
         big_turn,
     )
-    passed_half = next_chip(halves[lanes // 2 :])
-    last = after(passed_half, precond)
+    passed_noise = next_chip(jnp.concatenate([far[first:], halves[lanes // 2 :]], 0))
+    last = after(passed_noise, precond)
     noises = [halves, other_core(halves), last, other_core(last)]
     residual, *parts = adjoint_calls(
         rows, probes, blocks, noises, precond, circulant, spectrum, kernel, symbols, left, dft, turns, big_turn

time: 34.2 us -> 34 us (level)
    ppermute x14, waiting for transfers between devices: 11.2 us -> 10.9 us  [swapped(): lax.ppermute(x, axis, [(i, i ^ d) for i in range(lax.axis_size(axis))])]
  transfers between devices with their start and end apart: 14 -> 14, of which waited for: 7 -> 6; matrix products, arithmetic and copies ran while one was open for 2% -> 2% of each run, Pallas kernels for 13% -> 13%
where the time goes in v6:
time: 34 us; the launch traced here: 33.8 us
  starting transfers between devices  14.1 us (41%)
  waiting for transfers between devices  10.9 us (32%)
  Pallas kernels  6.83 us (20%)
  between operations  0.72 us (2%)
  local copies, waits for them, and re-layouts  0.66 us (2%)
  other arithmetic  0.65 us (2%)
    ppermute x14, starting transfers between devices, swapped(): lax.ppermute(x, axis, [(i, i ^ d) for i in range(lax.axis_size(axis))])  14.1 us
    ppermute x14, waiting for transfers between devices, swapped(): lax.ppermute(x, axis, [(i, i ^ d) for i in range(lax.axis_size(axis))])  10.9 us
    pallas_call x4, Pallas kernels, call(): pl.pallas_call(kernel, out_shape=shapes, in_specs=[whole] * len(operands)...  5.62 us
    pallas_call x1, Pallas kernels, gathered_shards(): pl.pallas_call(functools.partial(pack_kernel, half, first), out_shape=(pl...  1.21 us
  transfers between devices with their start and end apart: 14, of which 6 were waited for; matrix products, arithmetic and copies ran while one was open for 2% of the time, Pallas kernels for 13%

profile of v6, /device:TPU:0, one launch (start us, length us, event | category | flops | bytes accessed | tf_op | source)
XLA Modules:
  0.0 33.8 jit_solution(1637065814815631558)
XLA Ops:
  0.6 1.2 %shard_map.86 = (f32[392,128]{1,0:T(8,128)S(1)}, f32[328,128]{1,0:T(8,128)S(1)}, bf16[4,128,128]{2,1,0:T(8,128)(2,1)S(1)}, f32[2,128,256]{2,1,0:T(8,128)S(1)}) custom-call(s32[128,128]{1,0:T(8,128)} %bitcast.32, f32[128,128]{1,0:T(8,128)} %bitcast.33, f32[16,8,128]{2,1,0:T(8,128)} %bitcast.28, f32[16,8,128]{2,1,0:T(8,128)} %bitcast.30, ...), custom_call_target="tpu_custom_call" | custom-call | tf_op jit(solution)/shard_map/pallas_call | solution.py:479
  1.8 4.1 %collective-permute-start.2 = (f32[328,128]{1,0:T(8,128)S(1)}, f32[328,128]{1,0:T(8,128)S(1)}, u32[]{:S(2)}, u32[]{:S(2)}) collective-permute-start(f32[328,128]{1,0:T(8,128)S(1)} %get-tuple-element.26), channel_id=1, source_target_pairs={{0,4},{1,5},{2,6},{3,7},{4,0},{5,1},{6,2},{7,3},{8,12},{9,13},{10,... | collective-permute-start | bytes 503816 | tf_op jit(solution)/shard_map/ppermute | solution.py:410
  5.9 1.6 %collective-permute-start.1 = (f32[328,128]{1,0:T(8,128)S(1)}, f32[328,128]{1,0:T(8,128)S(1)}, u32[]{:S(2)}, u32[]{:S(2)}) collective-permute-start(f32[328,128]{1,0:T(8,128)S(1)} %get-tuple-element.26), channel_id=1, source_target_pairs={{0,2},{1,3},{2,0},{3,1},{4,6},{5,7},{6,4},{7,5},{8,10},{9,11},{10,... | collective-permute-start | bytes 503816 | tf_op jit(solution)/shard_map/ppermute | solution.py:410
  7.5 0.0 collective-permute-start
  7.5 6.4 %collective-permute-done.2.refs_3_.refs_4_ = f32[328,128]{1,0:T(8,128)S(1)} collective-permute-done((f32[328,128]{1,0:T(8,128)S(1)}, f32[328,128]{1,0:T(8,128)S(1)}, u32[]{:S(2)}, u32[]{:S(2)}) %collective-permute-start.2) | collective-permute-done | bytes 167968 | tf_op jit(solution)/shard_map/ppermute | solution.py:410
  14.0 0.7 %collective-permute-start.5 = (f32[264,128]{1,0:T(8,128)S(1)}, f32[264,128]{1,0:T(8,128)S(1)}, u32[]{:S(2)}, u32[]{:S(2)}) collective-permute-start(f32[264,128]{1,0:T(8,128)S(1)} %slice.17), channel_id=1, source_target_pairs={{0,2},{1,3},{2,0},{3,1},{4,6},{5,7},{6,4},{7,5},{8,10},{9,11},{10,... | collective-permute-start | bytes 405512 | tf_op jit(solution)/shard_map/ppermute | solution.py:410
  14.6 0.0 collective-permute-done.1.refs_2_
  14.7 1.6 %collective-permute-start.6 = (f32[128,128]{1,0:T(8,128)S(1)}, f32[128,128]{1,0:T(8,128)S(1)}, u32[]{:S(2)}, u32[]{:S(2)}) collective-permute-start(f32[128,128]{1,0:T(8,128)S(1)} %pad_maximum_fusion), channel_id=1, source_target_pairs={{0,8},{8,0},{16,24},{24,16},{1,9},{9,1},{17,25},{25,17},{2,10},{10... | collective-permute-start | bytes 196616 | tf_op jit(solution)/shard_map/ppermute | solution.py:410
  16.2 0.0 collective-permute-done.refs_1_
  16.2 0.7 %shard_map.87 = (f32[4,2,128,128]{3,2,1,0:T(8,128)S(1)}, bf16[512,256]{1,0:T(8,128)(2,1)S(1)}, f32[8,128,256]{2,1,0:T(8,128)S(1)}) custom-call(f32[392,128]{1,0:T(8,128)S(1)} %get-tuple-element.25.refs_0_, f32[392,128]{1,0:T(8,128)S(1)} %collective-permute-done.refs_1_, f32[328,128]{1,0:T(8,128)S(1)} %collective-permute-done.1.refs_2_, ...), custom_call_target="tpu_custom_call" | custom-call | tf_op jit(solution)/shard_map/pallas_call | solution.py:398
  16.9 0.1 collective-permute-start.3
  17.0 0.5 %collective-permute-start.4 = (f32[328,128]{1,0:T(8,128)S(1)}, f32[328,128]{1,0:T(8,128)S(1)}, u32[]{:S(2)}, u32[]{:S(2)}) collective-permute-start(f32[328,128]{1,0:T(8,128)S(1)} %collective-permute-done.2.refs_3_.refs_4_), channel_id=1, source_target_pairs={{0,1},{1,0},{2,3},{3,2},{4,5},{5,4},{6,7},{7,6},{8,9},{9,8},{10,11... | collective-permute-start | bytes 503816 | tf_op jit(solution)/shard_map/ppermute | solution.py:410
  17.5 1.5 %collective-permute-done.6.refs_6_ = f32[128,128]{1,0:T(8,128)S(1)} collective-permute-done((f32[128,128]{1,0:T(8,128)S(1)}, f32[128,128]{1,0:T(8,128)S(1)}, u32[]{:S(2)}, u32[]{:S(2)}) %collective-permute-start.6) | collective-permute-done | bytes 65568 | tf_op jit(solution)/shard_map/ppermute | solution.py:410
  19.0 0.0 collective-permute-done.5.refs_6_
  19.0 0.0 collective-permute-start.7
  19.0 1.5 %collective-permute-start.8 = (f32[128,128]{1,0:T(8,128)S(1)}, f32[128,128]{1,0:T(8,128)S(1)}, u32[]{:S(2)}, u32[]{:S(2)}) collective-permute-start(f32[128,128]{1,0:T(8,128)S(1)} %pad_maximum_fusion.1), channel_id=1, source_target_pairs={{0,2},{1,3},{2,0},{3,1},{4,6},{5,7},{6,4},{7,5},{8,10},{9,11},{10,... | collective-permute-start | bytes 196616 | tf_op jit(solution)/shard_map/ppermute | solution.py:410
  20.5 0.2 collective-permute-start.10
  20.7 0.0 collective-permute-done.3.refs_3_
  20.7 0.0 collective-permute-done.4.refs_5_
  20.7 0.0 collective-permute-done.7.refs_7_
  20.7 3.0 %shard_map.88 = (f32[8,2,16,128]{3,2,1,0:T(8,128)S(1)}, f32[8,128,128]{2,1,0:T(8,128)S(1)}, f32[8,128,128]{2,1,0:T(8,128)S(1)}) custom-call(f32[392,128]{1,0:T(8,128)S(1)} %get-tuple-element.25.refs_0_, f32[392,128]{1,0:T(8,128)S(1)} %collective-permute-done.refs_1_, f32[328,128]{1,0:T(8,128)S(1)} %collective-permute-done.1.refs_2_, ...), custom_call_target="tpu_custom_call" | custom-call | tf_op jit(solution)/shard_map/pallas_call | solution.py:398
  23.6 0.0 collective-permute-done.8.refs_8_
  23.7 0.4 %collective-permute-start.9 = (f32[128,128]{1,0:T(8,128)S(1)}, f32[128,128]{1,0:T(8,128)S(1)}, u32[]{:S(2)}, u32[]{:S(2)}) collective-permute-start(f32[128,128]{1,0:T(8,128)S(1)} %collective-permute-done.8.refs_8_), channel_id=1, source_target_pairs={{0,1},{1,0},{2,3},{3,2},{4,5},{5,4},{6,7},{7,6},{8,9},{9,8},{10,11... | collective-permute-start | bytes 196616 | tf_op jit(solution)/shard_map/ppermute | solution.py:410
  24.1 0.0 collective-permute-done.10.refs_7_
  24.1 0.0 copy-start
  24.1 0.0 copy-start.1
  24.1 0.7 %shard_map.89 = (f32[6,128,128]{2,1,0:T(8,128)S(1)}, f32[6,128,128]{2,1,0:T(8,128)S(1)}, f32[6,2,16,128]{3,2,1,0:T(8,128)S(1)}, f32[2,8,128]{2,1,0:T(8,128)S(1)}) custom-call(f32[392,128]{1,0:T(8,128)S(1)} %get-tuple-element.25.refs_0_, f32[392,128]{1,0:T(8,128)S(1)} %collective-permute-done.refs_1_, f32[328,128]{1,0:T(8,128)S(1)} %collective-permute-done.1.refs_2_, ...), custom_call_target="tpu_custom_call" | custom-call | tf_op jit(solution)/shard_map/pallas_call | solution.py:398
  24.7 0.2 collective-permute-done.9.refs_9_
  25.0 0.0 copy-done
  25.0 0.0 copy-done.1
  25.0 1.3 %shard_map.90 = (f32[128,128]{1,0:T(8,128)S(1)}, f32[16,2,128]{2,1,0:T(2,128)S(1)}, f32[16,2,128]{2,1,0:T(2,128)S(1)}, f32[16,2,128]{2,1,0:T(2,128)S(1)}, f32[16,2,128]{2,1,0:T(2,128)S(1)}) custom-call(f32[392,128]{1,0:T(8,128)S(1)} %get-tuple-element.25.refs_0_, f32[392,128]{1,0:T(8,128)S(1)} %collective-permute-done.refs_1_, ...), custom_call_target="tpu_custom_call" | custom-call | tf_op jit(solution)/shard_map/pallas_call | solution.py:398
  26.3 2.6 %collective-permute-start.11 = (f32[16,2,128]{2,1,0:T(2,128)S(1)}, f32[16,2,128]{2,1,0:T(2,128)S(1)}, u32[]{:S(2)}, u32[]{:S(2)}) collective-permute-start(f32[16,2,128]{2,1,0:T(2,128)S(1)} %get-tuple-element.45), channel_id=1, source_target_pairs={{0,24},{8,16},{16,8},{24,0},{1,25},{9,17},{17,9},{25,1},{2,26},{10... | collective-permute-start | bytes 49160 | tf_op jit(solution)/shard_map/ppermute | solution.py:410
  28.9 0.5 %collective-permute-start.12 = (f32[16,2,128]{2,1,0:T(2,128)S(1)}, f32[16,2,128]{2,1,0:T(2,128)S(1)}, u32[]{:S(2)}, u32[]{:S(2)}) collective-permute-start(f32[16,2,128]{2,1,0:T(2,128)S(1)} %get-tuple-element.46), channel_id=1, source_target_pairs={{0,8},{8,0},{16,24},{24,16},{1,9},{9,1},{17,25},{25,17},{2,10},{10... | collective-permute-start | bytes 49160 | tf_op jit(solution)/shard_map/ppermute | solution.py:410
  29.4 0.5 %collective-permute-start.13 = (f32[16,2,128]{2,1,0:T(2,128)S(1)}, f32[16,2,128]{2,1,0:T(2,128)S(1)}, u32[]{:S(2)}, u32[]{:S(2)}) collective-permute-start(f32[16,2,128]{2,1,0:T(2,128)S(1)} %get-tuple-element.47), channel_id=1, source_target_pairs={{0,16},{8,24},{16,0},{24,8},{1,17},{9,25},{17,1},{25,9},{2,18},{10... | collective-permute-start | bytes 49160 | tf_op jit(solution)/shard_map/ppermute | solution.py:410
  29.9 0.6 %copy.9 = f32[1,1,16384]{2,1,0:T(1,128)} copy(f32[1,1,16384]{2,1,0:T(1,128)S(1)} %bitcast.27) | data formatting | bytes 131072
  30.5 0.5 %collective-permute-done.11 = f32[16,2,128]{2,1,0:T(2,128)S(1)} collective-permute-done((f32[16,2,128]{2,1,0:T(2,128)S(1)}, f32[16,2,128]{2,1,0:T(2,128)S(1)}, u32[]{:S(2)}, u32[]{:S(2)}) %collective-permute-start.11) | collective-permute-done | bytes 16416 | tf_op jit(solution)/shard_map/ppermute | solution.py:410
  31.0 0.0 copy-start.2
  31.1 1.6 %collective-permute-done.12 = f32[16,2,128]{2,1,0:T(2,128)S(1)} collective-permute-done((f32[16,2,128]{2,1,0:T(2,128)S(1)}, f32[16,2,128]{2,1,0:T(2,128)S(1)}, u32[]{:S(2)}, u32[]{:S(2)}) %collective-permute-start.12) | collective-permute-done | bytes 16416 | tf_op jit(solution)/shard_map/ppermute | solution.py:410
  32.6 0.5 %collective-permute-done.13 = f32[16,2,128]{2,1,0:T(2,128)S(1)} collective-permute-done((f32[16,2,128]{2,1,0:T(2,128)S(1)}, f32[16,2,128]{2,1,0:T(2,128)S(1)}, u32[]{:S(2)}, u32[]{:S(2)}) %collective-permute-start.13) | collective-permute-done | bytes 16416 | tf_op jit(solution)/shard_map/ppermute | solution.py:410
  33.2 0.0 copy-done.2
  33.2 0.6 %fusion = f32[2048,2]{0,1:T(2,128)} fusion(f32[2048,2]{0,1:T(2,128)S(1)} %copy-done.2, f32[16,2,128]{2,1,0:T(2,128)S(1)} %collective-permute-done.13, f32[16,2,128]{2,1,0:T(2,128)S(1)} %add.12, f32[16,2,128]{2,1,0:T(2,128)S(1)} %collective-permute-done.12), kind=kLoop, calls=%fused_computation.3 | loop fusion | flops 16384 | bytes 81920 | tf_op jit(solution)/shard_map/transpose | solution.py:534
  (7 shorter events, 0.0 us)
Async XLA Ops:
  1.8 12.1 %collective-permute-start.2 = (f32[328,128]{1,0:T(8,128)S(1)}, f32[328,128]{1,0:T(8,128)S(1)}, u32[]{:S(2)}, u32[]{:S(2)}) collective-permute-start(f32[328,128]{1,0:T(8,128)S(1)} %get-tuple-element.26), channel_id=1, source_target_pairs={{0,4},{1,5},{2,6},{3,7},{4,0},{5,1},{6,2},{7,3},{8,12},{9,13},{10,... | collective-permute-start | bytes 503816 | tf_op jit(solution)/shard_map/ppermute | solution.py:410
  5.9 8.7 %collective-permute-start.1 = (f32[328,128]{1,0:T(8,128)S(1)}, f32[328,128]{1,0:T(8,128)S(1)}, u32[]{:S(2)}, u32[]{:S(2)}) collective-permute-start(f32[328,128]{1,0:T(8,128)S(1)} %get-tuple-element.26), channel_id=1, source_target_pairs={{0,2},{1,3},{2,0},{3,1},{4,6},{5,7},{6,4},{7,5},{8,10},{9,11},{10,... | collective-permute-start | bytes 503816 | tf_op jit(solution)/shard_map/ppermute | solution.py:410
  7.5 8.7 %collective-permute-start = (f32[392,128]{1,0:T(8,128)S(1)}, f32[392,128]{1,0:T(8,128)S(1)}, u32[]{:S(2)}, u32[]{:S(2)}) collective-permute-start(f32[392,128]{1,0:T(8,128)S(1)} %get-tuple-element.25.refs_0_), channel_id=1, source_target_pairs={{0,1},{1,0},{2,3},{3,2},{4,5},{5,4},{6,7},{7,6},{8,9},{9,8},{10,11... | collective-permute-start | bytes 602120 | tf_op jit(solution)/shard_map/ppermute | solution.py:410
  14.0 5.1 %collective-permute-start.5 = (f32[264,128]{1,0:T(8,128)S(1)}, f32[264,128]{1,0:T(8,128)S(1)}, u32[]{:S(2)}, u32[]{:S(2)}) collective-permute-start(f32[264,128]{1,0:T(8,128)S(1)} %slice.17), channel_id=1, source_target_pairs={{0,2},{1,3},{2,0},{3,1},{4,6},{5,7},{6,4},{7,5},{8,10},{9,11},{10,... | collective-permute-start | bytes 405512 | tf_op jit(solution)/shard_map/ppermute | solution.py:410
  14.7 4.3 %collective-permute-start.6 = (f32[128,128]{1,0:T(8,128)S(1)}, f32[128,128]{1,0:T(8,128)S(1)}, u32[]{:S(2)}, u32[]{:S(2)}) collective-permute-start(f32[128,128]{1,0:T(8,128)S(1)} %pad_maximum_fusion), channel_id=1, source_target_pairs={{0,8},{8,0},{16,24},{24,16},{1,9},{9,1},{17,25},{25,17},{2,10},{10... | collective-permute-start | bytes 196616 | tf_op jit(solution)/shard_map/ppermute | solution.py:410
  16.9 3.8 %collective-permute-start.3 = (f32[328,128]{1,0:T(8,128)S(1)}, f32[328,128]{1,0:T(8,128)S(1)}, u32[]{:S(2)}, u32[]{:S(2)}) collective-permute-start(f32[328,128]{1,0:T(8,128)S(1)} %collective-permute-done.1.refs_2_), channel_id=1, source_target_pairs={{0,1},{1,0},{2,3},{3,2},{4,5},{5,4},{6,7},{7,6},{8,9},{9,8},{10,11... | collective-permute-start | bytes 503816 | tf_op jit(solution)/shard_map/ppermute | solution.py:410
  17.0 3.7 %collective-permute-start.4 = (f32[328,128]{1,0:T(8,128)S(1)}, f32[328,128]{1,0:T(8,128)S(1)}, u32[]{:S(2)}, u32[]{:S(2)}) collective-permute-start(f32[328,128]{1,0:T(8,128)S(1)} %collective-permute-done.2.refs_3_.refs_4_), channel_id=1, source_target_pairs={{0,1},{1,0},{2,3},{3,2},{4,5},{5,4},{6,7},{7,6},{8,9},{9,8},{10,11... | collective-permute-start | bytes 503816 | tf_op jit(solution)/shard_map/ppermute | solution.py:410
  19.0 1.6 %collective-permute-start.7 = (f32[264,128]{1,0:T(8,128)S(1)}, f32[264,128]{1,0:T(8,128)S(1)}, u32[]{:S(2)}, u32[]{:S(2)}) collective-permute-start(f32[264,128]{1,0:T(8,128)S(1)} %collective-permute-done.5.refs_6_), channel_id=1, source_target_pairs={{0,1},{1,0},{2,3},{3,2},{4,5},{5,4},{6,7},{7,6},{8,9},{9,8},{10,11... | collective-permute-start | bytes 405512 | tf_op jit(solution)/shard_map/ppermute | solution.py:410
  19.0 4.6 %collective-permute-start.8 = (f32[128,128]{1,0:T(8,128)S(1)}, f32[128,128]{1,0:T(8,128)S(1)}, u32[]{:S(2)}, u32[]{:S(2)}) collective-permute-start(f32[128,128]{1,0:T(8,128)S(1)} %pad_maximum_fusion.1), channel_id=1, source_target_pairs={{0,2},{1,3},{2,0},{3,1},{4,6},{5,7},{6,4},{7,5},{8,10},{9,11},{10,... | collective-permute-start | bytes 196616 | tf_op jit(solution)/shard_map/ppermute | solution.py:410
  20.5 3.6 %collective-permute-start.10 = (f32[128,128]{1,0:T(8,128)S(1)}, f32[128,128]{1,0:T(8,128)S(1)}, u32[]{:S(2)}, u32[]{:S(2)}) collective-permute-start(f32[128,128]{1,0:T(8,128)S(1)} %collective-permute-done.6.refs_6_), channel_id=1, source_target_pairs={{0,1},{1,0},{2,3},{3,2},{4,5},{5,4},{6,7},{7,6},{8,9},{9,8},{10,11... | collective-permute-start | bytes 196616 | tf_op jit(solution)/shard_map/ppermute | solution.py:410
  23.7 1.3 %collective-permute-start.9 = (f32[128,128]{1,0:T(8,128)S(1)}, f32[128,128]{1,0:T(8,128)S(1)}, u32[]{:S(2)}, u32[]{:S(2)}) collective-permute-start(f32[128,128]{1,0:T(8,128)S(1)} %collective-permute-done.8.refs_8_), channel_id=1, source_target_pairs={{0,1},{1,0},{2,3},{3,2},{4,5},{5,4},{6,7},{7,6},{8,9},{9,8},{10,11... | collective-permute-start | bytes 196616 | tf_op jit(solution)/shard_map/ppermute | solution.py:410
  24.1 0.9 %copy-start = (f32[2048,8]{0,1:T(8,128)S(1)}, f32[2048,8]{0,1:T(8,128)}, u32[]{:S(2)}) copy-start(f32[2048,8]{0,1:T(8,128)} %param.9) | copy-start | bytes 196612
  24.1 0.9 %copy-start.1 = (f32[2048,8]{0,1:T(8,128)S(1)}, f32[2048,8]{0,1:T(8,128)}, u32[]{:S(2)}) copy-start(f32[2048,8]{0,1:T(8,128)} %param.10) | copy-start | bytes 196612
  26.3 4.7 %collective-permute-start.11 = (f32[16,2,128]{2,1,0:T(2,128)S(1)}, f32[16,2,128]{2,1,0:T(2,128)S(1)}, u32[]{:S(2)}, u32[]{:S(2)}) collective-permute-start(f32[16,2,128]{2,1,0:T(2,128)S(1)} %get-tuple-element.45), channel_id=1, source_target_pairs={{0,24},{8,16},{16,8},{24,0},{1,25},{9,17},{17,9},{25,1},{2,26},{10... | collective-permute-start | bytes 49160 | tf_op jit(solution)/shard_map/ppermute | solution.py:410
  28.9 3.7 %collective-permute-start.12 = (f32[16,2,128]{2,1,0:T(2,128)S(1)}, f32[16,2,128]{2,1,0:T(2,128)S(1)}, u32[]{:S(2)}, u32[]{:S(2)}) collective-permute-start(f32[16,2,128]{2,1,0:T(2,128)S(1)} %get-tuple-element.46), channel_id=1, source_target_pairs={{0,8},{8,0},{16,24},{24,16},{1,9},{9,1},{17,25},{25,17},{2,10},{10... | collective-permute-start | bytes 49160 | tf_op jit(solution)/shard_map/ppermute | solution.py:410
  29.4 3.7 %collective-permute-start.13 = (f32[16,2,128]{2,1,0:T(2,128)S(1)}, f32[16,2,128]{2,1,0:T(2,128)S(1)}, u32[]{:S(2)}, u32[]{:S(2)}) collective-permute-start(f32[16,2,128]{2,1,0:T(2,128)S(1)} %get-tuple-element.47), channel_id=1, source_target_pairs={{0,16},{8,24},{16,0},{24,8},{1,17},{9,25},{17,1},{25,9},{2,18},{10... | collective-permute-start | bytes 49160 | tf_op jit(solution)/shard_map/ppermute | solution.py:410
  31.0 2.1 %copy-start.2 = (f32[2048,2]{0,1:T(2,128)S(1)}, f32[2048,2]{0,1:T(2,128)}, u32[]{:S(2)}) copy-start(f32[2048,2]{0,1:T(2,128)} %param.11) | copy-start | bytes 49156

commit v7 on v6

--- a/solution.py
+++ b/solution.py
@@ -326,7 +326,8 @@
     fields, totals = images(range(n), blocks, noises, precond, circulant, image, (zero, zero))
     sums[0], sums[1] = totals
     at = [lax.axis_index("seq") ^ j for j in range(n)]
-    for j, x in enumerate(own_spectra(fields, at, left, dft, turns, big_turn)):
+    fields += [noises[j][...] * blocks[j][:lanes] for j in range(2)] + [noises[j][...] * image[j] for j in range(2)]
+    for j, x in enumerate(own_spectra(fields, at + at[:2] * 2, left, dft, turns, big_turn)):
         found[j, 0], found[j, 1] = x
 
 
@@ -362,11 +363,15 @@
     for j in range(rows):
         residual = signs[j][...] - step_size * image[j][...]
         cross += folded(residual * image[j][...])
-        fields.append(noises[j][...] * residual)
+        if j >= 2:
+            fields.append(noises[j][...] * residual)
         if j == 0:
             residual_out[...] = residual.T
     weight = -2.0 * whole_sum(cross)
-    for r, x in zip(at, own_spectra(fields, at, left, dft, turns, big_turn)):
+    for j in range(2):
+        for part in range(2):
+            work[at[j], 1, part] = near_found[n + j, part] - step_size * near_found[n + 2 + j, part]
+    for r, x in zip(at[2:], own_spectra(fields, at[2:], left, dft, turns, big_turn)):
         work[r, 1, 0], work[r, 1, 1] = x
     noisy = small_dft([(work[r, 0, 0], work[r, 0, 1]) for r in range(rows)], -1)
     noisy_residual = small_dft([(work[r, 1, 0], work[r, 1, 1]) for r in range(rows)], -1)
@@ -442,7 +447,7 @@
     tables_held = (left, dft, turns, big_turn)
     near_parts = call(
         functools.partial(near_kernel, rows),
-        [(n, *square), (n, *square), (n, 2, depth, lanes), (2, lead, lanes)],
+        [(n, *square), (n, *square), (n + 4, 2, depth, lanes), (2, lead, lanes)],
         [],
         *blocks[:n],
         *noises[:2],
@@ -528,9 +533,10 @@
     residual, *parts = adjoint_calls(
         rows, probes, blocks, noises, precond, circulant, spectrum, kernel, symbols, left, dft, turns, big_turn
     )
-    arrived = [swapped(parts[d], "probe", d) for d in range(1, probes)]
-    total = lax.optimization_barrier(parts[0] + arrived.pop())
-    total = before + sum(arrived, total) / probes
+    near_y, opposite, near_x = (swapped(parts[d], "probe", d) for d in (2, 3, 1))
+    total = lax.optimization_barrier(parts[0] + near_y)
+    total = lax.optimization_barrier(total + opposite)
+    total = before + (total + near_x) / probes
     total = total.transpose(1, 0, 2).reshape(width, depth * lanes).T
     return residual.reshape(probe_bits.shape), total
 

time: 34 us -> 33.8 us (level)
  transfers between devices with their start and end apart: 14 -> 14, of which waited for: 6 -> 4; matrix products, arithmetic and copies ran while one was open for 2% -> 2% of each run, Pallas kernels for 13% -> 13%
where the time goes in v7:
time: 33.8 us; the launch traced here: 33.7 us
  starting transfers between devices  14.1 us (42%)
  waiting for transfers between devices  10.6 us (31%)
  Pallas kernels  6.94 us (21%)
  between operations  0.75 us (2%)
  local copies, waits for them, and re-layouts  0.66 us (2%)
  other arithmetic  0.66 us (2%)
    ppermute x14, starting transfers between devices, swapped(): lax.ppermute(x, axis, [(i, i ^ d) for i in range(lax.axis_size(axis))])  14.1 us
    ppermute x14, waiting for transfers between devices, swapped(): lax.ppermute(x, axis, [(i, i ^ d) for i in range(lax.axis_size(axis))])  10.6 us
    pallas_call x4, Pallas kernels, call(): pl.pallas_call(kernel, out_shape=shapes, in_specs=[whole] * len(operands)...  5.73 us
    pallas_call x1, Pallas kernels, gathered_shards(): pl.pallas_call(functools.partial(pack_kernel, half, first), out_shape=(pl...  1.21 us
  transfers between devices with their start and end apart: 14, of which 4 were waited for; matrix products, arithmetic and copies ran while one was open for 2% of the time, Pallas kernels for 13%

profile of v7, /device:TPU:0, one launch (start us, length us, event | category | flops | bytes accessed | tf_op | source)
XLA Modules:
  0.0 33.7 jit_solution(12252640759109768399)
XLA Ops:
  0.6 1.2 %shard_map.86 = (f32[392,128]{1,0:T(8,128)S(1)}, f32[328,128]{1,0:T(8,128)S(1)}, bf16[4,128,128]{2,1,0:T(8,128)(2,1)S(1)}, f32[2,128,256]{2,1,0:T(8,128)S(1)}) custom-call(s32[128,128]{1,0:T(8,128)} %bitcast.32, f32[128,128]{1,0:T(8,128)} %bitcast.33, f32[16,8,128]{2,1,0:T(8,128)} %bitcast.28, f32[16,8,128]{2,1,0:T(8,128)} %bitcast.30, ...), custom_call_target="tpu_custom_call" | custom-call | tf_op jit(solution)/shard_map/pallas_call | solution.py:484
  1.8 4.1 %collective-permute-start.2 = (f32[328,128]{1,0:T(8,128)S(1)}, f32[328,128]{1,0:T(8,128)S(1)}, u32[]{:S(2)}, u32[]{:S(2)}) collective-permute-start(f32[328,128]{1,0:T(8,128)S(1)} %get-tuple-element.26), channel_id=1, source_target_pairs={{0,4},{1,5},{2,6},{3,7},{4,0},{5,1},{6,2},{7,3},{8,12},{9,13},{10,... | collective-permute-start | bytes 503816 | tf_op jit(solution)/shard_map/ppermute | solution.py:415
  5.9 1.6 %collective-permute-start.1 = (f32[328,128]{1,0:T(8,128)S(1)}, f32[328,128]{1,0:T(8,128)S(1)}, u32[]{:S(2)}, u32[]{:S(2)}) collective-permute-start(f32[328,128]{1,0:T(8,128)S(1)} %get-tuple-element.26), channel_id=1, source_target_pairs={{0,2},{1,3},{2,0},{3,1},{4,6},{5,7},{6,4},{7,5},{8,10},{9,11},{10,... | collective-permute-start | bytes 503816 | tf_op jit(solution)/shard_map/ppermute | solution.py:415
  7.5 0.0 collective-permute-start
  7.5 6.4 %collective-permute-done.2.refs_3_.refs_4_ = f32[328,128]{1,0:T(8,128)S(1)} collective-permute-done((f32[328,128]{1,0:T(8,128)S(1)}, f32[328,128]{1,0:T(8,128)S(1)}, u32[]{:S(2)}, u32[]{:S(2)}) %collective-permute-start.2) | collective-permute-done | bytes 167968 | tf_op jit(solution)/shard_map/ppermute | solution.py:415
  14.0 0.7 %collective-permute-start.5 = (f32[264,128]{1,0:T(8,128)S(1)}, f32[264,128]{1,0:T(8,128)S(1)}, u32[]{:S(2)}, u32[]{:S(2)}) collective-permute-start(f32[264,128]{1,0:T(8,128)S(1)} %slice.17), channel_id=1, source_target_pairs={{0,2},{1,3},{2,0},{3,1},{4,6},{5,7},{6,4},{7,5},{8,10},{9,11},{10,... | collective-permute-start | bytes 405512 | tf_op jit(solution)/shard_map/ppermute | solution.py:415
  14.6 0.0 collective-permute-done.1.refs_2_
  14.7 1.6 %collective-permute-start.6 = (f32[128,128]{1,0:T(8,128)S(1)}, f32[128,128]{1,0:T(8,128)S(1)}, u32[]{:S(2)}, u32[]{:S(2)}) collective-permute-start(f32[128,128]{1,0:T(8,128)S(1)} %pad_maximum_fusion), channel_id=1, source_target_pairs={{0,8},{8,0},{16,24},{24,16},{1,9},{9,1},{17,25},{25,17},{2,10},{10... | collective-permute-start | bytes 196616 | tf_op jit(solution)/shard_map/ppermute | solution.py:415
  16.2 0.0 collective-permute-done.refs_1_
  16.2 0.7 %shard_map.87 = (f32[4,2,128,128]{3,2,1,0:T(8,128)S(1)}, bf16[512,256]{1,0:T(8,128)(2,1)S(1)}, f32[8,128,256]{2,1,0:T(8,128)S(1)}) custom-call(f32[392,128]{1,0:T(8,128)S(1)} %get-tuple-element.25.refs_0_, f32[392,128]{1,0:T(8,128)S(1)} %collective-permute-done.refs_1_, f32[328,128]{1,0:T(8,128)S(1)} %collective-permute-done.1.refs_2_, ...), custom_call_target="tpu_custom_call" | custom-call | tf_op jit(solution)/shard_map/pallas_call | solution.py:403
  16.9 0.1 collective-permute-start.3
  17.0 0.5 %collective-permute-start.4 = (f32[328,128]{1,0:T(8,128)S(1)}, f32[328,128]{1,0:T(8,128)S(1)}, u32[]{:S(2)}, u32[]{:S(2)}) collective-permute-start(f32[328,128]{1,0:T(8,128)S(1)} %collective-permute-done.2.refs_3_.refs_4_), channel_id=1, source_target_pairs={{0,1},{1,0},{2,3},{3,2},{4,5},{5,4},{6,7},{7,6},{8,9},{9,8},{10,11... | collective-permute-start | bytes 503816 | tf_op jit(solution)/shard_map/ppermute | solution.py:415
  17.5 1.5 %collective-permute-done.6.refs_6_ = f32[128,128]{1,0:T(8,128)S(1)} collective-permute-done((f32[128,128]{1,0:T(8,128)S(1)}, f32[128,128]{1,0:T(8,128)S(1)}, u32[]{:S(2)}, u32[]{:S(2)}) %collective-permute-start.6) | collective-permute-done | bytes 65568 | tf_op jit(solution)/shard_map/ppermute | solution.py:415
  19.0 0.0 collective-permute-done.5.refs_6_
  19.0 0.0 collective-permute-start.7
  19.0 1.5 %collective-permute-start.8 = (f32[128,128]{1,0:T(8,128)S(1)}, f32[128,128]{1,0:T(8,128)S(1)}, u32[]{:S(2)}, u32[]{:S(2)}) collective-permute-start(f32[128,128]{1,0:T(8,128)S(1)} %pad_maximum_fusion.1), channel_id=1, source_target_pairs={{0,2},{1,3},{2,0},{3,1},{4,6},{5,7},{6,4},{7,5},{8,10},{9,11},{10,... | collective-permute-start | bytes 196616 | tf_op jit(solution)/shard_map/ppermute | solution.py:415
  20.5 0.2 collective-permute-start.10
  20.7 0.0 collective-permute-done.3.refs_3_
  20.7 0.0 collective-permute-done.4.refs_5_
  20.7 0.0 collective-permute-done.7.refs_7_
  20.7 3.0 %shard_map.88 = (f32[8,2,16,128]{3,2,1,0:T(8,128)S(1)}, f32[8,128,128]{2,1,0:T(8,128)S(1)}, f32[8,128,128]{2,1,0:T(8,128)S(1)}) custom-call(f32[392,128]{1,0:T(8,128)S(1)} %get-tuple-element.25.refs_0_, f32[392,128]{1,0:T(8,128)S(1)} %collective-permute-done.refs_1_, f32[328,128]{1,0:T(8,128)S(1)} %collective-permute-done.1.refs_2_, ...), custom_call_target="tpu_custom_call" | custom-call | tf_op jit(solution)/shard_map/pallas_call | solution.py:403
  23.6 0.0 collective-permute-done.8.refs_8_
  23.7 0.4 %collective-permute-start.9 = (f32[128,128]{1,0:T(8,128)S(1)}, f32[128,128]{1,0:T(8,128)S(1)}, u32[]{:S(2)}, u32[]{:S(2)}) collective-permute-start(f32[128,128]{1,0:T(8,128)S(1)} %collective-permute-done.8.refs_8_), channel_id=1, source_target_pairs={{0,1},{1,0},{2,3},{3,2},{4,5},{5,4},{6,7},{7,6},{8,9},{9,8},{10,11... | collective-permute-start | bytes 196616 | tf_op jit(solution)/shard_map/ppermute | solution.py:415
  24.1 0.0 collective-permute-done.10.refs_7_
  24.1 0.0 copy-start
  24.1 0.0 copy-start.1
  24.1 0.9 %shard_map.89 = (f32[6,128,128]{2,1,0:T(8,128)S(1)}, f32[6,128,128]{2,1,0:T(8,128)S(1)}, f32[10,2,16,128]{3,2,1,0:T(8,128)S(1)}, f32[2,8,128]{2,1,0:T(8,128)S(1)}) custom-call(f32[392,128]{1,0:T(8,128)S(1)} %get-tuple-element.25.refs_0_, f32[392,128]{1,0:T(8,128)S(1)} %collective-permute-done.refs_1_, f32[328,128]{1,0:T(8,128)S(1)} %collective-permute-done.1.refs_2_, ...), custom_call_target="tpu_custom_call" | custom-call | tf_op jit(solution)/shard_map/pallas_call | solution.py:403
  25.0 0.0 collective-permute-done.9.refs_9_
  25.0 0.0 copy-done
  25.0 0.0 copy-done.1
  25.0 1.2 %shard_map.90 = (f32[128,128]{1,0:T(8,128)S(1)}, f32[16,2,128]{2,1,0:T(2,128)S(1)}, f32[16,2,128]{2,1,0:T(2,128)S(1)}, f32[16,2,128]{2,1,0:T(2,128)S(1)}, f32[16,2,128]{2,1,0:T(2,128)S(1)}) custom-call(f32[392,128]{1,0:T(8,128)S(1)} %get-tuple-element.25.refs_0_, f32[392,128]{1,0:T(8,128)S(1)} %collective-permute-done.refs_1_, ...), custom_call_target="tpu_custom_call" | custom-call | tf_op jit(solution)/shard_map/pallas_call | solution.py:403
  26.2 1.6 %collective-permute-start.11 = (f32[16,2,128]{2,1,0:T(2,128)S(1)}, f32[16,2,128]{2,1,0:T(2,128)S(1)}, u32[]{:S(2)}, u32[]{:S(2)}) collective-permute-start(f32[16,2,128]{2,1,0:T(2,128)S(1)} %get-tuple-element.45), channel_id=1, source_target_pairs={{0,16},{8,24},{16,0},{24,8},{1,17},{9,25},{17,1},{25,9},{2,18},{10... | collective-permute-start | bytes 49160 | tf_op jit(solution)/shard_map/ppermute | solution.py:415
  27.9 1.4 %collective-permute-start.12 = (f32[16,2,128]{2,1,0:T(2,128)S(1)}, f32[16,2,128]{2,1,0:T(2,128)S(1)}, u32[]{:S(2)}, u32[]{:S(2)}) collective-permute-start(f32[16,2,128]{2,1,0:T(2,128)S(1)} %get-tuple-element.46), channel_id=1, source_target_pairs={{0,24},{8,16},{16,8},{24,0},{1,25},{9,17},{17,9},{25,1},{2,26},{10... | collective-permute-start | bytes 49160 | tf_op jit(solution)/shard_map/ppermute | solution.py:415
  29.3 0.5 %collective-permute-start.13 = (f32[16,2,128]{2,1,0:T(2,128)S(1)}, f32[16,2,128]{2,1,0:T(2,128)S(1)}, u32[]{:S(2)}, u32[]{:S(2)}) collective-permute-start(f32[16,2,128]{2,1,0:T(2,128)S(1)} %get-tuple-element.47), channel_id=1, source_target_pairs={{0,8},{8,0},{16,24},{24,16},{1,9},{9,1},{17,25},{25,17},{2,10},{10... | collective-permute-start | bytes 49160 | tf_op jit(solution)/shard_map/ppermute | solution.py:415
  29.8 0.6 %copy.9 = f32[1,1,16384]{2,1,0:T(1,128)} copy(f32[1,1,16384]{2,1,0:T(1,128)S(1)} %bitcast.27) | data formatting | bytes 131072
  30.4 0.0 collective-permute-done.11
  30.4 0.0 copy-start.2
  30.5 2.1 %collective-permute-done.12 = f32[16,2,128]{2,1,0:T(2,128)S(1)} collective-permute-done((f32[16,2,128]{2,1,0:T(2,128)S(1)}, f32[16,2,128]{2,1,0:T(2,128)S(1)}, u32[]{:S(2)}, u32[]{:S(2)}) %collective-permute-start.12) | collective-permute-done | bytes 16416 | tf_op jit(solution)/shard_map/ppermute | solution.py:415
  32.5 0.5 %collective-permute-done.13 = f32[16,2,128]{2,1,0:T(2,128)S(1)} collective-permute-done((f32[16,2,128]{2,1,0:T(2,128)S(1)}, f32[16,2,128]{2,1,0:T(2,128)S(1)}, u32[]{:S(2)}, u32[]{:S(2)}) %collective-permute-start.13) | collective-permute-done | bytes 16416 | tf_op jit(solution)/shard_map/ppermute | solution.py:415
  33.1 0.0 copy-done.2
  33.1 0.6 %fusion = f32[2048,2]{0,1:T(2,128)} fusion(f32[2048,2]{0,1:T(2,128)S(1)} %copy-done.2, f32[16,2,128]{2,1,0:T(2,128)S(1)} %add.13, f32[16,2,128]{2,1,0:T(2,128)S(1)} %collective-permute-done.13), kind=kLoop, calls=%fused_computation.3 | loop fusion | flops 12288 | bytes 65536 | tf_op jit(solution)/shard_map/transpose | solution.py:540
  (8 shorter events, 0.1 us)
Async XLA Ops:
  1.8 12.1 %collective-permute-start.2 = (f32[328,128]{1,0:T(8,128)S(1)}, f32[328,128]{1,0:T(8,128)S(1)}, u32[]{:S(2)}, u32[]{:S(2)}) collective-permute-start(f32[328,128]{1,0:T(8,128)S(1)} %get-tuple-element.26), channel_id=1, source_target_pairs={{0,4},{1,5},{2,6},{3,7},{4,0},{5,1},{6,2},{7,3},{8,12},{9,13},{10,... | collective-permute-start | bytes 503816 | tf_op jit(solution)/shard_map/ppermute | solution.py:415
  5.9 8.7 %collective-permute-start.1 = (f32[328,128]{1,0:T(8,128)S(1)}, f32[328,128]{1,0:T(8,128)S(1)}, u32[]{:S(2)}, u32[]{:S(2)}) collective-permute-start(f32[328,128]{1,0:T(8,128)S(1)} %get-tuple-element.26), channel_id=1, source_target_pairs={{0,2},{1,3},{2,0},{3,1},{4,6},{5,7},{6,4},{7,5},{8,10},{9,11},{10,... | collective-permute-start | bytes 503816 | tf_op jit(solution)/shard_map/ppermute | solution.py:415
  7.5 8.7 %collective-permute-start = (f32[392,128]{1,0:T(8,128)S(1)}, f32[392,128]{1,0:T(8,128)S(1)}, u32[]{:S(2)}, u32[]{:S(2)}) collective-permute-start(f32[392,128]{1,0:T(8,128)S(1)} %get-tuple-element.25.refs_0_), channel_id=1, source_target_pairs={{0,1},{1,0},{2,3},{3,2},{4,5},{5,4},{6,7},{7,6},{8,9},{9,8},{10,11... | collective-permute-start | bytes 602120 | tf_op jit(solution)/shard_map/ppermute | solution.py:415
  14.0 5.1 %collective-permute-start.5 = (f32[264,128]{1,0:T(8,128)S(1)}, f32[264,128]{1,0:T(8,128)S(1)}, u32[]{:S(2)}, u32[]{:S(2)}) collective-permute-start(f32[264,128]{1,0:T(8,128)S(1)} %slice.17), channel_id=1, source_target_pairs={{0,2},{1,3},{2,0},{3,1},{4,6},{5,7},{6,4},{7,5},{8,10},{9,11},{10,... | collective-permute-start | bytes 405512 | tf_op jit(solution)/shard_map/ppermute | solution.py:415
  14.7 4.3 %collective-permute-start.6 = (f32[128,128]{1,0:T(8,128)S(1)}, f32[128,128]{1,0:T(8,128)S(1)}, u32[]{:S(2)}, u32[]{:S(2)}) collective-permute-start(f32[128,128]{1,0:T(8,128)S(1)} %pad_maximum_fusion), channel_id=1, source_target_pairs={{0,8},{8,0},{16,24},{24,16},{1,9},{9,1},{17,25},{25,17},{2,10},{10... | collective-permute-start | bytes 196616 | tf_op jit(solution)/shard_map/ppermute | solution.py:415
  16.9 3.8 %collective-permute-start.3 = (f32[328,128]{1,0:T(8,128)S(1)}, f32[328,128]{1,0:T(8,128)S(1)}, u32[]{:S(2)}, u32[]{:S(2)}) collective-permute-start(f32[328,128]{1,0:T(8,128)S(1)} %collective-permute-done.1.refs_2_), channel_id=1, source_target_pairs={{0,1},{1,0},{2,3},{3,2},{4,5},{5,4},{6,7},{7,6},{8,9},{9,8},{10,11... | collective-permute-start | bytes 503816 | tf_op jit(solution)/shard_map/ppermute | solution.py:415
  17.0 3.7 %collective-permute-start.4 = (f32[328,128]{1,0:T(8,128)S(1)}, f32[328,128]{1,0:T(8,128)S(1)}, u32[]{:S(2)}, u32[]{:S(2)}) collective-permute-start(f32[328,128]{1,0:T(8,128)S(1)} %collective-permute-done.2.refs_3_.refs_4_), channel_id=1, source_target_pairs={{0,1},{1,0},{2,3},{3,2},{4,5},{5,4},{6,7},{7,6},{8,9},{9,8},{10,11... | collective-permute-start | bytes 503816 | tf_op jit(solution)/shard_map/ppermute | solution.py:415
  19.0 1.6 %collective-permute-start.7 = (f32[264,128]{1,0:T(8,128)S(1)}, f32[264,128]{1,0:T(8,128)S(1)}, u32[]{:S(2)}, u32[]{:S(2)}) collective-permute-start(f32[264,128]{1,0:T(8,128)S(1)} %collective-permute-done.5.refs_6_), channel_id=1, source_target_pairs={{0,1},{1,0},{2,3},{3,2},{4,5},{5,4},{6,7},{7,6},{8,9},{9,8},{10,11... | collective-permute-start | bytes 405512 | tf_op jit(solution)/shard_map/ppermute | solution.py:415
  19.0 4.6 %collective-permute-start.8 = (f32[128,128]{1,0:T(8,128)S(1)}, f32[128,128]{1,0:T(8,128)S(1)}, u32[]{:S(2)}, u32[]{:S(2)}) collective-permute-start(f32[128,128]{1,0:T(8,128)S(1)} %pad_maximum_fusion.1), channel_id=1, source_target_pairs={{0,2},{1,3},{2,0},{3,1},{4,6},{5,7},{6,4},{7,5},{8,10},{9,11},{10,... | collective-permute-start | bytes 196616 | tf_op jit(solution)/shard_map/ppermute | solution.py:415
  20.5 3.6 %collective-permute-start.10 = (f32[128,128]{1,0:T(8,128)S(1)}, f32[128,128]{1,0:T(8,128)S(1)}, u32[]{:S(2)}, u32[]{:S(2)}) collective-permute-start(f32[128,128]{1,0:T(8,128)S(1)} %collective-permute-done.6.refs_6_), channel_id=1, source_target_pairs={{0,1},{1,0},{2,3},{3,2},{4,5},{5,4},{6,7},{7,6},{8,9},{9,8},{10,11... | collective-permute-start | bytes 196616 | tf_op jit(solution)/shard_map/ppermute | solution.py:415
  23.7 1.3 %collective-permute-start.9 = (f32[128,128]{1,0:T(8,128)S(1)}, f32[128,128]{1,0:T(8,128)S(1)}, u32[]{:S(2)}, u32[]{:S(2)}) collective-permute-start(f32[128,128]{1,0:T(8,128)S(1)} %collective-permute-done.8.refs_8_), channel_id=1, source_target_pairs={{0,1},{1,0},{2,3},{3,2},{4,5},{5,4},{6,7},{7,6},{8,9},{9,8},{10,11... | collective-permute-start | bytes 196616 | tf_op jit(solution)/shard_map/ppermute | solution.py:415
  24.1 0.9 %copy-start = (f32[2048,8]{0,1:T(8,128)S(1)}, f32[2048,8]{0,1:T(8,128)}, u32[]{:S(2)}) copy-start(f32[2048,8]{0,1:T(8,128)} %param.9) | copy-start | bytes 196612
  24.1 0.9 %copy-start.1 = (f32[2048,8]{0,1:T(8,128)S(1)}, f32[2048,8]{0,1:T(8,128)}, u32[]{:S(2)}) copy-start(f32[2048,8]{0,1:T(8,128)} %param.10) | copy-start | bytes 196612
  26.2 4.2 %collective-permute-start.11 = (f32[16,2,128]{2,1,0:T(2,128)S(1)}, f32[16,2,128]{2,1,0:T(2,128)S(1)}, u32[]{:S(2)}, u32[]{:S(2)}) collective-permute-start(f32[16,2,128]{2,1,0:T(2,128)S(1)} %get-tuple-element.45), channel_id=1, source_target_pairs={{0,16},{8,24},{16,0},{24,8},{1,17},{9,25},{17,1},{25,9},{2,18},{10... | collective-permute-start | bytes 49160 | tf_op jit(solution)/shard_map/ppermute | solution.py:415
  27.9 4.6 %collective-permute-start.12 = (f32[16,2,128]{2,1,0:T(2,128)S(1)}, f32[16,2,128]{2,1,0:T(2,128)S(1)}, u32[]{:S(2)}, u32[]{:S(2)}) collective-permute-start(f32[16,2,128]{2,1,0:T(2,128)S(1)} %get-tuple-element.46), channel_id=1, source_target_pairs={{0,24},{8,16},{16,8},{24,0},{1,25},{9,17},{17,9},{25,1},{2,26},{10... | collective-permute-start | bytes 49160 | tf_op jit(solution)/shard_map/ppermute | solution.py:415
  29.3 3.7 %collective-permute-start.13 = (f32[16,2,128]{2,1,0:T(2,128)S(1)}, f32[16,2,128]{2,1,0:T(2,128)S(1)}, u32[]{:S(2)}, u32[]{:S(2)}) collective-permute-start(f32[16,2,128]{2,1,0:T(2,128)S(1)} %get-tuple-element.47), channel_id=1, source_target_pairs={{0,8},{8,0},{16,24},{24,16},{1,9},{9,1},{17,25},{25,17},{2,10},{10... | collective-permute-start | bytes 49160 | tf_op jit(solution)/shard_map/ppermute | solution.py:415
  30.4 2.6 %copy-start.2 = (f32[2048,2]{0,1:T(2,128)S(1)}, f32[2048,2]{0,1:T(2,128)}, u32[]{:S(2)}) copy-start(f32[2048,2]{0,1:T(2,128)} %param.11) | copy-start | bytes 49156

commit v8 on v7

--- a/solution.py
+++ b/solution.py
@@ -132,7 +132,7 @@
     out[first - lead : first] = jnp.concatenate([middle] * (lead // 2), 0)
     sent[:first] = out[:first]
     share = lanes // 2
-    side = lax.rem(lax.axis_index("probe"), 2)
+    side = lax.div(lax.axis_index("probe"), lax.axis_size("probe") // 2)
     sent[first:] = out[pl.ds(pl.multiple_of(first + side * share, lead), share)]
     copies[4].wait()
     copies[5].wait()
@@ -292,7 +292,7 @@
 
 def whole_noise(target, held, other):
     share = lanes // 2
-    side = lax.rem(lax.axis_index("probe"), 2) * share
+    side = lax.div(lax.axis_index("probe"), lax.axis_size("probe") // 2) * share
     target[pl.ds(pl.multiple_of(side, share), share)] = held[held.shape[0] - share :]
     target[pl.ds(pl.multiple_of(share - side, share), share)] = other[...]
 
@@ -427,8 +427,8 @@
     return swapped(x, "seq", 1)
 
 
-def across_x(x):
-    return swapped(x, "probe", 1)
+def across_y(x):
+    return swapped(x, "probe", lax.axis_size("probe") // 2)
 
 
 def next_chip(x):
@@ -511,7 +511,7 @@
         dft,
         turns,
     )
-    halves = across_x(jnp.concatenate([neighbour[first:], far[first:]], 0))
+    halves = across_y(jnp.concatenate([neighbour[first:], far[first:]], 0))
     blocks = early[:2]
     for x, earlier in ((neighbour, found), (far, found), (passed_on, halves)):
         blocks += [x, other_core(after(x, earlier))]

time: 33.8 us -> 33.8 us (level)
  no operation moved by 1% of the time
where the time goes in v8:
time: 33.8 us; the launch traced here: 33.7 us
  starting transfers between devices  14.1 us (42%)
  waiting for transfers between devices  10.6 us (31%)
  Pallas kernels  6.92 us (20%)
  between operations  0.73 us (2%)
  local copies, waits for them, and re-layouts  0.66 us (2%)
  other arithmetic  0.66 us (2%)
    ppermute x14, starting transfers between devices, swapped(): lax.ppermute(x, axis, [(i, i ^ d) for i in range(lax.axis_size(axis))])  14.1 us
    ppermute x14, waiting for transfers between devices, swapped(): lax.ppermute(x, axis, [(i, i ^ d) for i in range(lax.axis_size(axis))])  10.6 us
    pallas_call x4, Pallas kernels, call(): pl.pallas_call(kernel, out_shape=shapes, in_specs=[whole] * len(operands)...  5.71 us
    pallas_call x1, Pallas kernels, gathered_shards(): pl.pallas_call(functools.partial(pack_kernel, half, first), out_shape=(pl...  1.21 us
  transfers between devices with their start and end apart: 14, of which 4 were waited for; matrix products, arithmetic and copies ran while one was open for 2% of the time, Pallas kernels for 13%

profile of v8, /device:TPU:0, one launch (start us, length us, event | category | flops | bytes accessed | tf_op | source)
XLA Modules:
  0.0 33.7 jit_solution(14570944690067797997)
XLA Ops:
  0.6 1.2 %shard_map.86 = (f32[392,128]{1,0:T(8,128)S(1)}, f32[328,128]{1,0:T(8,128)S(1)}, bf16[4,128,128]{2,1,0:T(8,128)(2,1)S(1)}, f32[2,128,256]{2,1,0:T(8,128)S(1)}) custom-call(s32[128,128]{1,0:T(8,128)} %bitcast.32, f32[128,128]{1,0:T(8,128)} %bitcast.33, f32[16,8,128]{2,1,0:T(8,128)} %bitcast.28, f32[16,8,128]{2,1,0:T(8,128)} %bitcast.30, ...), custom_call_target="tpu_custom_call" | custom-call | tf_op jit(solution)/shard_map/pallas_call | solution.py:484
  1.8 4.1 %collective-permute-start.2 = (f32[328,128]{1,0:T(8,128)S(1)}, f32[328,128]{1,0:T(8,128)S(1)}, u32[]{:S(2)}, u32[]{:S(2)}) collective-permute-start(f32[328,128]{1,0:T(8,128)S(1)} %get-tuple-element.26), channel_id=1, source_target_pairs={{0,4},{1,5},{2,6},{3,7},{4,0},{5,1},{6,2},{7,3},{8,12},{9,13},{10,... | collective-permute-start | bytes 503816 | tf_op jit(solution)/shard_map/ppermute | solution.py:415
  5.9 1.6 %collective-permute-start.1 = (f32[328,128]{1,0:T(8,128)S(1)}, f32[328,128]{1,0:T(8,128)S(1)}, u32[]{:S(2)}, u32[]{:S(2)}) collective-permute-start(f32[328,128]{1,0:T(8,128)S(1)} %get-tuple-element.26), channel_id=1, source_target_pairs={{0,2},{1,3},{2,0},{3,1},{4,6},{5,7},{6,4},{7,5},{8,10},{9,11},{10,... | collective-permute-start | bytes 503816 | tf_op jit(solution)/shard_map/ppermute | solution.py:415
  7.5 0.0 collective-permute-start
  7.5 6.4 %collective-permute-done.2.refs_3_.refs_4_ = f32[328,128]{1,0:T(8,128)S(1)} collective-permute-done((f32[328,128]{1,0:T(8,128)S(1)}, f32[328,128]{1,0:T(8,128)S(1)}, u32[]{:S(2)}, u32[]{:S(2)}) %collective-permute-start.2) | collective-permute-done | bytes 167968 | tf_op jit(solution)/shard_map/ppermute | solution.py:415
  14.0 0.7 %collective-permute-start.5 = (f32[264,128]{1,0:T(8,128)S(1)}, f32[264,128]{1,0:T(8,128)S(1)}, u32[]{:S(2)}, u32[]{:S(2)}) collective-permute-start(f32[264,128]{1,0:T(8,128)S(1)} %slice.17), channel_id=1, source_target_pairs={{0,2},{1,3},{2,0},{3,1},{4,6},{5,7},{6,4},{7,5},{8,10},{9,11},{10,... | collective-permute-start | bytes 405512 | tf_op jit(solution)/shard_map/ppermute | solution.py:415
  14.6 0.0 collective-permute-done.1.refs_2_
  14.7 1.6 %collective-permute-start.6 = (f32[128,128]{1,0:T(8,128)S(1)}, f32[128,128]{1,0:T(8,128)S(1)}, u32[]{:S(2)}, u32[]{:S(2)}) collective-permute-start(f32[128,128]{1,0:T(8,128)S(1)} %pad_maximum_fusion), channel_id=1, source_target_pairs={{0,16},{8,24},{16,0},{24,8},{1,17},{9,25},{17,1},{25,9},{2,18},{10... | collective-permute-start | bytes 196616 | tf_op jit(solution)/shard_map/ppermute | solution.py:415
  16.2 0.0 collective-permute-done.refs_1_
  16.3 0.7 %shard_map.87 = (f32[4,2,128,128]{3,2,1,0:T(8,128)S(1)}, bf16[512,256]{1,0:T(8,128)(2,1)S(1)}, f32[8,128,256]{2,1,0:T(8,128)S(1)}) custom-call(f32[392,128]{1,0:T(8,128)S(1)} %get-tuple-element.25.refs_0_, f32[392,128]{1,0:T(8,128)S(1)} %collective-permute-done.refs_1_, f32[328,128]{1,0:T(8,128)S(1)} %collective-permute-done.1.refs_2_, ...), custom_call_target="tpu_custom_call" | custom-call | tf_op jit(solution)/shard_map/pallas_call | solution.py:403
  16.9 0.1 collective-permute-start.3
  17.0 0.5 %collective-permute-start.4 = (f32[328,128]{1,0:T(8,128)S(1)}, f32[328,128]{1,0:T(8,128)S(1)}, u32[]{:S(2)}, u32[]{:S(2)}) collective-permute-start(f32[328,128]{1,0:T(8,128)S(1)} %collective-permute-done.2.refs_3_.refs_4_), channel_id=1, source_target_pairs={{0,1},{1,0},{2,3},{3,2},{4,5},{5,4},{6,7},{7,6},{8,9},{9,8},{10,11... | collective-permute-start | bytes 503816 | tf_op jit(solution)/shard_map/ppermute | solution.py:415
  17.5 1.5 %collective-permute-done.6.refs_6_ = f32[128,128]{1,0:T(8,128)S(1)} collective-permute-done((f32[128,128]{1,0:T(8,128)S(1)}, f32[128,128]{1,0:T(8,128)S(1)}, u32[]{:S(2)}, u32[]{:S(2)}) %collective-permute-start.6) | collective-permute-done | bytes 65568 | tf_op jit(solution)/shard_map/ppermute | solution.py:415
  19.0 0.0 collective-permute-done.5.refs_6_
  19.0 0.0 collective-permute-start.7
  19.0 1.5 %collective-permute-start.8 = (f32[128,128]{1,0:T(8,128)S(1)}, f32[128,128]{1,0:T(8,128)S(1)}, u32[]{:S(2)}, u32[]{:S(2)}) collective-permute-start(f32[128,128]{1,0:T(8,128)S(1)} %pad_maximum_fusion.1), channel_id=1, source_target_pairs={{0,2},{1,3},{2,0},{3,1},{4,6},{5,7},{6,4},{7,5},{8,10},{9,11},{10,... | collective-permute-start | bytes 196616 | tf_op jit(solution)/shard_map/ppermute | solution.py:415
  20.5 0.2 collective-permute-start.10
  20.7 0.0 collective-permute-done.3.refs_3_
  20.7 0.0 collective-permute-done.4.refs_5_
  20.7 0.0 collective-permute-done.7.refs_7_
  20.7 3.0 %shard_map.88 = (f32[8,2,16,128]{3,2,1,0:T(8,128)S(1)}, f32[8,128,128]{2,1,0:T(8,128)S(1)}, f32[8,128,128]{2,1,0:T(8,128)S(1)}) custom-call(f32[392,128]{1,0:T(8,128)S(1)} %get-tuple-element.25.refs_0_, f32[392,128]{1,0:T(8,128)S(1)} %collective-permute-done.refs_1_, f32[328,128]{1,0:T(8,128)S(1)} %collective-permute-done.1.refs_2_, ...), custom_call_target="tpu_custom_call" | custom-call | tf_op jit(solution)/shard_map/pallas_call | solution.py:403
  23.6 0.0 collective-permute-done.8.refs_8_
  23.7 0.4 %collective-permute-start.9 = (f32[128,128]{1,0:T(8,128)S(1)}, f32[128,128]{1,0:T(8,128)S(1)}, u32[]{:S(2)}, u32[]{:S(2)}) collective-permute-start(f32[128,128]{1,0:T(8,128)S(1)} %collective-permute-done.8.refs_8_), channel_id=1, source_target_pairs={{0,1},{1,0},{2,3},{3,2},{4,5},{5,4},{6,7},{7,6},{8,9},{9,8},{10,11... | collective-permute-start | bytes 196616 | tf_op jit(solution)/shard_map/ppermute | solution.py:415
  24.1 0.0 collective-permute-done.10.refs_7_
  24.1 0.0 copy-start
  24.1 0.0 copy-start.1
  24.1 0.9 %shard_map.89 = (f32[6,128,128]{2,1,0:T(8,128)S(1)}, f32[6,128,128]{2,1,0:T(8,128)S(1)}, f32[10,2,16,128]{3,2,1,0:T(8,128)S(1)}, f32[2,8,128]{2,1,0:T(8,128)S(1)}) custom-call(f32[392,128]{1,0:T(8,128)S(1)} %get-tuple-element.25.refs_0_, f32[392,128]{1,0:T(8,128)S(1)} %collective-permute-done.refs_1_, f32[328,128]{1,0:T(8,128)S(1)} %collective-permute-done.1.refs_2_, ...), custom_call_target="tpu_custom_call" | custom-call | tf_op jit(solution)/shard_map/pallas_call | solution.py:403
  24.9 0.0 collective-permute-done.9.refs_9_
  25.0 0.0 copy-done
  25.0 0.0 copy-done.1
  25.0 1.2 %shard_map.90 = (f32[128,128]{1,0:T(8,128)S(1)}, f32[16,2,128]{2,1,0:T(2,128)S(1)}, f32[16,2,128]{2,1,0:T(2,128)S(1)}, f32[16,2,128]{2,1,0:T(2,128)S(1)}, f32[16,2,128]{2,1,0:T(2,128)S(1)}) custom-call(f32[392,128]{1,0:T(8,128)S(1)} %get-tuple-element.25.refs_0_, f32[392,128]{1,0:T(8,128)S(1)} %collective-permute-done.refs_1_, ...), custom_call_target="tpu_custom_call" | custom-call | tf_op jit(solution)/shard_map/pallas_call | solution.py:403
  26.2 1.6 %collective-permute-start.11 = (f32[16,2,128]{2,1,0:T(2,128)S(1)}, f32[16,2,128]{2,1,0:T(2,128)S(1)}, u32[]{:S(2)}, u32[]{:S(2)}) collective-permute-start(f32[16,2,128]{2,1,0:T(2,128)S(1)} %get-tuple-element.45), channel_id=1, source_target_pairs={{0,16},{8,24},{16,0},{24,8},{1,17},{9,25},{17,1},{25,9},{2,18},{10... | collective-permute-start | bytes 49160 | tf_op jit(solution)/shard_map/ppermute | solution.py:415
  27.9 1.4 %collective-permute-start.12 = (f32[16,2,128]{2,1,0:T(2,128)S(1)}, f32[16,2,128]{2,1,0:T(2,128)S(1)}, u32[]{:S(2)}, u32[]{:S(2)}) collective-permute-start(f32[16,2,128]{2,1,0:T(2,128)S(1)} %get-tuple-element.46), channel_id=1, source_target_pairs={{0,24},{8,16},{16,8},{24,0},{1,25},{9,17},{17,9},{25,1},{2,26},{10... | collective-permute-start | bytes 49160 | tf_op jit(solution)/shard_map/ppermute | solution.py:415
  29.3 0.5 %collective-permute-start.13 = (f32[16,2,128]{2,1,0:T(2,128)S(1)}, f32[16,2,128]{2,1,0:T(2,128)S(1)}, u32[]{:S(2)}, u32[]{:S(2)}) collective-permute-start(f32[16,2,128]{2,1,0:T(2,128)S(1)} %get-tuple-element.47), channel_id=1, source_target_pairs={{0,8},{8,0},{16,24},{24,16},{1,9},{9,1},{17,25},{25,17},{2,10},{10... | collective-permute-start | bytes 49160 | tf_op jit(solution)/shard_map/ppermute | solution.py:415
  29.8 0.6 %copy.9 = f32[1,1,16384]{2,1,0:T(1,128)} copy(f32[1,1,16384]{2,1,0:T(1,128)S(1)} %bitcast.27) | data formatting | bytes 131072
  30.4 0.0 collective-permute-done.11
  30.4 0.0 copy-start.2
  30.4 2.1 %collective-permute-done.12 = f32[16,2,128]{2,1,0:T(2,128)S(1)} collective-permute-done((f32[16,2,128]{2,1,0:T(2,128)S(1)}, f32[16,2,128]{2,1,0:T(2,128)S(1)}, u32[]{:S(2)}, u32[]{:S(2)}) %collective-permute-start.12) | collective-permute-done | bytes 16416 | tf_op jit(solution)/shard_map/ppermute | solution.py:415
  32.5 0.5 %collective-permute-done.13 = f32[16,2,128]{2,1,0:T(2,128)S(1)} collective-permute-done((f32[16,2,128]{2,1,0:T(2,128)S(1)}, f32[16,2,128]{2,1,0:T(2,128)S(1)}, u32[]{:S(2)}, u32[]{:S(2)}) %collective-permute-start.13) | collective-permute-done | bytes 16416 | tf_op jit(solution)/shard_map/ppermute | solution.py:415
  33.0 0.0 copy-done.2
  33.0 0.6 %fusion = f32[2048,2]{0,1:T(2,128)} fusion(f32[2048,2]{0,1:T(2,128)S(1)} %copy-done.2, f32[16,2,128]{2,1,0:T(2,128)S(1)} %add.13, f32[16,2,128]{2,1,0:T(2,128)S(1)} %collective-permute-done.13), kind=kLoop, calls=%fused_computation.3 | loop fusion | flops 12288 | bytes 65536 | tf_op jit(solution)/shard_map/transpose | solution.py:540
  (8 shorter events, 0.1 us)
Async XLA Ops:
  1.8 12.1 %collective-permute-start.2 = (f32[328,128]{1,0:T(8,128)S(1)}, f32[328,128]{1,0:T(8,128)S(1)}, u32[]{:S(2)}, u32[]{:S(2)}) collective-permute-start(f32[328,128]{1,0:T(8,128)S(1)} %get-tuple-element.26), channel_id=1, source_target_pairs={{0,4},{1,5},{2,6},{3,7},{4,0},{5,1},{6,2},{7,3},{8,12},{9,13},{10,... | collective-permute-start | bytes 503816 | tf_op jit(solution)/shard_map/ppermute | solution.py:415
  5.9 8.7 %collective-permute-start.1 = (f32[328,128]{1,0:T(8,128)S(1)}, f32[328,128]{1,0:T(8,128)S(1)}, u32[]{:S(2)}, u32[]{:S(2)}) collective-permute-start(f32[328,128]{1,0:T(8,128)S(1)} %get-tuple-element.26), channel_id=1, source_target_pairs={{0,2},{1,3},{2,0},{3,1},{4,6},{5,7},{6,4},{7,5},{8,10},{9,11},{10,... | collective-permute-start | bytes 503816 | tf_op jit(solution)/shard_map/ppermute | solution.py:415
  7.5 8.7 %collective-permute-start = (f32[392,128]{1,0:T(8,128)S(1)}, f32[392,128]{1,0:T(8,128)S(1)}, u32[]{:S(2)}, u32[]{:S(2)}) collective-permute-start(f32[392,128]{1,0:T(8,128)S(1)} %get-tuple-element.25.refs_0_), channel_id=1, source_target_pairs={{0,1},{1,0},{2,3},{3,2},{4,5},{5,4},{6,7},{7,6},{8,9},{9,8},{10,11... | collective-permute-start | bytes 602120 | tf_op jit(solution)/shard_map/ppermute | solution.py:415
  14.0 5.1 %collective-permute-start.5 = (f32[264,128]{1,0:T(8,128)S(1)}, f32[264,128]{1,0:T(8,128)S(1)}, u32[]{:S(2)}, u32[]{:S(2)}) collective-permute-start(f32[264,128]{1,0:T(8,128)S(1)} %slice.17), channel_id=1, source_target_pairs={{0,2},{1,3},{2,0},{3,1},{4,6},{5,7},{6,4},{7,5},{8,10},{9,11},{10,... | collective-permute-start | bytes 405512 | tf_op jit(solution)/shard_map/ppermute | solution.py:415
  14.7 4.3 %collective-permute-start.6 = (f32[128,128]{1,0:T(8,128)S(1)}, f32[128,128]{1,0:T(8,128)S(1)}, u32[]{:S(2)}, u32[]{:S(2)}) collective-permute-start(f32[128,128]{1,0:T(8,128)S(1)} %pad_maximum_fusion), channel_id=1, source_target_pairs={{0,16},{8,24},{16,0},{24,8},{1,17},{9,25},{17,1},{25,9},{2,18},{10... | collective-permute-start | bytes 196616 | tf_op jit(solution)/shard_map/ppermute | solution.py:415
  16.9 3.8 %collective-permute-start.3 = (f32[328,128]{1,0:T(8,128)S(1)}, f32[328,128]{1,0:T(8,128)S(1)}, u32[]{:S(2)}, u32[]{:S(2)}) collective-permute-start(f32[328,128]{1,0:T(8,128)S(1)} %collective-permute-done.1.refs_2_), channel_id=1, source_target_pairs={{0,1},{1,0},{2,3},{3,2},{4,5},{5,4},{6,7},{7,6},{8,9},{9,8},{10,11... | collective-permute-start | bytes 503816 | tf_op jit(solution)/shard_map/ppermute | solution.py:415
  17.0 3.7 %collective-permute-start.4 = (f32[328,128]{1,0:T(8,128)S(1)}, f32[328,128]{1,0:T(8,128)S(1)}, u32[]{:S(2)}, u32[]{:S(2)}) collective-permute-start(f32[328,128]{1,0:T(8,128)S(1)} %collective-permute-done.2.refs_3_.refs_4_), channel_id=1, source_target_pairs={{0,1},{1,0},{2,3},{3,2},{4,5},{5,4},{6,7},{7,6},{8,9},{9,8},{10,11... | collective-permute-start | bytes 503816 | tf_op jit(solution)/shard_map/ppermute | solution.py:415
  19.0 1.6 %collective-permute-start.7 = (f32[264,128]{1,0:T(8,128)S(1)}, f32[264,128]{1,0:T(8,128)S(1)}, u32[]{:S(2)}, u32[]{:S(2)}) collective-permute-start(f32[264,128]{1,0:T(8,128)S(1)} %collective-permute-done.5.refs_6_), channel_id=1, source_target_pairs={{0,1},{1,0},{2,3},{3,2},{4,5},{5,4},{6,7},{7,6},{8,9},{9,8},{10,11... | collective-permute-start | bytes 405512 | tf_op jit(solution)/shard_map/ppermute | solution.py:415
  19.0 4.6 %collective-permute-start.8 = (f32[128,128]{1,0:T(8,128)S(1)}, f32[128,128]{1,0:T(8,128)S(1)}, u32[]{:S(2)}, u32[]{:S(2)}) collective-permute-start(f32[128,128]{1,0:T(8,128)S(1)} %pad_maximum_fusion.1), channel_id=1, source_target_pairs={{0,2},{1,3},{2,0},{3,1},{4,6},{5,7},{6,4},{7,5},{8,10},{9,11},{10,... | collective-permute-start | bytes 196616 | tf_op jit(solution)/shard_map/ppermute | solution.py:415
  20.5 3.6 %collective-permute-start.10 = (f32[128,128]{1,0:T(8,128)S(1)}, f32[128,128]{1,0:T(8,128)S(1)}, u32[]{:S(2)}, u32[]{:S(2)}) collective-permute-start(f32[128,128]{1,0:T(8,128)S(1)} %collective-permute-done.6.refs_6_), channel_id=1, source_target_pairs={{0,1},{1,0},{2,3},{3,2},{4,5},{5,4},{6,7},{7,6},{8,9},{9,8},{10,11... | collective-permute-start | bytes 196616 | tf_op jit(solution)/shard_map/ppermute | solution.py:415
  23.7 1.3 %collective-permute-start.9 = (f32[128,128]{1,0:T(8,128)S(1)}, f32[128,128]{1,0:T(8,128)S(1)}, u32[]{:S(2)}, u32[]{:S(2)}) collective-permute-start(f32[128,128]{1,0:T(8,128)S(1)} %collective-permute-done.8.refs_8_), channel_id=1, source_target_pairs={{0,1},{1,0},{2,3},{3,2},{4,5},{5,4},{6,7},{7,6},{8,9},{9,8},{10,11... | collective-permute-start | bytes 196616 | tf_op jit(solution)/shard_map/ppermute | solution.py:415
  24.1 0.9 %copy-start = (f32[2048,8]{0,1:T(8,128)S(1)}, f32[2048,8]{0,1:T(8,128)}, u32[]{:S(2)}) copy-start(f32[2048,8]{0,1:T(8,128)} %param.9) | copy-start | bytes 196612
  24.1 0.9 %copy-start.1 = (f32[2048,8]{0,1:T(8,128)S(1)}, f32[2048,8]{0,1:T(8,128)}, u32[]{:S(2)}) copy-start(f32[2048,8]{0,1:T(8,128)} %param.10) | copy-start | bytes 196612
  26.2 4.2 %collective-permute-start.11 = (f32[16,2,128]{2,1,0:T(2,128)S(1)}, f32[16,2,128]{2,1,0:T(2,128)S(1)}, u32[]{:S(2)}, u32[]{:S(2)}) collective-permute-start(f32[16,2,128]{2,1,0:T(2,128)S(1)} %get-tuple-element.45), channel_id=1, source_target_pairs={{0,16},{8,24},{16,0},{24,8},{1,17},{9,25},{17,1},{25,9},{2,18},{10... | collective-permute-start | bytes 49160 | tf_op jit(solution)/shard_map/ppermute | solution.py:415
  27.9 4.6 %collective-permute-start.12 = (f32[16,2,128]{2,1,0:T(2,128)S(1)}, f32[16,2,128]{2,1,0:T(2,128)S(1)}, u32[]{:S(2)}, u32[]{:S(2)}) collective-permute-start(f32[16,2,128]{2,1,0:T(2,128)S(1)} %get-tuple-element.46), channel_id=1, source_target_pairs={{0,24},{8,16},{16,8},{24,0},{1,25},{9,17},{17,9},{25,1},{2,26},{10... | collective-permute-start | bytes 49160 | tf_op jit(solution)/shard_map/ppermute | solution.py:415
  29.3 3.7 %collective-permute-start.13 = (f32[16,2,128]{2,1,0:T(2,128)S(1)}, f32[16,2,128]{2,1,0:T(2,128)S(1)}, u32[]{:S(2)}, u32[]{:S(2)}) collective-permute-start(f32[16,2,128]{2,1,0:T(2,128)S(1)} %get-tuple-element.47), channel_id=1, source_target_pairs={{0,8},{8,0},{16,24},{24,16},{1,9},{9,1},{17,25},{25,17},{2,10},{10... | collective-permute-start | bytes 49160 | tf_op jit(solution)/shard_map/ppermute | solution.py:415
  30.4 2.6 %copy-start.2 = (f32[2048,2]{0,1:T(2,128)S(1)}, f32[2048,2]{0,1:T(2,128)}, u32[]{:S(2)}) copy-start(f32[2048,2]{0,1:T(2,128)} %param.11) | copy-start | bytes 49156

commit v9 on v8

--- a/solution.py
+++ b/solution.py
@@ -533,10 +533,10 @@
     residual, *parts = adjoint_calls(
         rows, probes, blocks, noises, precond, circulant, spectrum, kernel, symbols, left, dft, turns, big_turn
     )
-    near_y, opposite, near_x = (swapped(parts[d], "probe", d) for d in (2, 3, 1))
-    total = lax.optimization_barrier(parts[0] + near_y)
+    near_x, opposite, near_y = (swapped(parts[d], "probe", d) for d in (1, 3, 2))
+    total = lax.optimization_barrier(parts[0] + near_x)
     total = lax.optimization_barrier(total + opposite)
-    total = before + (total + near_x) / probes
+    total = before + (total + near_y) / probes
     total = total.transpose(1, 0, 2).reshape(width, depth * lanes).T
     return residual.reshape(probe_bits.shape), total
 

time: 33.8 us -> 33.9 us (level)
  no operation moved by 1% of the time
where the time goes in v9:
time: 33.9 us; the launch traced here: 33.7 us
  starting transfers between devices  14.1 us (42%)
  waiting for transfers between devices  10.6 us (31%)
  Pallas kernels  6.92 us (20%)
  between operations  0.73 us (2%)
  local copies, waits for them, and re-layouts  0.66 us (2%)
  other arithmetic  0.66 us (2%)
    ppermute x14, starting transfers between devices, swapped(): lax.ppermute(x, axis, [(i, i ^ d) for i in range(lax.axis_size(axis))])  14.1 us
    ppermute x14, waiting for transfers between devices, swapped(): lax.ppermute(x, axis, [(i, i ^ d) for i in range(lax.axis_size(axis))])  10.6 us
    pallas_call x4, Pallas kernels, call(): pl.pallas_call(kernel, out_shape=shapes, in_specs=[whole] * len(operands)...  5.71 us
    pallas_call x1, Pallas kernels, gathered_shards(): pl.pallas_call(functools.partial(pack_kernel, half, first), out_shape=(pl...  1.21 us
  transfers between devices with their start and end apart: 14, of which 4 were waited for; matrix products, arithmetic and copies ran while one was open for 2% of the time, Pallas kernels for 13%

profile of v9, /device:TPU:0, one launch (start us, length us, event | category | flops | bytes accessed | tf_op | source)
XLA Modules:
  0.0 33.7 jit_solution(8352298472444322233)
XLA Ops:
  0.6 1.2 %shard_map.86 = (f32[392,128]{1,0:T(8,128)S(1)}, f32[328,128]{1,0:T(8,128)S(1)}, bf16[4,128,128]{2,1,0:T(8,128)(2,1)S(1)}, f32[2,128,256]{2,1,0:T(8,128)S(1)}) custom-call(s32[128,128]{1,0:T(8,128)} %bitcast.32, f32[128,128]{1,0:T(8,128)} %bitcast.33, f32[16,8,128]{2,1,0:T(8,128)} %bitcast.28, f32[16,8,128]{2,1,0:T(8,128)} %bitcast.30, ...), custom_call_target="tpu_custom_call" | custom-call | tf_op jit(solution)/shard_map/pallas_call | solution.py:484
  1.8 4.1 %collective-permute-start.2 = (f32[328,128]{1,0:T(8,128)S(1)}, f32[328,128]{1,0:T(8,128)S(1)}, u32[]{:S(2)}, u32[]{:S(2)}) collective-permute-start(f32[328,128]{1,0:T(8,128)S(1)} %get-tuple-element.26), channel_id=1, source_target_pairs={{0,4},{1,5},{2,6},{3,7},{4,0},{5,1},{6,2},{7,3},{8,12},{9,13},{10,... | collective-permute-start | bytes 503816 | tf_op jit(solution)/shard_map/ppermute | solution.py:415
  5.9 1.6 %collective-permute-start.1 = (f32[328,128]{1,0:T(8,128)S(1)}, f32[328,128]{1,0:T(8,128)S(1)}, u32[]{:S(2)}, u32[]{:S(2)}) collective-permute-start(f32[328,128]{1,0:T(8,128)S(1)} %get-tuple-element.26), channel_id=1, source_target_pairs={{0,2},{1,3},{2,0},{3,1},{4,6},{5,7},{6,4},{7,5},{8,10},{9,11},{10,... | collective-permute-start | bytes 503816 | tf_op jit(solution)/shard_map/ppermute | solution.py:415
  7.5 0.0 collective-permute-start
  7.5 6.4 %collective-permute-done.2.refs_3_.refs_4_ = f32[328,128]{1,0:T(8,128)S(1)} collective-permute-done((f32[328,128]{1,0:T(8,128)S(1)}, f32[328,128]{1,0:T(8,128)S(1)}, u32[]{:S(2)}, u32[]{:S(2)}) %collective-permute-start.2) | collective-permute-done | bytes 167968 | tf_op jit(solution)/shard_map/ppermute | solution.py:415
  14.0 0.7 %collective-permute-start.5 = (f32[264,128]{1,0:T(8,128)S(1)}, f32[264,128]{1,0:T(8,128)S(1)}, u32[]{:S(2)}, u32[]{:S(2)}) collective-permute-start(f32[264,128]{1,0:T(8,128)S(1)} %slice.17), channel_id=1, source_target_pairs={{0,2},{1,3},{2,0},{3,1},{4,6},{5,7},{6,4},{7,5},{8,10},{9,11},{10,... | collective-permute-start | bytes 405512 | tf_op jit(solution)/shard_map/ppermute | solution.py:415
  14.6 0.0 collective-permute-done.1.refs_2_
  14.7 1.6 %collective-permute-start.6 = (f32[128,128]{1,0:T(8,128)S(1)}, f32[128,128]{1,0:T(8,128)S(1)}, u32[]{:S(2)}, u32[]{:S(2)}) collective-permute-start(f32[128,128]{1,0:T(8,128)S(1)} %pad_maximum_fusion), channel_id=1, source_target_pairs={{0,16},{8,24},{16,0},{24,8},{1,17},{9,25},{17,1},{25,9},{2,18},{10... | collective-permute-start | bytes 196616 | tf_op jit(solution)/shard_map/ppermute | solution.py:415
  16.2 0.0 collective-permute-done.refs_1_
  16.3 0.7 %shard_map.87 = (f32[4,2,128,128]{3,2,1,0:T(8,128)S(1)}, bf16[512,256]{1,0:T(8,128)(2,1)S(1)}, f32[8,128,256]{2,1,0:T(8,128)S(1)}) custom-call(f32[392,128]{1,0:T(8,128)S(1)} %get-tuple-element.25.refs_0_, f32[392,128]{1,0:T(8,128)S(1)} %collective-permute-done.refs_1_, f32[328,128]{1,0:T(8,128)S(1)} %collective-permute-done.1.refs_2_, ...), custom_call_target="tpu_custom_call" | custom-call | tf_op jit(solution)/shard_map/pallas_call | solution.py:403
  16.9 0.1 collective-permute-start.3
  17.0 0.5 %collective-permute-start.4 = (f32[328,128]{1,0:T(8,128)S(1)}, f32[328,128]{1,0:T(8,128)S(1)}, u32[]{:S(2)}, u32[]{:S(2)}) collective-permute-start(f32[328,128]{1,0:T(8,128)S(1)} %collective-permute-done.2.refs_3_.refs_4_), channel_id=1, source_target_pairs={{0,1},{1,0},{2,3},{3,2},{4,5},{5,4},{6,7},{7,6},{8,9},{9,8},{10,11... | collective-permute-start | bytes 503816 | tf_op jit(solution)/shard_map/ppermute | solution.py:415
  17.5 1.5 %collective-permute-done.6.refs_6_ = f32[128,128]{1,0:T(8,128)S(1)} collective-permute-done((f32[128,128]{1,0:T(8,128)S(1)}, f32[128,128]{1,0:T(8,128)S(1)}, u32[]{:S(2)}, u32[]{:S(2)}) %collective-permute-start.6) | collective-permute-done | bytes 65568 | tf_op jit(solution)/shard_map/ppermute | solution.py:415
  19.0 0.0 collective-permute-done.5.refs_6_
  19.0 0.0 collective-permute-start.7
  19.0 1.5 %collective-permute-start.8 = (f32[128,128]{1,0:T(8,128)S(1)}, f32[128,128]{1,0:T(8,128)S(1)}, u32[]{:S(2)}, u32[]{:S(2)}) collective-permute-start(f32[128,128]{1,0:T(8,128)S(1)} %pad_maximum_fusion.1), channel_id=1, source_target_pairs={{0,2},{1,3},{2,0},{3,1},{4,6},{5,7},{6,4},{7,5},{8,10},{9,11},{10,... | collective-permute-start | bytes 196616 | tf_op jit(solution)/shard_map/ppermute | solution.py:415
  20.5 0.2 collective-permute-start.10
  20.7 0.0 collective-permute-done.3.refs_3_
  20.7 0.0 collective-permute-done.4.refs_5_
  20.7 0.0 collective-permute-done.7.refs_7_
  20.7 3.0 %shard_map.88 = (f32[8,2,16,128]{3,2,1,0:T(8,128)S(1)}, f32[8,128,128]{2,1,0:T(8,128)S(1)}, f32[8,128,128]{2,1,0:T(8,128)S(1)}) custom-call(f32[392,128]{1,0:T(8,128)S(1)} %get-tuple-element.25.refs_0_, f32[392,128]{1,0:T(8,128)S(1)} %collective-permute-done.refs_1_, f32[328,128]{1,0:T(8,128)S(1)} %collective-permute-done.1.refs_2_, ...), custom_call_target="tpu_custom_call" | custom-call | tf_op jit(solution)/shard_map/pallas_call | solution.py:403
  23.6 0.0 collective-permute-done.8.refs_8_
  23.7 0.4 %collective-permute-start.9 = (f32[128,128]{1,0:T(8,128)S(1)}, f32[128,128]{1,0:T(8,128)S(1)}, u32[]{:S(2)}, u32[]{:S(2)}) collective-permute-start(f32[128,128]{1,0:T(8,128)S(1)} %collective-permute-done.8.refs_8_), channel_id=1, source_target_pairs={{0,1},{1,0},{2,3},{3,2},{4,5},{5,4},{6,7},{7,6},{8,9},{9,8},{10,11... | collective-permute-start | bytes 196616 | tf_op jit(solution)/shard_map/ppermute | solution.py:415
  24.1 0.0 collective-permute-done.10.refs_7_
  24.1 0.0 copy-start
  24.1 0.0 copy-start.1
  24.1 0.9 %shard_map.89 = (f32[6,128,128]{2,1,0:T(8,128)S(1)}, f32[6,128,128]{2,1,0:T(8,128)S(1)}, f32[10,2,16,128]{3,2,1,0:T(8,128)S(1)}, f32[2,8,128]{2,1,0:T(8,128)S(1)}) custom-call(f32[392,128]{1,0:T(8,128)S(1)} %get-tuple-element.25.refs_0_, f32[392,128]{1,0:T(8,128)S(1)} %collective-permute-done.refs_1_, f32[328,128]{1,0:T(8,128)S(1)} %collective-permute-done.1.refs_2_, ...), custom_call_target="tpu_custom_call" | custom-call | tf_op jit(solution)/shard_map/pallas_call | solution.py:403
  24.9 0.0 collective-permute-done.9.refs_9_
  25.0 0.0 copy-done
  25.0 0.0 copy-done.1
  25.0 1.2 %shard_map.90 = (f32[128,128]{1,0:T(8,128)S(1)}, f32[16,2,128]{2,1,0:T(2,128)S(1)}, f32[16,2,128]{2,1,0:T(2,128)S(1)}, f32[16,2,128]{2,1,0:T(2,128)S(1)}, f32[16,2,128]{2,1,0:T(2,128)S(1)}) custom-call(f32[392,128]{1,0:T(8,128)S(1)} %get-tuple-element.25.refs_0_, f32[392,128]{1,0:T(8,128)S(1)} %collective-permute-done.refs_1_, ...), custom_call_target="tpu_custom_call" | custom-call | tf_op jit(solution)/shard_map/pallas_call | solution.py:403
  26.2 1.6 %collective-permute-start.11 = (f32[16,2,128]{2,1,0:T(2,128)S(1)}, f32[16,2,128]{2,1,0:T(2,128)S(1)}, u32[]{:S(2)}, u32[]{:S(2)}) collective-permute-start(f32[16,2,128]{2,1,0:T(2,128)S(1)} %get-tuple-element.45), channel_id=1, source_target_pairs={{0,8},{8,0},{16,24},{24,16},{1,9},{9,1},{17,25},{25,17},{2,10},{10... | collective-permute-start | bytes 49160 | tf_op jit(solution)/shard_map/ppermute | solution.py:415
  27.8 1.5 %collective-permute-start.12 = (f32[16,2,128]{2,1,0:T(2,128)S(1)}, f32[16,2,128]{2,1,0:T(2,128)S(1)}, u32[]{:S(2)}, u32[]{:S(2)}) collective-permute-start(f32[16,2,128]{2,1,0:T(2,128)S(1)} %get-tuple-element.46), channel_id=1, source_target_pairs={{0,24},{8,16},{16,8},{24,0},{1,25},{9,17},{17,9},{25,1},{2,26},{10... | collective-permute-start | bytes 49160 | tf_op jit(solution)/shard_map/ppermute | solution.py:415
  29.3 0.5 %collective-permute-start.13 = (f32[16,2,128]{2,1,0:T(2,128)S(1)}, f32[16,2,128]{2,1,0:T(2,128)S(1)}, u32[]{:S(2)}, u32[]{:S(2)}) collective-permute-start(f32[16,2,128]{2,1,0:T(2,128)S(1)} %get-tuple-element.47), channel_id=1, source_target_pairs={{0,16},{8,24},{16,0},{24,8},{1,17},{9,25},{17,1},{25,9},{2,18},{10... | collective-permute-start | bytes 49160 | tf_op jit(solution)/shard_map/ppermute | solution.py:415
  29.8 0.6 %copy.9 = f32[1,1,16384]{2,1,0:T(1,128)} copy(f32[1,1,16384]{2,1,0:T(1,128)S(1)} %bitcast.27) | data formatting | bytes 131072
  30.4 0.0 collective-permute-done.11
  30.4 0.0 copy-start.2
  30.4 2.0 %collective-permute-done.12 = f32[16,2,128]{2,1,0:T(2,128)S(1)} collective-permute-done((f32[16,2,128]{2,1,0:T(2,128)S(1)}, f32[16,2,128]{2,1,0:T(2,128)S(1)}, u32[]{:S(2)}, u32[]{:S(2)}) %collective-permute-start.12) | collective-permute-done | bytes 16416 | tf_op jit(solution)/shard_map/ppermute | solution.py:415
  32.5 0.6 %collective-permute-done.13 = f32[16,2,128]{2,1,0:T(2,128)S(1)} collective-permute-done((f32[16,2,128]{2,1,0:T(2,128)S(1)}, f32[16,2,128]{2,1,0:T(2,128)S(1)}, u32[]{:S(2)}, u32[]{:S(2)}) %collective-permute-start.13) | collective-permute-done | bytes 16416 | tf_op jit(solution)/shard_map/ppermute | solution.py:415
  33.1 0.0 copy-done.2
  33.1 0.6 %fusion = f32[2048,2]{0,1:T(2,128)} fusion(f32[2048,2]{0,1:T(2,128)S(1)} %copy-done.2, f32[16,2,128]{2,1,0:T(2,128)S(1)} %add.13, f32[16,2,128]{2,1,0:T(2,128)S(1)} %collective-permute-done.13), kind=kLoop, calls=%fused_computation.3 | loop fusion | flops 12288 | bytes 65536 | tf_op jit(solution)/shard_map/transpose | solution.py:540
  (8 shorter events, 0.1 us)
Async XLA Ops:
  1.8 12.1 %collective-permute-start.2 = (f32[328,128]{1,0:T(8,128)S(1)}, f32[328,128]{1,0:T(8,128)S(1)}, u32[]{:S(2)}, u32[]{:S(2)}) collective-permute-start(f32[328,128]{1,0:T(8,128)S(1)} %get-tuple-element.26), channel_id=1, source_target_pairs={{0,4},{1,5},{2,6},{3,7},{4,0},{5,1},{6,2},{7,3},{8,12},{9,13},{10,... | collective-permute-start | bytes 503816 | tf_op jit(solution)/shard_map/ppermute | solution.py:415
  5.9 8.7 %collective-permute-start.1 = (f32[328,128]{1,0:T(8,128)S(1)}, f32[328,128]{1,0:T(8,128)S(1)}, u32[]{:S(2)}, u32[]{:S(2)}) collective-permute-start(f32[328,128]{1,0:T(8,128)S(1)} %get-tuple-element.26), channel_id=1, source_target_pairs={{0,2},{1,3},{2,0},{3,1},{4,6},{5,7},{6,4},{7,5},{8,10},{9,11},{10,... | collective-permute-start | bytes 503816 | tf_op jit(solution)/shard_map/ppermute | solution.py:415
  7.5 8.7 %collective-permute-start = (f32[392,128]{1,0:T(8,128)S(1)}, f32[392,128]{1,0:T(8,128)S(1)}, u32[]{:S(2)}, u32[]{:S(2)}) collective-permute-start(f32[392,128]{1,0:T(8,128)S(1)} %get-tuple-element.25.refs_0_), channel_id=1, source_target_pairs={{0,1},{1,0},{2,3},{3,2},{4,5},{5,4},{6,7},{7,6},{8,9},{9,8},{10,11... | collective-permute-start | bytes 602120 | tf_op jit(solution)/shard_map/ppermute | solution.py:415
  14.0 5.1 %collective-permute-start.5 = (f32[264,128]{1,0:T(8,128)S(1)}, f32[264,128]{1,0:T(8,128)S(1)}, u32[]{:S(2)}, u32[]{:S(2)}) collective-permute-start(f32[264,128]{1,0:T(8,128)S(1)} %slice.17), channel_id=1, source_target_pairs={{0,2},{1,3},{2,0},{3,1},{4,6},{5,7},{6,4},{7,5},{8,10},{9,11},{10,... | collective-permute-start | bytes 405512 | tf_op jit(solution)/shard_map/ppermute | solution.py:415
  14.7 4.3 %collective-permute-start.6 = (f32[128,128]{1,0:T(8,128)S(1)}, f32[128,128]{1,0:T(8,128)S(1)}, u32[]{:S(2)}, u32[]{:S(2)}) collective-permute-start(f32[128,128]{1,0:T(8,128)S(1)} %pad_maximum_fusion), channel_id=1, source_target_pairs={{0,16},{8,24},{16,0},{24,8},{1,17},{9,25},{17,1},{25,9},{2,18},{10... | collective-permute-start | bytes 196616 | tf_op jit(solution)/shard_map/ppermute | solution.py:415
  16.9 3.8 %collective-permute-start.3 = (f32[328,128]{1,0:T(8,128)S(1)}, f32[328,128]{1,0:T(8,128)S(1)}, u32[]{:S(2)}, u32[]{:S(2)}) collective-permute-start(f32[328,128]{1,0:T(8,128)S(1)} %collective-permute-done.1.refs_2_), channel_id=1, source_target_pairs={{0,1},{1,0},{2,3},{3,2},{4,5},{5,4},{6,7},{7,6},{8,9},{9,8},{10,11... | collective-permute-start | bytes 503816 | tf_op jit(solution)/shard_map/ppermute | solution.py:415
  17.0 3.7 %collective-permute-start.4 = (f32[328,128]{1,0:T(8,128)S(1)}, f32[328,128]{1,0:T(8,128)S(1)}, u32[]{:S(2)}, u32[]{:S(2)}) collective-permute-start(f32[328,128]{1,0:T(8,128)S(1)} %collective-permute-done.2.refs_3_.refs_4_), channel_id=1, source_target_pairs={{0,1},{1,0},{2,3},{3,2},{4,5},{5,4},{6,7},{7,6},{8,9},{9,8},{10,11... | collective-permute-start | bytes 503816 | tf_op jit(solution)/shard_map/ppermute | solution.py:415
  19.0 1.6 %collective-permute-start.7 = (f32[264,128]{1,0:T(8,128)S(1)}, f32[264,128]{1,0:T(8,128)S(1)}, u32[]{:S(2)}, u32[]{:S(2)}) collective-permute-start(f32[264,128]{1,0:T(8,128)S(1)} %collective-permute-done.5.refs_6_), channel_id=1, source_target_pairs={{0,1},{1,0},{2,3},{3,2},{4,5},{5,4},{6,7},{7,6},{8,9},{9,8},{10,11... | collective-permute-start | bytes 405512 | tf_op jit(solution)/shard_map/ppermute | solution.py:415
  19.0 4.6 %collective-permute-start.8 = (f32[128,128]{1,0:T(8,128)S(1)}, f32[128,128]{1,0:T(8,128)S(1)}, u32[]{:S(2)}, u32[]{:S(2)}) collective-permute-start(f32[128,128]{1,0:T(8,128)S(1)} %pad_maximum_fusion.1), channel_id=1, source_target_pairs={{0,2},{1,3},{2,0},{3,1},{4,6},{5,7},{6,4},{7,5},{8,10},{9,11},{10,... | collective-permute-start | bytes 196616 | tf_op jit(solution)/shard_map/ppermute | solution.py:415
  20.5 3.6 %collective-permute-start.10 = (f32[128,128]{1,0:T(8,128)S(1)}, f32[128,128]{1,0:T(8,128)S(1)}, u32[]{:S(2)}, u32[]{:S(2)}) collective-permute-start(f32[128,128]{1,0:T(8,128)S(1)} %collective-permute-done.6.refs_6_), channel_id=1, source_target_pairs={{0,1},{1,0},{2,3},{3,2},{4,5},{5,4},{6,7},{7,6},{8,9},{9,8},{10,11... | collective-permute-start | bytes 196616 | tf_op jit(solution)/shard_map/ppermute | solution.py:415
  23.7 1.3 %collective-permute-start.9 = (f32[128,128]{1,0:T(8,128)S(1)}, f32[128,128]{1,0:T(8,128)S(1)}, u32[]{:S(2)}, u32[]{:S(2)}) collective-permute-start(f32[128,128]{1,0:T(8,128)S(1)} %collective-permute-done.8.refs_8_), channel_id=1, source_target_pairs={{0,1},{1,0},{2,3},{3,2},{4,5},{5,4},{6,7},{7,6},{8,9},{9,8},{10,11... | collective-permute-start | bytes 196616 | tf_op jit(solution)/shard_map/ppermute | solution.py:415
  24.1 0.9 %copy-start = (f32[2048,8]{0,1:T(8,128)S(1)}, f32[2048,8]{0,1:T(8,128)}, u32[]{:S(2)}) copy-start(f32[2048,8]{0,1:T(8,128)} %param.9) | copy-start | bytes 196612
  24.1 0.9 %copy-start.1 = (f32[2048,8]{0,1:T(8,128)S(1)}, f32[2048,8]{0,1:T(8,128)}, u32[]{:S(2)}) copy-start(f32[2048,8]{0,1:T(8,128)} %param.10) | copy-start | bytes 196612
  26.2 4.2 %collective-permute-start.11 = (f32[16,2,128]{2,1,0:T(2,128)S(1)}, f32[16,2,128]{2,1,0:T(2,128)S(1)}, u32[]{:S(2)}, u32[]{:S(2)}) collective-permute-start(f32[16,2,128]{2,1,0:T(2,128)S(1)} %get-tuple-element.45), channel_id=1, source_target_pairs={{0,8},{8,0},{16,24},{24,16},{1,9},{9,1},{17,25},{25,17},{2,10},{10... | collective-permute-start | bytes 49160 | tf_op jit(solution)/shard_map/ppermute | solution.py:415
  27.8 4.6 %collective-permute-start.12 = (f32[16,2,128]{2,1,0:T(2,128)S(1)}, f32[16,2,128]{2,1,0:T(2,128)S(1)}, u32[]{:S(2)}, u32[]{:S(2)}) collective-permute-start(f32[16,2,128]{2,1,0:T(2,128)S(1)} %get-tuple-element.46), channel_id=1, source_target_pairs={{0,24},{8,16},{16,8},{24,0},{1,25},{9,17},{17,9},{25,1},{2,26},{10... | collective-permute-start | bytes 49160 | tf_op jit(solution)/shard_map/ppermute | solution.py:415
  29.3 3.7 %collective-permute-start.13 = (f32[16,2,128]{2,1,0:T(2,128)S(1)}, f32[16,2,128]{2,1,0:T(2,128)S(1)}, u32[]{:S(2)}, u32[]{:S(2)}) collective-permute-start(f32[16,2,128]{2,1,0:T(2,128)S(1)} %get-tuple-element.47), channel_id=1, source_target_pairs={{0,16},{8,24},{16,0},{24,8},{1,17},{9,25},{17,1},{25,9},{2,18},{10... | collective-permute-start | bytes 49160 | tf_op jit(solution)/shard_map/ppermute | solution.py:415
  30.4 2.6 %copy-start.2 = (f32[2048,2]{0,1:T(2,128)S(1)}, f32[2048,2]{0,1:T(2,128)}, u32[]{:S(2)}) copy-start(f32[2048,2]{0,1:T(2,128)} %param.11) | copy-start | bytes 49156
